TPU v7x, 256 devices: a whole 4x4x8 slice. The times are simulated.
256 devices in a mesh: lat: 8 (over x_hi, y), lon: 32 (over z, x_lo, core).
Axes of the slice: x: 4 (x_hi: 2, x_lo: 2; x = x_hi * 2 + x_lo), y: 4, z: 8, core: 2. Of those that a mesh axis runs over, the one named last changes fastest.
Arguments:
- background: bfloat16 [8, 32, 512, 1024], P('lat', 'lon'), may hold values from -6 to 6
- conv_pert: bfloat16 [8, 32, 128, 512], P('lat', 'lon'), may hold values from -6 to 6
- conv_misfit: bfloat16 [8, 32, 128], P('lat', 'lon'), may hold values from -6 to 6
- conv_column: int32 [8, 32, 128], P('lat', 'lon'), may hold values from 0 to 255
- sat_pert: bfloat16 [8, 512, 32, 512], P('lat', 'lon'), may hold values from -6 to 6
- sat_misfit: bfloat16 [8, 512, 32], P('lat', 'lon'), may hold values from -6 to 6
- sat_rows: int32 [8, 512], P('lat', 'lon'), may hold values from 1 to 32
- sat_targets: int32 [8, 512, 2], P('lat', 'lon'), may hold values from 0 to 31, all different within a row; in each aligned block of 16 rows (0 to 15, 16 to 31, ..., all dimensions but the last counted through in order) at most 2 rows name the same one
Outputs:
- analysis: float32 [8, 32, 512, 1024], P('lat', 'lon')
Inputs may be any that keep to these rules, and one draw needn't show every extreme that they name: `sat_targets`: each tile names 2 different blocks. The tiles of one device name one block at most 2 times in all, and some device names some block exactly 2 times.
All inputs are finite; a program needn't handle non-finite values.
Results may differ from a plain program's by a relative error of at most 0.0073.
Values may be sent and summed in bfloat16 or wider, within the bound.
No kernel may reach another device: no remote copies, remote signals or barrier semaphores. Data moves between devices by JAX's collectives and lax.ppermute only.
A program may use at most 128 MiB of HBM per device.

v0:
```python
import jax
import jax.numpy as jnp
from jax import lax
from jax.sharding import PartitionSpec as P

BLK = 16
LOC = 2
NS_ITERS = 3


def extended(block, sides, width, periodic):
    for axis, dim in sides:
        count = lax.axis_size(axis)
        forward = [(i, i + 1) for i in range(count - 1)]
        if periodic:
            forward.append((count - 1, 0))
        backward = [(target, source) for source, target in forward]
        low = lax.ppermute(
            lax.slice_in_dim(block, block.shape[dim] - width, None, axis=dim), axis, forward
        )
        high = lax.ppermute(lax.slice_in_dim(block, 0, width, axis=dim), axis, backward)
        block = jnp.concatenate([low, block, high], axis=dim)
    return block


def local_weight(column, lat_shift, lon_shift):
    lat_place = BLK * lat_shift + (column // BLK).astype(jnp.float32) + 0.5 - 0.5 * BLK
    lon_place = BLK * lon_shift + (column % BLK).astype(jnp.float32) + 0.5 - 0.5 * BLK
    return jnp.exp(-(lat_place * lat_place + lon_place * lon_place) / (2.0 * BLK * BLK))


def analyse(gram_sum, drive_sum, ensemble):
    members = ensemble.shape[0]
    highest = lax.Precision.HIGHEST
    identity = jnp.eye(members, dtype=jnp.float32)
    system = (members - 1.0) * identity + gram_sum
    scale = jnp.sqrt(jnp.sum(system * system))
    iterate = system / scale
    inverse_root = identity
    for sweep_index in range(NS_ITERS):
        middle = 1.5 * identity - 0.5 * jnp.dot(inverse_root, iterate, precision=highest)
        iterate = jnp.dot(iterate, middle, precision=highest)
        inverse_root = jnp.dot(middle, inverse_root, precision=highest)
    covariance = jnp.dot(inverse_root, inverse_root, precision=highest) / scale
    mean_weight = jnp.dot(covariance, drive_sum, precision=highest)
    transform = (jnp.sqrt((members - 1.0) / scale) * inverse_root + mean_weight[:, None]).astype(
        jnp.bfloat16
    )
    state_mean = jnp.mean(ensemble.astype(jnp.float32), axis=0)
    anomaly = (ensemble.astype(jnp.float32) - state_mean).astype(jnp.bfloat16)
    return state_mean + lax.dot_general(
        transform, anomaly, (((0,), (0,)), ((), ())), preferred_element_type=jnp.float32
    )


def outer_sum(scaled, spread):
    return lax.dot_general(
        scaled, spread, (((0,), (0,)), ((), ())), preferred_element_type=jnp.float32
    )


def conv_terms(nearby, conv_obs, members):
    pert_span = conv_obs * members
    spread = nearby[:, :, :pert_span].reshape(3, 3, conv_obs, members)
    misfit = nearby[:, :, pert_span : pert_span + conv_obs]
    column = nearby[:, :, pert_span + conv_obs :].astype(jnp.int32)
    shifts = jnp.arange(3).astype(jnp.float32) - 1.0
    weight = local_weight(column, shifts[:, None, None], shifts[None, :, None])
    scaled = (weight[..., None] * spread).astype(jnp.bfloat16).reshape(-1, members)
    gram_part = outer_sum(scaled, spread.reshape(-1, members))
    drive_part = jnp.dot(misfit.reshape(-1), scaled, preferred_element_type=jnp.float32)
    return (gram_part, drive_part)


def shards(
    background, conv_pert, conv_misfit, conv_column, sat_pert, sat_misfit, sat_rows, sat_targets
):
    members = background.shape[2]
    my_block = lax.axis_index("lon")
    conv_obs = conv_pert.shape[2]
    packed = jnp.concatenate(
        [conv_pert.reshape(1, 1, -1), conv_misfit, conv_column.astype(jnp.bfloat16)], axis=2
    )
    widened = extended(packed, (("lon", 1),), 1, True)
    nearby = extended(widened, (("lat", 0),), 1, False)
    gram_conv, drive_conv = conv_terms(nearby, conv_obs, members)
    entry_weight = 0.5 ** jnp.arange(LOC).astype(jnp.float32)
    obs_per_tile = sat_pert.shape[2]
    obs_index = jnp.arange(obs_per_tile)
    spread = lax.all_gather(sat_pert, "lon", axis=1, tiled=True)
    misfit = lax.all_gather(sat_misfit, "lon", axis=1, tiled=True)
    live_rows = lax.all_gather(sat_rows, "lon", axis=1, tiled=True)
    targets = lax.all_gather(sat_targets, "lon", axis=1, tiled=True)
    hit_weight = jnp.sum(jnp.where(targets == my_block, entry_weight, 0.0), axis=-1)
    keep_rows = jnp.where(obs_index < live_rows[..., None], hit_weight[..., None], 0.0)
    scaled = (keep_rows[..., None] * spread).astype(jnp.bfloat16).reshape(-1, members)
    gram_part = outer_sum(scaled, spread.reshape(-1, members))
    drive_part = jnp.dot(misfit.reshape(-1), scaled, preferred_element_type=jnp.float32)
    result = analyse(gram_conv + gram_part, drive_conv + drive_part, background[0, 0])
    return result[None, None]


def solution(mesh):
    placed = (
        P("lat", "lon", None, None),
        P("lat", "lon", None, None),
        P("lat", "lon", None),
        P("lat", "lon", None),
        P("lat", "lon", None, None),
        P("lat", "lon", None),
        P("lat", "lon"),
        P("lat", "lon", None),
    )
    return jax.shard_map(
        shards, mesh=mesh, in_specs=placed, out_specs=P("lat", "lon", None, None), check_vma=False
    )
```

profile of v0, /device:TPU:24, one launch (start us, length us, event | category | flops | bytes accessed | tf_op | source)
XLA Modules:
  0.0 209.4 jit_solution(2800184626400431324)
XLA Ops:
  9.3 6.3 %collective-permute-start.1 = (bf16[1,1,65792]{2,1,0:T(2,128)(2,1)S(1)}, bf16[1,1,65792]{2,1,0:T(2,128)(2,1)S(1)}, u32[]{:S(2)}, u32[]{:S(2)}) collective-permute-start(bf16[1,1,65792]{2,1,0:T(2,128)(2,1)S(1)} %pad_maximum_fusion.2), channel_id=1, source_target_pairs={{1,0},{2,1},{3,2},{4,3},{5,4},{6,5},{7,6},{8,7},{9,8},{10,9},{11,1... | collective-permute-start | bytes 394760 | tf_op jit(solution)/shard_map/ppermute | solution.py:21
  15.6 2.1 %copy.12 = bf16[1,16,32,512]{3,1,2,0:T(8,128)(2,1)} copy(bf16[1,16,32,512]{3,2,1,0:T(8,128)(2,1)} %param.12) | data formatting | bytes 1048576 | tf_op args[4]
  20.0 32.2 %all_gather.15 = bf16[1,512,32]{2,1,0:T(8,128)(2,1)S(1)} all-gather(bf16[1,16,32]{2,1,0:T(8,128)(2,1)S(1)} %copy-done.12), channel_id=1, replica_groups=mesh['lat'=8,'lon'=32] {'lon'}, dimensions={1}, use_global_device_ids=true | all-gather | bytes 33792 | tf_op jit(solution)/shard_map/all_gather | solution.py:91
  52.4 32.9 %all_gather.13 = s32[1,512,2]{2,0,1:T(1,128)S(1)} all-gather(s32[1,16,2]{2,0,1:T(1,128)S(1)} %copy.11), channel_id=1, replica_groups=mesh['lat'=8,'lon'=32] {'lon'}, dimensions={1}, use_global_device_ids=true | all-gather | bytes 4224 | tf_op jit(solution)/shard_map/all_gather | solution.py:93
  85.3 13.8 %all-reduce = s32[512]{0:T(512)S(1)} all-reduce(s32[512]{0:T(512)S(1)} %bitcast_dynamic-update-slice_fusion), channel_id=1, replica_groups=mesh['lat'=8,'lon'=32] {'lon'}, use_global_device_ids=true, to_apply=%add | all-reduce | flops 512 | bytes 4096
  100.1 2.7 %collective-permute-start.3 = (bf16[1,3,65792]{2,1,0:T(4,128)(2,1)S(1)}, bf16[1,3,65792]{2,1,0:T(4,128)(2,1)S(1)}, u32[]{:S(2)}, u32[]{:S(2)}) collective-permute-start(bf16[1,3,65792]{2,1,0:T(4,128)(2,1)S(1)} %pad_maximum_fusion.1), channel_id=1, source_target_pairs={{32,0},{64,32},{96,64},{128,96},{160,128},{192,160},{224,192},{33,... | collective-permute-start | bytes 1184264 | tf_op jit(solution)/shard_map/ppermute | solution.py:21
  102.7 7.0 %collective-permute-start.2 = (bf16[1,3,65792]{2,1,0:T(4,128)(2,1)S(1)}, bf16[1,3,65792]{2,1,0:T(4,128)(2,1)S(1)}, u32[]{:S(2)}, u32[]{:S(2)}) collective-permute-start(bf16[1,3,65792]{2,1,0:T(4,128)(2,1)S(1)} %pad_maximum_fusion.1), channel_id=1, source_target_pairs={{0,32},{32,64},{64,96},{96,128},{128,160},{160,192},{192,224},{1,3... | collective-permute-start | bytes 1184264 | tf_op jit(solution)/shard_map/ppermute | solution.py:18
  110.9 19.6 %collective-permute-done.3 = bf16[1,3,65792]{2,1,0:T(4,128)(2,1)S(1)} collective-permute-done((bf16[1,3,65792]{2,1,0:T(4,128)(2,1)S(1)}, bf16[1,3,65792]{2,1,0:T(4,128)(2,1)S(1)}, u32[]{:S(2)}, u32[]{:S(2)}) %collective-permute-start.3) | collective-permute-done | bytes 394784 | tf_op jit(solution)/shard_map/ppermute | solution.py:21
  130.5 2.4 %pad_maximum_fusion = bf16[3,3,65792]{2,1,0:T(4,128)(2,1)S(1)} fusion(bf16[1,3,65792]{2,1,0:T(4,128)(2,1)S(1)} %collective-permute-done.3, bf16[1,1,65792]{2,1,0:T(2,128)(2,1)S(1)} %collective-permute-done.1, bf16[1,1,128]{2,1,0:T(2,128)(2,1)S(1)} %convert_element_type.69, bf16[1,1,128]{2,1,0:T(2,128)(2,1)S(1)} %copy-done.10, ...), kind=kLoop, calls=%fused_computation.15 | loop fusion | flops 8289792 | bytes 2368512 | tf_op jit(solution)/shard_map/concatenate | solution.py:22
  134.7 4.8 %mul.83 = f32[3,3,65536]{2,1,0:T(4,128)} reshape(f32[3,3,128,512]{3,2,1,0:T(8,128)} %mul.82) | data formatting | bytes 4718592 | tf_op jit(solution)/shard_map/mul | solution.py:69
  139.6 2.7 %multiply_convert_fusion.1 = bf16[3,3,65536]{2,1,0:T(4,128)(2,1)S(1)} fusion(f32[3,3,65536]{2,1,0:T(4,128)} %mul.83, bf16[3,3,65792]{2,1,0:T(4,128)(2,1)S(1)} %pad_maximum_fusion), kind=kLoop, calls=%fused_computation.5 | loop fusion | flops 1769472 | bytes 4718592 | tf_op jit(solution)/shard_map/convert_element_type | solution.py:69
  142.3 2.6 %convert_element_type.75 = bf16[1152,512]{1,0:T(8,128)(2,1)} reshape(bf16[3,3,65536]{2,1,0:T(4,128)(2,1)S(1)} %multiply_convert_fusion.1) | data formatting | bytes 2359296 | tf_op jit(solution)/shard_map/convert_element_type | solution.py:69
  144.9 3.0 %slice_convert_fusion = (f32[3,3,65536]{2,1,0:T(4,128)}, bf16[3,3,65536]{2,1,0:T(4,128)(2,1)}) fusion(bf16[3,3,65792]{2,1,0:T(4,128)(2,1)S(1)} %pad_maximum_fusion), kind=kLoop, calls=%fused_computation.68 | loop fusion | flops 589824 | bytes 4718592 | tf_op jit(solution)/shard_map/convert_element_type | solution.py:69
  147.8 3.6 %reshape.104 = f32[3,3,128,512]{3,2,1,0:T(8,128)S(1)} reshape(f32[3,3,65536]{2,1,0:T(4,128)} %get-tuple-element.5) | data formatting | bytes 4718592 | tf_op jit(solution)/shard_map/convert_element_type | solution.py:69
  151.5 4.1 %reshape_reshape.3 = bf16[1152,512]{1,0:T(8,128)(2,1)} reshape(bf16[3,3,65536]{2,1,0:T(4,128)(2,1)} %get-tuple-element.6) | data formatting | bytes 2359296 | tf_op jit(solution)/shard_map/reshape;reshape | solution.py:70
  156.7 15.0 %fusion.8 = f32[512,512]{1,0:T(8,128)S(1)} fusion(bf16[1,512,32,512]{3,1,2,0:T(8,128)(2,1)} %all-gather.2.cloned.1.call-done, f32[512,32]{0,1:T(8,128)S(1)} %fusion.23), kind=kOutput, calls=%fused_computation.16 | convolution fusion | flops 8615100416 | bytes 17891328 | tf_op jit(solution)/shard_map/dot_general | solution.py:57
  171.7 2.5 %multiply_reduce_fusion = (f32[]{:T(128)}, f32[512,512]{1,0:T(8,128)}) fusion(f32[512,512]{1,0:T(8,128)S(1)} %fusion.8, bf16[1152,512]{1,0:T(8,128)(2,1)S(1)} %copy-done.6, bf16[1152,512]{1,0:T(8,128)(2,1)S(1)} %copy-done.7), kind=kOutput, calls=%fused_computation.26 | convolution fusion | flops 605552640 | bytes 4456452 | tf_op jit(solution)/shard_map/dot_general | solution.py:57
  174.8 2.4 %select_subtract_fusion.2 = f32[512,512]{1,0:T(8,128)S(1)} fusion(f32[512,512]{1,0:T(8,128)} %get-tuple-element.8, f32[]{:T(128)S(6)} %sqrt.6), kind=kOutput, calls=%fused_computation.14 | convolution fusion | flops 1612185600 | bytes 2097156 | tf_op jit(solution)/shard_map/dot_general | solution.py:41
  177.2 1.9 fusion.21
  180.1 1.9 select_subtract_fusion.1
  185.8 1.8 select_subtract_fusion
  187.6 2.1 %fusion.40 = f32[512,512]{1,0:T(8,128)S(1)} fusion(f32[512,512]{1,0:T(8,128)S(1)} %select_subtract_fusion, f32[512,512]{1,0:T(8,128)S(1)} %fusion.38), kind=kOutput, calls=%fused_computation.71 | convolution fusion | flops 1610612736 | bytes 3145728 | tf_op jit(solution)/shard_map/dot_general | solution.py:43
  191.6 7.7 %fusion.3 = f32[1,512,1]{1,0,2:T(1,128)S(1)} fusion(bf16[512,32,1]{0,2,1:T(2,128)(2,1)S(1)} %copy.17, bf16[1,512,32,512]{3,1,2,0:T(8,128)(2,1)} %all-gather.2.cloned.1.call-done, f32[512,32]{0,1:T(8,128)S(1)} %fusion.23), kind=kOutput, calls=%fused_computation.4 | convolution fusion | flops 41943040 | bytes 16877568 | tf_op jit(solution)/shard_map/dot_general | solution.py:98
  200.4 2.2 %add_bitcast_fusion = f32[1,1,512,1024]{3,2,1,0:T(8,128)} fusion(bf16[1,1,512,1024]{3,2,1,0:T(8,128)(2,1)S(1)} %copy-done.9, f32[1024]{0:T(1024)S(1)} %copy-done.13, f32[512,512]{1,0:T(8,128)S(1)} %fusion.40, f32[512]{0:T(512)S(1)} %bitcast.61, f32[]{:T(128)S(6)} %sqrt.7), kind=kOutput, calls=%fused_computation.11 | convolution fusion | flops 539754496 | bytes 4200452 | tf_op jit(solution)/shard_map/dot_general | solution.py:51
  (68 shorter events, 16.9 us)
Async XLA Ops:
  6.5 12.1 %copy-start.16 = (u32[256]{0:T(256)S(1)}, u32[256]{0:T(256)}, u32[]{:S(2)}) copy-start(u32[256]{0:T(256)} %constant.72) | copy-start | bytes 3076
  6.5 11.2 %copy-start.8 = (bf16[1,1,512,1024]{3,2,1,0:T(8,128)(2,1)S(1)}, bf16[1,1,512,1024]{3,2,1,0:T(8,128)(2,1)}, u32[]{:S(2)}) copy-start(bf16[1,1,512,1024]{3,2,1,0:T(8,128)(2,1)} %param.8) | copy-start | bytes 3145732
  6.5 12.0 %copy-start.14 = (s32[1,16,2]{1,2,0:T(2,128)S(1)}, s32[1,16,2]{1,2,0:T(2,128)}, u32[]{:S(2)}) copy-start(s32[1,16,2]{1,2,0:T(2,128)} %param.15) | copy-start | bytes 388
  6.5 13.3 %copy-start.15 = (s32[1,16]{1,0:T(1,128)S(1)}, s32[1,16]{1,0:T(1,128)}, u32[]{:S(2)}) copy-start(s32[1,16]{1,0:T(1,128)} %param.14) | copy-start | bytes 196
  6.5 13.4 %copy-start.12 = (bf16[1,16,32]{2,1,0:T(8,128)(2,1)S(1)}, bf16[1,16,32]{2,1,0:T(8,128)(2,1)}, u32[]{:S(2)}) copy-start(bf16[1,16,32]{2,1,0:T(8,128)(2,1)} %param.13) | copy-start | bytes 3076
  6.5 150.1 %all-gather.2.cloned.1.call-start = ((), (), s32[]{:S(2)}) async-start(), calls=%async_computation | async-start | bytes 17301504 | tf_op jit(solution)/shard_map/all_gather | solution.py:90
  7.3 125.6 %copy-start.11 = (bf16[1,1,128]{2,1,0:T(2,128)(2,1)}, bf16[1,1,128]{2,1,0:T(2,128)(2,1)S(1)}, u32[]{:S(2)}) copy-start(bf16[1,1,128]{2,1,0:T(2,128)(2,1)S(1)} %convert_element_type.69) | copy-start | bytes 772
  7.3 91.8 %copy-start.10 = (bf16[1,1,128]{2,1,0:T(2,128)(2,1)S(1)}, bf16[1,1,128]{2,1,0:T(2,128)(2,1)}, u32[]{:S(2)}) copy-start(bf16[1,1,128]{2,1,0:T(2,128)(2,1)} %param.10) | copy-start | bytes 772
  9.3 89.9 %collective-permute-start.1 = (bf16[1,1,65792]{2,1,0:T(2,128)(2,1)S(1)}, bf16[1,1,65792]{2,1,0:T(2,128)(2,1)S(1)}, u32[]{:S(2)}, u32[]{:S(2)}) collective-permute-start(bf16[1,1,65792]{2,1,0:T(2,128)(2,1)S(1)} %pad_maximum_fusion.2), channel_id=1, source_target_pairs={{1,0},{2,1},{3,2},{4,3},{5,4},{6,5},{7,6},{8,7},{9,8},{10,9},{11,1... | collective-permute-start | bytes 394760 | tf_op jit(solution)/shard_map/ppermute | solution.py:21
  15.6 83.6 %collective-permute-start = (bf16[1,1,65792]{2,1,0:T(2,128)(2,1)S(1)}, bf16[1,1,65792]{2,1,0:T(2,128)(2,1)S(1)}, u32[]{:S(2)}, u32[]{:S(2)}) collective-permute-start(bf16[1,1,65792]{2,1,0:T(2,128)(2,1)S(1)} %pad_maximum_fusion.2), channel_id=1, source_target_pairs={{0,1},{1,2},{2,3},{3,4},{4,5},{5,6},{6,7},{7,8},{8,9},{9,10},{10,1... | collective-permute-start | bytes 394760 | tf_op jit(solution)/shard_map/ppermute | solution.py:18
  99.2 33.8 %copy-start.3 = (bf16[1,1,65792]{2,1,0:T(2,128)(2,1)}, bf16[1,1,65792]{2,1,0:T(2,128)(2,1)S(1)}, u32[]{:S(2)}) copy-start(bf16[1,1,65792]{2,1,0:T(2,128)(2,1)S(1)} %collective-permute-done.1) | copy-start | bytes 394756
  99.2 33.8 %copy-start.5 = (bf16[1,1,65792]{2,1,0:T(2,128)(2,1)}, bf16[1,1,65792]{2,1,0:T(2,128)(2,1)S(1)}, u32[]{:S(2)}) copy-start(bf16[1,1,65792]{2,1,0:T(2,128)(2,1)S(1)} %collective-permute-done) | copy-start | bytes 394756
  100.1 30.4 %collective-permute-start.3 = (bf16[1,3,65792]{2,1,0:T(4,128)(2,1)S(1)}, bf16[1,3,65792]{2,1,0:T(4,128)(2,1)S(1)}, u32[]{:S(2)}, u32[]{:S(2)}) collective-permute-start(bf16[1,3,65792]{2,1,0:T(4,128)(2,1)S(1)} %pad_maximum_fusion.1), channel_id=1, source_target_pairs={{32,0},{64,32},{96,64},{128,96},{160,128},{192,160},{224,192},{33,... | collective-permute-start | bytes 1184264 | tf_op jit(solution)/shard_map/ppermute | solution.py:21
  102.7 27.7 %collective-permute-start.2 = (bf16[1,3,65792]{2,1,0:T(4,128)(2,1)S(1)}, bf16[1,3,65792]{2,1,0:T(4,128)(2,1)S(1)}, u32[]{:S(2)}, u32[]{:S(2)}) collective-permute-start(bf16[1,3,65792]{2,1,0:T(4,128)(2,1)S(1)} %pad_maximum_fusion.1), channel_id=1, source_target_pairs={{0,32},{32,64},{64,96},{96,128},{128,160},{160,192},{192,224},{1,3... | collective-permute-start | bytes 1184264 | tf_op jit(solution)/shard_map/ppermute | solution.py:18
  130.5 2.6 %copy-start = (bf16[1,3,65792]{2,1,0:T(4,128)(2,1)}, bf16[1,3,65792]{2,1,0:T(4,128)(2,1)S(1)}, u32[]{:S(2)}) copy-start(bf16[1,3,65792]{2,1,0:T(4,128)(2,1)S(1)} %collective-permute-done.3) | copy-start | bytes 1184260
  130.5 2.6 %copy-start.2 = (bf16[1,3,65792]{2,1,0:T(4,128)(2,1)}, bf16[1,3,65792]{2,1,0:T(4,128)(2,1)S(1)}, u32[]{:S(2)}) copy-start(bf16[1,3,65792]{2,1,0:T(4,128)(2,1)S(1)} %collective-permute-done.2) | copy-start | bytes 1184260
  151.5 4.1 %copy-start.1 = (bf16[1,3,65792]{2,1,0:T(4,128)(2,1)S(1)}, bf16[1,3,65792]{2,1,0:T(4,128)(2,1)}, u32[]{:S(2)}) copy-start(bf16[1,3,65792]{2,1,0:T(4,128)(2,1)} %copy-done) | copy-start | bytes 1184260
  151.5 4.1 %copy-start.4 = (bf16[1,1,65792]{2,1,0:T(2,128)(2,1)S(1)}, bf16[1,1,65792]{2,1,0:T(2,128)(2,1)}, u32[]{:S(2)}) copy-start(bf16[1,1,65792]{2,1,0:T(2,128)(2,1)} %copy-done.3) | copy-start | bytes 394756
  156.7 15.0 %copy-start.6 = (bf16[1152,512]{1,0:T(8,128)(2,1)S(1)}, bf16[1152,512]{1,0:T(8,128)(2,1)}, u32[]{:S(2)}) copy-start(bf16[1152,512]{1,0:T(8,128)(2,1)} %convert_element_type.75) | copy-start | bytes 3538948
  156.7 15.0 %copy-start.7 = (bf16[1152,512]{1,0:T(8,128)(2,1)S(1)}, bf16[1152,512]{1,0:T(8,128)(2,1)}, u32[]{:S(2)}) copy-start(bf16[1152,512]{1,0:T(8,128)(2,1)} %reshape_reshape.3) | copy-start | bytes 3538948
  174.8 2.4 %copy-start.17 = (f32[512,512]{1,0:T(8,128)S(1)}, f32[512,512]{1,0:T(8,128)}, u32[]{:S(2)}) copy-start(f32[512,512]{1,0:T(8,128)} %get-tuple-element.8) | copy-start | bytes 3145732
  191.6 8.7 %copy-start.9 = (bf16[1,1,512,1024]{3,2,1,0:T(8,128)(2,1)S(1)}, bf16[1,1,512,1024]{3,2,1,0:T(8,128)(2,1)}, u32[]{:S(2)}) copy-start(bf16[1,1,512,1024]{3,2,1,0:T(8,128)(2,1)} %param.8) | copy-start | bytes 3145732
  191.6 8.8 %copy-start.13 = (f32[1024]{0:T(1024)S(1)}, f32[1024]{0:T(1024)}, u32[]{:S(2)}) copy-start(f32[1024]{0:T(1024)} %broadcast_multiply_fusion) | copy-start | bytes 12292
Sparse Core Ops, SparseCore 0:
  17.8 110.0 all-gather.1
where the time goes:
time: 211 us; the launch traced here: 209 us
  blocking collectives  79 us (37%)
  matrix products  45.3 us (21%)
  local copies, waits for them, and re-layouts  21 us (10%)
  waiting for transfers between devices  19.6 us (9%)
  starting transfers between devices  16 us (8%)
  between operations  15.2 us (7%)
  other arithmetic  13.4 us (6%)
    all_gather x1, blocking collectives, shards(): targets = lax.all_gather(sat_targets, 'lon', axis=1, tiled=True)  32.9 us
    all_gather x1, blocking collectives, shards(): misfit = lax.all_gather(sat_misfit, 'lon', axis=1, tiled=True)  32.2 us
    ppermute x2, waiting for transfers between devices, extended(): lax.ppermute(lax.slice_in_dim(block, 0, width, axis=dim), axis, backward)  19.6 us
    dot_general x2, matrix products, outer_sum(): lax.dot_general(scaled, spread, (((0,), (0,)), ((), ())), preferred_eleme...  17.4 us
    unnamed x1, blocking collectives  13.8 us
    ppermute x2, starting transfers between devices, extended(): lax.ppermute(lax.slice_in_dim(block, 0, width, axis=dim), axis, backward)  8.95 us
    dot_general x1, matrix products, shards(): jnp.dot(misfit.reshape(-1), scaled, preferred_element_type=jnp.float32)  7.73 us
    ppermute x2, starting transfers between devices, extended(): lax.ppermute(lax.slice_in_dim(block, block.shape[dim] - width, None, axis...  6.99 us
  transfers between devices with their start and end apart: 5, of which 1 were waited for; matrix products, arithmetic and copies ran while one was open for 15% of the time, Pallas kernels for 0%

commit v1 on v0

v1 whole, which is shorter than its diff:
```python
import functools

import jax
import jax.numpy as jnp
from jax import lax
from jax.experimental import pallas as pl
from jax.experimental.pallas import tpu as pltpu
from jax.sharding import PartitionSpec as P

BLK = 16
LOC = 2
F32 = jnp.float32
BF16 = jnp.bfloat16
PAD = 16
VMEM = pltpu.VMEM
SMEM = pltpu.SMEM
LIMIT = 48 * 1024 * 1024


def call(body, outs, in_spaces, scratch=(), flops=0, moved=0):
    return pl.pallas_call(
        body,
        out_shape=outs,
        in_specs=[pl.BlockSpec(memory_space=space) for space in in_spaces],
        out_specs=jax.tree.map(lambda _: pl.BlockSpec(memory_space=VMEM), outs),
        scratch_shapes=list(scratch),
        compiler_params=pltpu.CompilerParams(vmem_limit_bytes=LIMIT),
        cost_estimate=pl.CostEstimate(flops=flops, bytes_accessed=moved, transcendentals=0),
    )


def transposed_dot(left, right):
    return lax.dot_general(left, right, (((0,), (0,)), ((), ())), preferred_element_type=F32)


def dot(left, right):
    return jnp.dot(left, right, preferred_element_type=F32)


def background_body(ensemble_ref, anomaly_ref, mean_ref):
    values = ensemble_ref[...].astype(F32)
    mean = jnp.mean(values, axis=0, keepdims=True)
    mean_ref[...] = mean
    anomaly_ref[...] = (values - mean).astype(BF16)


def route_body(pert_ref, misfit_ref, rows_ref, targets_ref, slots_ref, drive_ref, entry_ref, count_ref):
    tiles, obs, members = pert_ref.shape
    blocks = slots_ref.shape[0]

    def clear(block, _):
        count_ref[block] = 0
        entry_ref[2 * block] = -1
        entry_ref[2 * block + 1] = -1
        return 0

    lax.fori_loop(0, blocks, clear, 0)
    for tile in range(tiles):
        for k in range(LOC):
            block = targets_ref[LOC * tile + k]
            used = count_ref[block]
            entry_ref[2 * block + used] = LOC * tile + k
            count_ref[block] = used + 1
    row = lax.broadcasted_iota(jnp.int32, (obs, members), 0)

    def fill(slot, _):
        entry = entry_ref[slot]
        safe = jnp.maximum(entry, 0)
        tile = safe // LOC
        live = jnp.where(entry >= 0, rows_ref[tile], 0)
        factor = jnp.where(safe % LOC == 0, 1.0, 0.5**0.5).astype(F32)
        values = pert_ref[tile].astype(F32) * factor
        start = pl.multiple_of((slot % 2) * obs, obs)
        slots_ref[slot // 2, pl.ds(start, obs), :] = jnp.where(row < live, values, 0.0).astype(BF16)
        return 0

    lax.fori_loop(0, 2 * blocks, fill, 0)
    total = tiles * obs
    lane = lax.broadcasted_iota(jnp.int32, (1, total), 1)
    own_tile = lane // obs
    live = jnp.zeros((1, total), jnp.int32)
    named = [jnp.zeros((1, total), jnp.int32) for _ in range(LOC)]
    for tile in range(tiles):
        here = own_tile == tile
        live = jnp.where(here, rows_ref[tile], live)
        for k in range(LOC):
            named[k] = jnp.where(here, targets_ref[LOC * tile + k], named[k])
    repeat = (
        lax.broadcasted_iota(jnp.int32, (obs, total), 1) % obs
        == lax.broadcasted_iota(jnp.int32, (obs, total), 0)
    )
    spread = dot(misfit_ref[...], jnp.where(repeat, 1.0, 0.0).astype(BF16))
    pick = lax.broadcasted_iota(jnp.int32, (tiles, total), 1) // obs == lax.broadcasted_iota(
        jnp.int32, (tiles, total), 0
    )
    misfit = jnp.sum(jnp.where(pick, spread, 0.0), axis=0, keepdims=True)
    misfit = jnp.where(lane % obs < live, misfit, 0.0)
    block = lax.broadcasted_iota(jnp.int32, (blocks, total), 0)
    weight = jnp.zeros((blocks, total), F32)
    for k in range(LOC):
        weight = weight + jnp.where(block == named[k], 0.5**k, 0.0)
    drive_ref[...] = dot((weight * misfit).astype(BF16), pert_ref[...].reshape(total, members))


def conv_body(middle_ref, south_ref, north_ref, gram_ref, drive_ref, scaled_ref, spread_ref):
    conv, members = middle_ref.shape[1] - PAD, middle_ref.shape[2]
    eye = lax.broadcasted_iota(jnp.int32, (conv, conv), 0) == lax.broadcasted_iota(
        jnp.int32, (conv, conv), 1
    )
    drive = jnp.zeros((8, members), F32)
    for a, ref in ((-1, south_ref), (0, middle_ref), (1, north_ref)):
        for b in (-1, 0, 1):
            misfit = ref[b + 1, conv : conv + 1, 0:conv]
            column = ref[b + 1, conv : conv + 1, conv : 2 * conv].astype(F32)
            lat_cell = jnp.floor(column * (1.0 / BLK))
            lon_cell = column - BLK * lat_cell
            lat_place = BLK * a + lat_cell + 0.5 - 0.5 * BLK
            lon_place = BLK * b + lon_cell + 0.5 - 0.5 * BLK
            weight = jnp.exp(-(lat_place * lat_place + lon_place * lon_place) / (2.0 * BLK * BLK))
            weight = jnp.sum(jnp.where(eye, weight, 0.0), axis=1, keepdims=True)
            rows = ref[b + 1, 0:conv, :]
            scaled = (weight * rows.astype(F32)).astype(BF16)
            at = ((a + 1) * 3 + b + 1) * conv
            scaled_ref[at : at + conv, :] = scaled
            spread_ref[at : at + conv, :] = rows
            drive = drive + dot(jnp.broadcast_to(misfit, (8, conv)), scaled)
    drive_ref[...] = drive[0:1]
    gram_ref[...] = transposed_dot(scaled_ref[...], spread_ref[...])


def root_and_apply(gram, drive, mean_ref, anomaly_ref, out_ref):
    members = gram.shape[0]
    eye = lax.broadcasted_iota(jnp.int32, gram.shape, 0) == lax.broadcasted_iota(
        jnp.int32, gram.shape, 1
    )
    system = gram + jnp.where(eye, members - 1.0, 0.0)
    square = jnp.sum(jnp.sum(system * system, axis=0, keepdims=True), axis=1, keepdims=True)
    inverse_scale = lax.rsqrt(square)
    power1 = system * inverse_scale
    half1 = power1.astype(BF16)
    power2 = dot(half1, half1)
    half2 = power2.astype(BF16)
    power3 = dot(half1, half2)
    power4 = dot(half2, half2)
    product = 2.25 * power1 - 1.5 * power2 + 0.25 * power3
    excess = -0.75 * (power1 + product) + 0.25 * (2.25 * power2 - 1.5 * power3 + 0.25 * power4)
    half_excess = excess.astype(BF16)
    lifted = 4.5 * excess + dot(half_excess, half_excess)
    product = 5.0625 * power1 + dot(half1, lifted.astype(BF16))
    inverse_root = 1.5 * excess - 1.125 * product - 0.5 * dot(product.astype(BF16), half_excess)
    inverse_root = inverse_root + jnp.where(eye, 3.375, 0.0)
    first = jnp.sum(inverse_root * drive, axis=1, keepdims=True)
    weight = jnp.sum(inverse_root * first, axis=0, keepdims=True) * inverse_scale
    transform = (jnp.sqrt((members - 1.0) * inverse_scale) * inverse_root + weight).astype(BF16)
    out_ref[...] = mean_ref[...] + dot(transform, anomaly_ref[...])


def final_body(rows_ref, conv_ref, drive1_ref, drive2_ref, mean_ref, anomaly_ref, out_ref):
    rows = rows_ref[...]
    gram = conv_ref[...] + transposed_dot(rows, rows)
    root_and_apply(gram, drive1_ref[...] + drive2_ref[...], mean_ref, anomaly_ref, out_ref)


def shards(
    background, conv_pert, conv_misfit, conv_column, sat_pert, sat_misfit, sat_rows, sat_targets
):
    members, cells = background.shape[2:]
    conv = conv_pert.shape[2]
    tiles, obs = sat_pert.shape[1:3]
    blocks, bands = lax.axis_size("lon"), lax.axis_size("lat")
    shape = jax.ShapeDtypeStruct

    extra = jnp.concatenate([conv_misfit[0], conv_column[0].astype(BF16)], axis=1)
    extra = jnp.pad(extra, ((0, PAD - 1), (0, members - 2 * conv)))
    own = jnp.concatenate([conv_pert[0, 0], extra], axis=0)
    east = [(i, (i + 1) % blocks) for i in range(blocks)]
    west = [(target, source) for source, target in east]
    low = lax.ppermute(own, "lon", east)
    high = lax.ppermute(own, "lon", west)

    slots, drive = call(
        route_body,
        (shape((blocks, 2 * obs, members), BF16), shape((blocks, members), F32)),
        [VMEM, VMEM, SMEM, SMEM],
        [pltpu.SMEM((2 * blocks,), jnp.int32), pltpu.SMEM((blocks,), jnp.int32)],
    )(sat_pert[0], sat_misfit[0], sat_rows[0], sat_targets.reshape(-1))

    middle = jnp.stack([low, own, high])
    up = [(i, i + 1) for i in range(bands - 1)]
    down = [(target, source) for source, target in up]
    south = lax.ppermute(middle, "lat", up)
    north = lax.ppermute(middle, "lat", down)
    drive_sat = lax.psum_scatter(drive, "lon", scatter_dimension=0, tiled=True)
    rows = lax.all_to_all(slots, "lon", 0, 0, tiled=True).reshape(blocks * 2 * obs, members)

    anomaly, mean = call(
        background_body, (shape((members, cells), BF16), shape((1, cells), F32)), [VMEM]
    )(background[0, 0])
    gram_conv, drive_conv = call(
        conv_body,
        (shape((members, members), F32), shape((1, members), F32)),
        [VMEM] * 3,
        [pltpu.VMEM((9 * conv, members), BF16), pltpu.VMEM((9 * conv, members), BF16)],
    )(middle, south, north)
    result = call(final_body, shape((members, cells), F32), [VMEM] * 6)(
        rows, gram_conv, drive_conv, drive_sat, mean, anomaly
    )
    return result[None, None]


def solution(mesh):
    placed = (
        P("lat", "lon", None, None),
        P("lat", "lon", None, None),
        P("lat", "lon", None),
        P("lat", "lon", None),
        P("lat", "lon", None, None),
        P("lat", "lon", None),
        P("lat", "lon"),
        P("lat", "lon", None),
    )
    return jax.shard_map(
        shards, mesh=mesh, in_specs=placed, out_specs=P("lat", "lon", None, None), check_vma=False
    )
```

time: 211 us -> 294 us (1.39)
  waiting for transfers between devices: 19.6 us -> 237 us
  blocking collectives: 79 us -> 0 us
  matrix products: 45.3 us -> 0 us
  other arithmetic: 13.4 us -> 0.09 us
  Pallas kernels: 0 us -> 10.7 us
  local copies, waits for them, and re-layouts: 21 us -> 12.1 us
  starting transfers between devices: 16 us -> 20.1 us
    unnamed x1 -> x2, waiting for transfers between devices: 0.02 us -> 189 us
    all_gather x2 -> x0, blocking collectives: 65.2 us -> none  [the longest x1 32.9 us: shards(): targets = lax.all_gather(sat_targets, 'lon', axis=1, tiled=True)]
    dot_general x15 -> x0, matrix products: 45.3 us -> none  [the longest x2 17.4 us: outer_sum(): lax.dot_general(scaled, spread, (((0,), (0,)), ((), ())), preferred_eleme...]
    ppermute x4, waiting for transfers between devices: 19.6 us -> 47.1 us  [the longest x1 47.1 us: shards(): low = lax.ppermute(own, 'lon', east)]
    unnamed x1 -> x0, blocking collectives: 13.8 us -> none
    pallas_call x0 -> x4, Pallas kernels: none -> 10.7 us  [the longest x1 5.92 us: shards(): call(final_body, shape((members, cells), F32), [VMEM] * 6)]
    all_to_all x0 -> x1, starting transfers between devices: none -> 9.91 us  [shards(): lax.all_to_all(slots, 'lon', 0, 0, tiled=True)]
    unnamed x41 -> x29, local copies, waits for them, and re-layouts: 2.99 us -> 12 us
  transfers between devices with their start and end apart: 5 -> 6, of which waited for: 1 -> 2; matrix products, arithmetic and copies ran while one was open for 15% -> 1% of each run, Pallas kernels for 0% -> 1%
where the time goes in v1:
time: 294 us; the launch traced here: 293 us
  waiting for transfers between devices  237 us (81%)
  starting transfers between devices  20.1 us (7%)
  between operations  13.5 us (5%)
  local copies, waits for them, and re-layouts  12.1 us (4%)
  Pallas kernels  10.7 us (4%)
    unnamed x2, waiting for transfers between devices  189 us
    ppermute x1, waiting for transfers between devices, shards(): low = lax.ppermute(own, 'lon', east)  47.1 us
    unnamed x29, local copies, waits for them, and re-layouts  12 us
    all_to_all x1, starting transfers between devices, shards(): lax.all_to_all(slots, 'lon', 0, 0, tiled=True)  9.91 us
    pallas_call x1, Pallas kernels, shards(): call(final_body, shape((members, cells), F32), [VMEM] * 6)  5.92 us
  transfers between devices with their start and end apart: 6, of which 2 were waited for; matrix products, arithmetic and copies ran while one was open for 1% of the time, Pallas kernels for 1%

profile of v1, /device:TPU:24, one launch (start us, length us, event | category | flops | bytes accessed | tf_op | source)
XLA Modules:
  0.0 293.1 jit_solution(17516076294043301735)
XLA Ops:
  6.5 0.8 copy.11
  7.3 0.1 reshape.19.targets_ref
  7.4 1.0 copy-done.6
  8.4 0.7 copy-done.7
  9.1 0.7 copy-done.8
  9.8 3.2 %shard_map.82 = (bf16[32,64,512]{2,1,0:T(8,128)(2,1)S(1)}, f32[32,512]{1,0:T(8,128)}) custom-call(bf16[16,32,512]{2,1,0:T(8,128)(2,1)S(1)} %bitcast.17, bf16[16,32]{1,0:T(8,128)(2,1)S(1)} %bitcast.18, s32[16]{0:T(128)S(1)} %bitcast.19, s32[32]{0:T(128)S(1)} %reshape.19.targets_ref), custom_call_target="tpu_custom_call" | custom-call | tf_op jit(solution)/shard_map/pallas_call | solution.py:181
  13.0 1.3 copy-done
  14.3 9.9 %all-to-all-start = ((bf16[32,64,512]{2,1,0:T(8,128)(2,1)}), bf16[32,64,512]{2,1,0:T(8,128)(2,1)S(1)}, u32[]{:S(2)}, u32[]{:S(2)}) async-start(bf16[32,64,512]{2,1,0:T(8,128)(2,1)} %copy-done), calls=%async_computation | async-start | bytes 4194304 | tf_op jit(solution)/shard_map/all_to_all | solution.py:194
  24.4 0.4 collective-permute-start
  24.7 3.6 %collective-permute-start.1 = (bf16[144,512]{1,0:T(8,128)(2,1)S(1)}, bf16[144,512]{1,0:T(8,128)(2,1)S(1)}, u32[]{:S(2)}, u32[]{:S(2)}) collective-permute-start(bf16[144,512]{1,0:T(8,128)(2,1)S(1)} %get-tuple-element.18), channel_id=1, source_target_pairs={{1,0},{2,1},{3,2},{4,3},{5,4},{6,5},{7,6},{8,7},{9,8},{10,9},{11,1... | collective-permute-start | bytes 442376 | tf_op jit(solution)/shard_map/ppermute | solution.py:179
  28.3 47.1 %collective-permute-done = bf16[144,512]{1,0:T(8,128)(2,1)S(1)} collective-permute-done((bf16[144,512]{1,0:T(8,128)(2,1)S(1)}, bf16[144,512]{1,0:T(8,128)(2,1)S(1)}, u32[]{:S(2)}, u32[]{:S(2)}) %collective-permute-start) | collective-permute-done | bytes 147488 | tf_op jit(solution)/shard_map/ppermute | solution.py:178
  75.5 4.3 %collective-permute-start.2 = (bf16[3,144,512]{2,1,0:T(8,128)(2,1)S(1)}, bf16[3,144,512]{2,1,0:T(8,128)(2,1)S(1)}, u32[]{:S(2)}, u32[]{:S(2)}) collective-permute-start(bf16[3,144,512]{2,1,0:T(8,128)(2,1)S(1)} %pad_maximum_fusion.middle_ref), channel_id=1, source_target_pairs={{0,32},{32,64},{64,96},{96,128},{128,160},{160,192},{192,224},{1,3... | collective-permute-start | bytes 1327112 | tf_op jit(solution)/shard_map/ppermute | solution.py:191
  79.8 1.9 collective-permute-start.3
  81.7 1.2 copy-done.1
  83.0 0.4 shard_map.84
  83.4 1.0 copy-done.2
  84.4 0.6 dynamic-slice
  85.0 189.4 %all-reduce.4.cloned.1.call-done = f32[32,512]{1,0:T(8,128)} async-done(((f32[32,512]{1,0:T(8,128)}), f32[32,512]{1,0:T(8,128)}) %all-reduce.4.cloned.1.call-update) | async-done | bytes 65552
  274.4 1.3 constant_dynamic-slice_fusion.drive2_ref
  275.8 1.2 shard_map.83
  276.9 1.0 copy-done.4
  277.9 1.2 copy-done.3
  279.1 1.2 copy-done.5
  280.4 5.9 %shard_map.85 = f32[512,1024]{1,0:T(8,128)} custom-call(bf16[2048,512]{1,0:T(8,128)(2,1)S(1)} %bitcast.15, f32[512,512]{1,0:T(8,128)S(1)} %copy-done.5, f32[1,512]{1,0:T(1,128)S(1)} %get-tuple-element.13.drive1_ref, f32[1,512]{1,0:T(1,128)S(1)} %constant_dynamic-slice_fusion.drive2_ref, f32[1,1024]{1,0:T(1,128)S(1)} %get-tuple-element.15.mean_ref, ...), custom_call_target="tpu_custom_call" | custom-call | tf_op jit(solution)/shard_map/pallas_call | solution.py:205
  (27 shorter events, 0.2 us)
Async XLA Ops:
  7.4 1.0 copy-start.6
  8.4 0.7 copy-start.7
  9.1 0.7 copy-start.8
  13.0 1.3 copy-start
  14.3 10.0 %copy-start.11 = (s32[1,1,128]{2,1,0:T(1,128)S(1)}, s32[1,1,128]{2,1,0:T(1,128)}, u32[]{:S(2)}) copy-start(s32[1,1,128]{2,1,0:T(1,128)} %param.11) | copy-start | bytes 1540
  14.3 10.0 %copy-start.10 = (bf16[1,1,128]{2,1,0:T(2,128)(2,1)S(1)}, bf16[1,1,128]{2,1,0:T(2,128)(2,1)}, u32[]{:S(2)}) copy-start(bf16[1,1,128]{2,1,0:T(2,128)(2,1)} %param.10) | copy-start | bytes 772
  14.3 10.0 %copy-start.9 = (bf16[1,1,128,512]{3,2,1,0:T(8,128)(2,1)S(1)}, bf16[1,1,128,512]{3,2,1,0:T(8,128)(2,1)}, u32[]{:S(2)}) copy-start(bf16[1,1,128,512]{3,2,1,0:T(8,128)(2,1)} %param.9) | copy-start | bytes 393220
  14.3 263.6 %all-to-all-start = ((bf16[32,64,512]{2,1,0:T(8,128)(2,1)}), bf16[32,64,512]{2,1,0:T(8,128)(2,1)S(1)}, u32[]{:S(2)}, u32[]{:S(2)}) async-start(bf16[32,64,512]{2,1,0:T(8,128)(2,1)} %copy-done), calls=%async_computation | async-start | bytes 4194304 | tf_op jit(solution)/shard_map/all_to_all | solution.py:194
  24.2 60.2 %copy-start.12 = (u32[256]{0:T(256)S(1)}, u32[256]{0:T(256)}, u32[]{:S(2)}) copy-start(u32[256]{0:T(256)} %constant.15) | copy-start | bytes 3076
  24.2 250.2 %all-reduce.4.cloned.1.call-start = ((), (), s32[]{:S(2)}) async-start(), calls=%async_computation.1 | async-start | bytes 131072
  24.4 51.0 %collective-permute-start = (bf16[144,512]{1,0:T(8,128)(2,1)S(1)}, bf16[144,512]{1,0:T(8,128)(2,1)S(1)}, u32[]{:S(2)}, u32[]{:S(2)}) collective-permute-start(bf16[144,512]{1,0:T(8,128)(2,1)S(1)} %get-tuple-element.18), channel_id=1, source_target_pairs={{0,1},{1,2},{2,3},{3,4},{4,5},{5,6},{6,7},{7,8},{8,9},{9,10},{10,1... | collective-permute-start | bytes 442376 | tf_op jit(solution)/shard_map/ppermute | solution.py:178
  24.7 50.7 %collective-permute-start.1 = (bf16[144,512]{1,0:T(8,128)(2,1)S(1)}, bf16[144,512]{1,0:T(8,128)(2,1)S(1)}, u32[]{:S(2)}, u32[]{:S(2)}) collective-permute-start(bf16[144,512]{1,0:T(8,128)(2,1)S(1)} %get-tuple-element.18), channel_id=1, source_target_pairs={{1,0},{2,1},{3,2},{4,3},{5,4},{6,5},{7,6},{8,7},{9,8},{10,9},{11,1... | collective-permute-start | bytes 442376 | tf_op jit(solution)/shard_map/ppermute | solution.py:179
  75.5 200.3 %collective-permute-start.2 = (bf16[3,144,512]{2,1,0:T(8,128)(2,1)S(1)}, bf16[3,144,512]{2,1,0:T(8,128)(2,1)S(1)}, u32[]{:S(2)}, u32[]{:S(2)}) collective-permute-start(bf16[3,144,512]{2,1,0:T(8,128)(2,1)S(1)} %pad_maximum_fusion.middle_ref), channel_id=1, source_target_pairs={{0,32},{32,64},{64,96},{96,128},{128,160},{160,192},{192,224},{1,3... | collective-permute-start | bytes 1327112 | tf_op jit(solution)/shard_map/ppermute | solution.py:191
  79.8 196.0 %collective-permute-start.3 = (bf16[3,144,512]{2,1,0:T(8,128)(2,1)S(1)}, bf16[3,144,512]{2,1,0:T(8,128)(2,1)S(1)}, u32[]{:S(2)}, u32[]{:S(2)}) collective-permute-start(bf16[3,144,512]{2,1,0:T(8,128)(2,1)S(1)} %pad_maximum_fusion.middle_ref), channel_id=1, source_target_pairs={{32,0},{64,32},{96,64},{128,96},{160,128},{192,160},{224,192},{33,... | collective-permute-start | bytes 1327112 | tf_op jit(solution)/shard_map/ppermute | solution.py:192
  81.7 1.2 copy-start.1
  83.4 1.0 copy-start.2
  276.9 1.0 copy-start.4
  277.9 1.2 copy-start.3
  279.1 1.2 copy-start.5
Sparse Core Ops, SparseCore 0:
  81.8 192.5 all-reduce.3

commit v2 on v1

--- a/solution.py
+++ b/solution.py
@@ -12,6 +12,7 @@
 F32 = jnp.float32
 BF16 = jnp.bfloat16
 PAD = 16
+LANES = 128
 VMEM = pltpu.VMEM
 SMEM = pltpu.SMEM
 LIMIT = 48 * 1024 * 1024
@@ -44,7 +45,7 @@
     anomaly_ref[...] = (values - mean).astype(BF16)
 
 
-def route_body(pert_ref, misfit_ref, rows_ref, targets_ref, slots_ref, drive_ref, entry_ref, count_ref):
+def route_body(pert_ref, misfit_ref, rows_ref, targets_ref, slots_ref, entry_ref, count_ref):
     tiles, obs, members = pert_ref.shape
     blocks = slots_ref.shape[0]
 
@@ -70,8 +71,10 @@
         live = jnp.where(entry >= 0, rows_ref[tile], 0)
         factor = jnp.where(safe % LOC == 0, 1.0, 0.5**0.5).astype(F32)
         values = pert_ref[tile].astype(F32) * factor
-        start = pl.multiple_of((slot % 2) * obs, obs)
-        slots_ref[slot // 2, pl.ds(start, obs), :] = jnp.where(row < live, values, 0.0).astype(BF16)
+        values = jnp.where(row < live, values, 0.0).astype(BF16)
+        for part in range(members // LANES):
+            start = pl.multiple_of(part * 2 * obs + (slot % 2) * obs, obs)
+            slots_ref[slot // 2, pl.ds(start, obs), :] = values[:, part * LANES : (part + 1) * LANES]
         return 0
 
     lax.fori_loop(0, 2 * blocks, fill, 0)
@@ -99,7 +102,14 @@
     weight = jnp.zeros((blocks, total), F32)
     for k in range(LOC):
         weight = weight + jnp.where(block == named[k], 0.5**k, 0.0)
-    drive_ref[...] = dot((weight * misfit).astype(BF16), pert_ref[...].reshape(total, members))
+    drive = dot((weight * misfit).astype(BF16), pert_ref[...].reshape(total, members))
+    upper = drive.astype(BF16).astype(F32)
+    parts = []
+    for piece in (upper, drive - upper):
+        for part in range(members // LANES):
+            parts.append(piece[:, None, part * LANES : (part + 1) * LANES])
+    parts.append(jnp.zeros((blocks, PAD - len(parts), LANES), F32))
+    slots_ref[:, members // LANES * 2 * obs :, :] = jnp.concatenate(parts, axis=1).astype(BF16)
 
 
 def conv_body(middle_ref, south_ref, north_ref, gram_ref, drive_ref, scaled_ref, spread_ref):
@@ -155,10 +165,19 @@
     out_ref[...] = mean_ref[...] + dot(transform, anomaly_ref[...])
 
 
-def final_body(rows_ref, conv_ref, drive1_ref, drive2_ref, mean_ref, anomaly_ref, out_ref):
+def final_body(slots_ref, conv_ref, drive_ref, mean_ref, anomaly_ref, out_ref, rows_ref):
+    blocks, pieces = slots_ref.shape[0], out_ref.shape[0] // LANES
+    count = (slots_ref.shape[1] - PAD) // pieces
+    for part in range(pieces):
+        rows_ref[:, part * LANES : (part + 1) * LANES] = slots_ref[
+            :, part * count : (part + 1) * count, :
+        ].reshape(blocks * count, LANES)
     rows = rows_ref[...]
     gram = conv_ref[...] + transposed_dot(rows, rows)
-    root_and_apply(gram, drive1_ref[...] + drive2_ref[...], mean_ref, anomaly_ref, out_ref)
+    extra = jnp.sum(slots_ref[:, pieces * count :, :].astype(F32), axis=0)
+    extra = extra[0:pieces] + extra[pieces : 2 * pieces]
+    extra = jnp.concatenate([extra[part : part + 1] for part in range(pieces)], axis=1)
+    root_and_apply(gram, drive_ref[...] + extra, mean_ref, anomaly_ref, out_ref)
 
 
 def shards(
@@ -178,9 +197,9 @@
     low = lax.ppermute(own, "lon", east)
     high = lax.ppermute(own, "lon", west)
 
-    slots, drive = call(
+    slots = call(
         route_body,
-        (shape((blocks, 2 * obs, members), BF16), shape((blocks, members), F32)),
+        shape((blocks, members // LANES * 2 * obs + PAD, LANES), BF16),
         [VMEM, VMEM, SMEM, SMEM],
         [pltpu.SMEM((2 * blocks,), jnp.int32), pltpu.SMEM((blocks,), jnp.int32)],
     )(sat_pert[0], sat_misfit[0], sat_rows[0], sat_targets.reshape(-1))
@@ -190,8 +209,7 @@
     down = [(target, source) for source, target in up]
     south = lax.ppermute(middle, "lat", up)
     north = lax.ppermute(middle, "lat", down)
-    drive_sat = lax.psum_scatter(drive, "lon", scatter_dimension=0, tiled=True)
-    rows = lax.all_to_all(slots, "lon", 0, 0, tiled=True).reshape(blocks * 2 * obs, members)
+    slots = lax.all_to_all(slots, "lon", 0, 0, tiled=True)
 
     anomaly, mean = call(
         background_body, (shape((members, cells), BF16), shape((1, cells), F32)), [VMEM]
@@ -202,9 +220,12 @@
         [VMEM] * 3,
         [pltpu.VMEM((9 * conv, members), BF16), pltpu.VMEM((9 * conv, members), BF16)],
     )(middle, south, north)
-    result = call(final_body, shape((members, cells), F32), [VMEM] * 6)(
-        rows, gram_conv, drive_conv, drive_sat, mean, anomaly
-    )
+    result = call(
+        final_body,
+        shape((members, cells), F32),
+        [VMEM] * 5,
+        [pltpu.VMEM((blocks * 2 * obs, members), BF16)],
+    )(slots, gram_conv, drive_conv, mean, anomaly)
     return result[None, None]
 
 

time: 294 us -> 99.4 us (0.34)
  waiting for transfers between devices: 237 us -> 60.4 us
  between operations: 13.5 us -> 0.13 us
  local copies, waits for them, and re-layouts: 12.1 us -> 8 us
    unnamed x2 -> x0, waiting for transfers between devices: 189 us -> none
    ppermute x1, waiting for transfers between devices: 0.01 us -> 46.2 us  [shards(): high = lax.ppermute(own, 'lon', west)]
    ppermute x1, waiting for transfers between devices: 47.1 us -> 3.95 us  [shards(): low = lax.ppermute(own, 'lon', east)]
    ppermute x1, waiting for transfers between devices: 0.01 us -> 7.92 us  [shards(): north = lax.ppermute(middle, 'lat', down)]
    unnamed x29 -> x21, local copies, waits for them, and re-layouts: 12 us -> 7.92 us
  transfers between devices with their start and end apart: 6 -> 5, of which waited for: 2 -> 4; matrix products, arithmetic and copies ran while one was open for 1% -> 0% of each run, Pallas kernels for 1% -> 2%
where the time goes in v2:
time: 99.4 us; the launch traced here: 99 us
  waiting for transfers between devices  60.4 us (61%)
  starting transfers between devices  20 us (20%)
  Pallas kernels  10.4 us (10%)
  local copies, waits for them, and re-layouts  8 us (8%)
    ppermute x1, waiting for transfers between devices, shards(): high = lax.ppermute(own, 'lon', west)  46.2 us
    all_to_all x1, starting transfers between devices, shards(): slots = lax.all_to_all(slots, 'lon', 0, 0, tiled=True)  9.92 us
    ppermute x1, waiting for transfers between devices, shards(): north = lax.ppermute(middle, 'lat', down)  7.92 us
    unnamed x21, local copies, waits for them, and re-layouts  7.92 us
    pallas_call x1, Pallas kernels, shards(): call(final_body, shape((members, cells), F32), [VMEM] * 5, [pltpu.VMEM((b...  6.06 us
    ppermute x1, starting transfers between devices, shards(): south = lax.ppermute(middle, 'lat', up)  4.3 us
    ppermute x1, waiting for transfers between devices, shards(): low = lax.ppermute(own, 'lon', east)  3.95 us
    ppermute x1, starting transfers between devices, shards(): high = lax.ppermute(own, 'lon', west)  3.82 us
  transfers between devices with their start and end apart: 5, of which 4 were waited for; matrix products, arithmetic and copies ran while one was open for 0% of the time, Pallas kernels for 2%

profile of v2, /device:TPU:24, one launch (start us, length us, event | category | flops | bytes accessed | tf_op | source)
XLA Modules:
  0.0 99.0 jit_solution(10386584458628098078)
XLA Ops:
  0.0 0.8 copy.10
  0.8 0.1 reshape.16.targets_ref
  0.8 0.0 copy-start.4
  0.9 1.0 %copy-done.4 = bf16[1,16,32,512]{3,2,1,0:T(8,128)(2,1)S(1)} copy-done((bf16[1,16,32,512]{3,2,1,0:T(8,128)(2,1)S(1)}, bf16[1,16,32,512]{3,2,1,0:T(8,128)(2,1)}, u32[]{:S(2)}) %copy-start.4) | copy-done | bytes 524312
  1.9 0.7 copy-done.5
  2.6 0.7 copy-done.6
  3.2 2.7 %shard_map.82 = bf16[32,272,128]{2,1,0:T(8,128)(2,1)S(1)} custom-call(bf16[16,32,512]{2,1,0:T(8,128)(2,1)S(1)} %bitcast.14, bf16[16,32]{1,0:T(8,128)(2,1)S(1)} %bitcast.15, s32[16]{0:T(128)S(1)} %bitcast.16, s32[32]{0:T(128)S(1)} %reshape.16.targets_ref), custom_call_target="tpu_custom_call" | custom-call | tf_op jit(solution)/shard_map/pallas_call | solution.py:200
  6.0 1.4 %copy-done = bf16[32,272,128]{2,1,0:T(8,128)(2,1)} copy-done((bf16[32,272,128]{2,1,0:T(8,128)(2,1)}, bf16[32,272,128]{2,1,0:T(8,128)(2,1)S(1)}, u32[]{:S(2)}) %copy-start) | copy-done | bytes 2228248
  7.4 9.9 %all-to-all-start = ((bf16[32,272,128]{2,1,0:T(8,128)(2,1)}), bf16[32,272,128]{2,1,0:T(8,128)(2,1)S(1)}, u32[]{:S(2)}, u32[]{:S(2)}) async-start(bf16[32,272,128]{2,1,0:T(8,128)(2,1)} %copy-done), calls=%async_computation | async-start | bytes 4456448 | tf_op jit(solution)/shard_map/all_to_all | solution.py:212
  17.4 3.8 %collective-permute-start.1 = (bf16[144,512]{1,0:T(8,128)(2,1)S(1)}, bf16[144,512]{1,0:T(8,128)(2,1)S(1)}, u32[]{:S(2)}, u32[]{:S(2)}) collective-permute-start(bf16[144,512]{1,0:T(8,128)(2,1)S(1)} %get-tuple-element.14), channel_id=1, source_target_pairs={{1,0},{2,1},{3,2},{4,3},{5,4},{6,5},{7,6},{8,7},{9,8},{10,9},{11,1... | collective-permute-start | bytes 442376 | tf_op jit(solution)/shard_map/ppermute | solution.py:198
  21.2 46.2 %collective-permute-done.1 = bf16[144,512]{1,0:T(8,128)(2,1)S(1)} collective-permute-done((bf16[144,512]{1,0:T(8,128)(2,1)S(1)}, bf16[144,512]{1,0:T(8,128)(2,1)S(1)}, u32[]{:S(2)}, u32[]{:S(2)}) %collective-permute-start.1) | collective-permute-done | bytes 147488 | tf_op jit(solution)/shard_map/ppermute | solution.py:198
  67.4 4.0 %collective-permute-done = bf16[144,512]{1,0:T(8,128)(2,1)S(1)} collective-permute-done((bf16[144,512]{1,0:T(8,128)(2,1)S(1)}, bf16[144,512]{1,0:T(8,128)(2,1)S(1)}, u32[]{:S(2)}, u32[]{:S(2)}) %collective-permute-start) | collective-permute-done | bytes 147488 | tf_op jit(solution)/shard_map/ppermute | solution.py:197
  71.4 0.1 pad_maximum_fusion.middle_ref
  71.4 4.3 %collective-permute-start.2 = (bf16[3,144,512]{2,1,0:T(8,128)(2,1)S(1)}, bf16[3,144,512]{2,1,0:T(8,128)(2,1)S(1)}, u32[]{:S(2)}, u32[]{:S(2)}) collective-permute-start(bf16[3,144,512]{2,1,0:T(8,128)(2,1)S(1)} %pad_maximum_fusion.middle_ref), channel_id=1, source_target_pairs={{0,32},{32,64},{64,96},{96,128},{128,160},{160,192},{192,224},{1,3... | collective-permute-start | bytes 1327112 | tf_op jit(solution)/shard_map/ppermute | solution.py:210
  75.7 1.9 %collective-permute-start.3 = (bf16[3,144,512]{2,1,0:T(8,128)(2,1)S(1)}, bf16[3,144,512]{2,1,0:T(8,128)(2,1)S(1)}, u32[]{:S(2)}, u32[]{:S(2)}) collective-permute-start(bf16[3,144,512]{2,1,0:T(8,128)(2,1)S(1)} %pad_maximum_fusion.middle_ref), channel_id=1, source_target_pairs={{32,0},{64,32},{96,64},{128,96},{160,128},{192,160},{224,192},{33,... | collective-permute-start | bytes 1327112 | tf_op jit(solution)/shard_map/ppermute | solution.py:211
  77.7 1.2 %copy-done.3 = bf16[1,1,512,1024]{3,2,1,0:T(8,128)(2,1)S(1)} copy-done((bf16[1,1,512,1024]{3,2,1,0:T(8,128)(2,1)S(1)}, bf16[1,1,512,1024]{3,2,1,0:T(8,128)(2,1)}, u32[]{:S(2)}) %copy-start.3) | copy-done | bytes 1048600
  78.9 0.4 shard_map.84
  79.3 2.3 %collective-permute-done.2.south_ref = bf16[3,144,512]{2,1,0:T(8,128)(2,1)S(1)} collective-permute-done((bf16[3,144,512]{2,1,0:T(8,128)(2,1)S(1)}, bf16[3,144,512]{2,1,0:T(8,128)(2,1)S(1)}, u32[]{:S(2)}, u32[]{:S(2)}) %collective-permute-start.2) | collective-permute-done | bytes 442400 | tf_op jit(solution)/shard_map/ppermute | solution.py:210
  81.6 7.9 %collective-permute-done.3.north_ref = bf16[3,144,512]{2,1,0:T(8,128)(2,1)S(1)} collective-permute-done((bf16[3,144,512]{2,1,0:T(8,128)(2,1)S(1)}, bf16[3,144,512]{2,1,0:T(8,128)(2,1)S(1)}, u32[]{:S(2)}, u32[]{:S(2)}) %collective-permute-start.3) | collective-permute-done | bytes 442400 | tf_op jit(solution)/shard_map/ppermute | solution.py:211
  89.5 1.2 %shard_map.83 = (f32[512,512]{1,0:T(8,128)S(1)}, f32[1,512]{1,0:T(1,128)S(1)}) custom-call(bf16[3,144,512]{2,1,0:T(8,128)(2,1)S(1)} %pad_maximum_fusion.middle_ref, bf16[3,144,512]{2,1,0:T(8,128)(2,1)S(1)} %collective-permute-done.2.south_ref, bf16[3,144,512]{2,1,0:T(8,128)(2,1)S(1)} %collective-permute-done.3.north_ref), custom_call_target="tpu_custom_call" | custom-call | tf_op jit(solution)/shard_map/pallas_call | solution.py:217
  90.7 0.0 copy-start.1
  90.7 1.0 copy-done.1
  91.7 1.2 %copy-done.2 = f32[512,512]{1,0:T(8,128)S(1)} copy-done((f32[512,512]{1,0:T(8,128)S(1)}, f32[512,512]{1,0:T(8,128)}, u32[]{:S(2)}) %copy-start.2) | copy-done | bytes 1048600
  92.9 6.1 %shard_map.85 = f32[512,1024]{1,0:T(8,128)} custom-call(bf16[32,272,128]{2,1,0:T(8,128)(2,1)S(1)} %all-to-all-done.slots_ref, f32[512,512]{1,0:T(8,128)S(1)} %copy-done.2, f32[1,512]{1,0:T(1,128)S(1)} %get-tuple-element.10.drive_ref, f32[1,1024]{1,0:T(1,128)S(1)} %get-tuple-element.11.mean_ref, bf16[512,1024]{1,0:T(8,128)(2,1)S(1)} %get-tuple-element.12.anomaly_ref), custom_call_target="tpu_custom_call" | custom-call | tf_op jit(solution)/shard_map/pallas_call | solution.py:223
  (16 shorter events, 0.1 us)
Async XLA Ops:
  0.8 1.0 %copy-start.4 = (bf16[1,16,32,512]{3,2,1,0:T(8,128)(2,1)S(1)}, bf16[1,16,32,512]{3,2,1,0:T(8,128)(2,1)}, u32[]{:S(2)}) copy-start(bf16[1,16,32,512]{3,2,1,0:T(8,128)(2,1)} %param.12) | copy-start | bytes 1572868
  1.9 0.7 copy-start.5
  2.6 0.7 copy-start.6
  6.0 1.4 %copy-start = (bf16[32,272,128]{2,1,0:T(8,128)(2,1)}, bf16[32,272,128]{2,1,0:T(8,128)(2,1)S(1)}, u32[]{:S(2)}) copy-start(bf16[32,272,128]{2,1,0:T(8,128)(2,1)S(1)} %shard_map.82) | copy-start | bytes 6684676
  7.4 9.9 %copy-start.9 = (s32[1,1,128]{2,1,0:T(1,128)S(1)}, s32[1,1,128]{2,1,0:T(1,128)}, u32[]{:S(2)}) copy-start(s32[1,1,128]{2,1,0:T(1,128)} %param.11) | copy-start | bytes 1540
  7.4 10.0 %copy-start.8 = (bf16[1,1,128]{2,1,0:T(2,128)(2,1)S(1)}, bf16[1,1,128]{2,1,0:T(2,128)(2,1)}, u32[]{:S(2)}) copy-start(bf16[1,1,128]{2,1,0:T(2,128)(2,1)} %param.10) | copy-start | bytes 772
  7.4 10.0 %copy-start.7 = (bf16[1,1,128,512]{3,2,1,0:T(8,128)(2,1)S(1)}, bf16[1,1,128,512]{3,2,1,0:T(8,128)(2,1)}, u32[]{:S(2)}) copy-start(bf16[1,1,128,512]{3,2,1,0:T(8,128)(2,1)} %param.9) | copy-start | bytes 393220
  7.4 84.3 %all-to-all-start = ((bf16[32,272,128]{2,1,0:T(8,128)(2,1)}), bf16[32,272,128]{2,1,0:T(8,128)(2,1)S(1)}, u32[]{:S(2)}, u32[]{:S(2)}) async-start(bf16[32,272,128]{2,1,0:T(8,128)(2,1)} %copy-done), calls=%async_computation | async-start | bytes 4456448 | tf_op jit(solution)/shard_map/all_to_all | solution.py:212
  17.4 50.0 %collective-permute-start.1 = (bf16[144,512]{1,0:T(8,128)(2,1)S(1)}, bf16[144,512]{1,0:T(8,128)(2,1)S(1)}, u32[]{:S(2)}, u32[]{:S(2)}) collective-permute-start(bf16[144,512]{1,0:T(8,128)(2,1)S(1)} %get-tuple-element.14), channel_id=1, source_target_pairs={{1,0},{2,1},{3,2},{4,3},{5,4},{6,5},{7,6},{8,7},{9,8},{10,9},{11,1... | collective-permute-start | bytes 442376 | tf_op jit(solution)/shard_map/ppermute | solution.py:198
  21.2 50.2 %collective-permute-start = (bf16[144,512]{1,0:T(8,128)(2,1)S(1)}, bf16[144,512]{1,0:T(8,128)(2,1)S(1)}, u32[]{:S(2)}, u32[]{:S(2)}) collective-permute-start(bf16[144,512]{1,0:T(8,128)(2,1)S(1)} %get-tuple-element.14), channel_id=1, source_target_pairs={{0,1},{1,2},{2,3},{3,4},{4,5},{5,6},{6,7},{7,8},{8,9},{9,10},{10,1... | collective-permute-start | bytes 442376 | tf_op jit(solution)/shard_map/ppermute | solution.py:197
  71.4 10.2 %collective-permute-start.2 = (bf16[3,144,512]{2,1,0:T(8,128)(2,1)S(1)}, bf16[3,144,512]{2,1,0:T(8,128)(2,1)S(1)}, u32[]{:S(2)}, u32[]{:S(2)}) collective-permute-start(bf16[3,144,512]{2,1,0:T(8,128)(2,1)S(1)} %pad_maximum_fusion.middle_ref), channel_id=1, source_target_pairs={{0,32},{32,64},{64,96},{96,128},{128,160},{160,192},{192,224},{1,3... | collective-permute-start | bytes 1327112 | tf_op jit(solution)/shard_map/ppermute | solution.py:210
  75.7 13.8 %collective-permute-start.3 = (bf16[3,144,512]{2,1,0:T(8,128)(2,1)S(1)}, bf16[3,144,512]{2,1,0:T(8,128)(2,1)S(1)}, u32[]{:S(2)}, u32[]{:S(2)}) collective-permute-start(bf16[3,144,512]{2,1,0:T(8,128)(2,1)S(1)} %pad_maximum_fusion.middle_ref), channel_id=1, source_target_pairs={{32,0},{64,32},{96,64},{128,96},{160,128},{192,160},{224,192},{33,... | collective-permute-start | bytes 1327112 | tf_op jit(solution)/shard_map/ppermute | solution.py:211
  77.7 1.2 %copy-start.3 = (bf16[1,1,512,1024]{3,2,1,0:T(8,128)(2,1)S(1)}, bf16[1,1,512,1024]{3,2,1,0:T(8,128)(2,1)}, u32[]{:S(2)}) copy-start(bf16[1,1,512,1024]{3,2,1,0:T(8,128)(2,1)} %param.8) | copy-start | bytes 3145732
  90.7 1.0 copy-start.1
  91.7 1.2 %copy-start.2 = (f32[512,512]{1,0:T(8,128)S(1)}, f32[512,512]{1,0:T(8,128)}, u32[]{:S(2)}) copy-start(f32[512,512]{1,0:T(8,128)} %copy-done.1) | copy-start | bytes 3145732

commit v3 on v2

--- a/solution.py
+++ b/solution.py
@@ -204,6 +204,7 @@
         [pltpu.SMEM((2 * blocks,), jnp.int32), pltpu.SMEM((blocks,), jnp.int32)],
     )(sat_pert[0], sat_misfit[0], sat_rows[0], sat_targets.reshape(-1))
 
+    low, high, slots = lax.optimization_barrier((low, high, slots))
     middle = jnp.stack([low, own, high])
     up = [(i, i + 1) for i in range(bands - 1)]
     down = [(target, source) for source, target in up]

time: 99.4 us -> 83.3 us (0.84)
  waiting for transfers between devices: 60.4 us -> 39.7 us
  other arithmetic: 0.09 us -> 2.3 us
  Pallas kernels: 10.4 us -> 11.8 us
  starting transfers between devices: 20 us -> 21.4 us
  local copies, waits for them, and re-layouts: 8 us -> 6.63 us
    ppermute x1, waiting for transfers between devices: 46.2 us -> 0.01 us  [shards(): high = lax.ppermute(own, 'lon', west)]
    all_to_all x1, waiting for transfers between devices: 0.01 us -> 23.2 us  [shards(): slots = lax.all_to_all(slots, 'lon', 0, 0, tiled=True)]
    ppermute x1, waiting for transfers between devices: 7.92 us -> 16.5 us  [shards(): north = lax.ppermute(middle, 'lat', down)]
    all_to_all x1, starting transfers between devices: 9.92 us -> 5.65 us  [shards(): slots = lax.all_to_all(slots, 'lon', 0, 0, tiled=True)]
    ppermute x1, waiting for transfers between devices: 3.95 us -> 0.01 us  [shards(): low = lax.ppermute(own, 'lon', east)]
    ppermute x1, starting transfers between devices: 4.3 us -> 6.8 us  [shards(): south = lax.ppermute(middle, 'lat', up)]
    ppermute x1, starting transfers between devices: 3.82 us -> 6.3 us  [shards(): high = lax.ppermute(own, 'lon', west)]
    ppermute x1, waiting for transfers between devices: 2.31 us -> 0.01 us  [shards(): south = lax.ppermute(middle, 'lat', up)]
  transfers between devices with their start and end apart: 5 -> 5, of which waited for: 4 -> 2; matrix products, arithmetic and copies ran while one was open for 0% -> 1% of each run, Pallas kernels for 2% -> 7%
where the time goes in v3:
time: 83.3 us; the launch traced here: 81.9 us
  waiting for transfers between devices  39.7 us (48%)
  starting transfers between devices  21.4 us (26%)
  Pallas kernels  11.8 us (14%)
  local copies, waits for them, and re-layouts  6.63 us (8%)
  other arithmetic  2.3 us (3%)
    all_to_all x1, waiting for transfers between devices, shards(): slots = lax.all_to_all(slots, 'lon', 0, 0, tiled=True)  23.2 us
    ppermute x1, waiting for transfers between devices, shards(): north = lax.ppermute(middle, 'lat', down)  16.5 us
    ppermute x1, starting transfers between devices, shards(): south = lax.ppermute(middle, 'lat', up)  6.8 us
    unnamed x13, local copies, waits for them, and re-layouts  6.54 us
    ppermute x1, starting transfers between devices, shards(): high = lax.ppermute(own, 'lon', west)  6.3 us
    pallas_call x1, Pallas kernels, shards(): call(final_body, shape((members, cells), F32), [VMEM] * 5, [pltpu.VMEM((b...  6.07 us
    all_to_all x1, starting transfers between devices, shards(): slots = lax.all_to_all(slots, 'lon', 0, 0, tiled=True)  5.65 us
    pallas_call x1, Pallas kernels, shards(): call(route_body, shape((blocks, members // LANES * 2 * obs + PAD, LANES),...  4.11 us
  transfers between devices with their start and end apart: 5, of which 2 were waited for; matrix products, arithmetic and copies ran while one was open for 1% of the time, Pallas kernels for 7%

profile of v3, /device:TPU:24, one launch (start us, length us, event | category | flops | bytes accessed | tf_op | source)
XLA Modules:
  0.0 81.9 jit_solution(570603123335358428)
XLA Ops:
  0.0 0.7 convert_bitcast_fusion
  0.7 0.7 fusion.5
  1.3 0.9 %fusion.6 = (bf16[1,144,512]{2,1,0:T(8,128)(2,1)S(1)}, bf16[144,512]{1,0:T(8,128)(2,1)S(1)}) fusion(bf16[16,512]{1,0:T(8,128)(2,1)S(1)} %fusion.5, bf16[128,512]{1,0:T(8,128)(2,1)} %bitcast.19), kind=kLoop, calls=%fused_computation.11 | loop fusion | flops 294912 | bytes 442368 | tf_op jit(solution)/shard_map/stack | solution.py:208
  2.2 6.3 %collective-permute-start.1 = (bf16[144,512]{1,0:T(8,128)(2,1)S(1)}, bf16[144,512]{1,0:T(8,128)(2,1)S(1)}, u32[]{:S(2)}, u32[]{:S(2)}) collective-permute-start(bf16[144,512]{1,0:T(8,128)(2,1)S(1)} %get-tuple-element.20), channel_id=1, source_target_pairs={{1,0},{2,1},{3,2},{4,3},{5,4},{6,5},{7,6},{8,7},{9,8},{10,9},{11,1... | collective-permute-start | bytes 442376 | tf_op jit(solution)/shard_map/ppermute | solution.py:198
  8.6 0.8 copy.10
  9.3 0.1 reshape.16.targets_ref
  9.4 1.0 %copy-done.3 = bf16[1,16,32,512]{3,2,1,0:T(8,128)(2,1)S(1)} copy-done((bf16[1,16,32,512]{3,2,1,0:T(8,128)(2,1)S(1)}, bf16[1,16,32,512]{3,2,1,0:T(8,128)(2,1)}, u32[]{:S(2)}) %copy-start.3) | copy-done | bytes 524312
  10.4 0.7 copy-done.4
  11.1 0.7 copy-done.5
  11.8 4.1 %shard_map.82 = bf16[32,272,128]{2,1,0:T(8,128)(2,1)} custom-call(bf16[16,32,512]{2,1,0:T(8,128)(2,1)S(1)} %bitcast.14, bf16[16,32]{1,0:T(8,128)(2,1)S(1)} %bitcast.15, s32[16]{0:T(128)S(1)} %bitcast.16, s32[32]{0:T(128)S(1)} %reshape.16.targets_ref), custom_call_target="tpu_custom_call" | custom-call | tf_op jit(solution)/shard_map/pallas_call | solution.py:200
  15.9 5.6 %all-to-all-start = ((bf16[32,272,128]{2,1,0:T(8,128)(2,1)}), bf16[32,272,128]{2,1,0:T(8,128)(2,1)S(1)}, u32[]{:S(2)}, u32[]{:S(2)}) async-start(bf16[32,272,128]{2,1,0:T(8,128)(2,1)} %shard_map.82), calls=%async_computation | async-start | bytes 4456448 | tf_op jit(solution)/shard_map/all_to_all | solution.py:213
  21.6 0.1 pad_maximum_fusion.middle_ref
  21.6 2.7 %collective-permute-start.3 = (bf16[3,144,512]{2,1,0:T(8,128)(2,1)S(1)}, bf16[3,144,512]{2,1,0:T(8,128)(2,1)S(1)}, u32[]{:S(2)}, u32[]{:S(2)}) collective-permute-start(bf16[3,144,512]{2,1,0:T(8,128)(2,1)S(1)} %pad_maximum_fusion.middle_ref), channel_id=1, source_target_pairs={{32,0},{64,32},{96,64},{128,96},{160,128},{192,160},{224,192},{33,... | collective-permute-start | bytes 1327112 | tf_op jit(solution)/shard_map/ppermute | solution.py:212
  24.3 6.8 %collective-permute-start.2 = (bf16[3,144,512]{2,1,0:T(8,128)(2,1)S(1)}, bf16[3,144,512]{2,1,0:T(8,128)(2,1)S(1)}, u32[]{:S(2)}, u32[]{:S(2)}) collective-permute-start(bf16[3,144,512]{2,1,0:T(8,128)(2,1)S(1)} %pad_maximum_fusion.middle_ref), channel_id=1, source_target_pairs={{0,32},{32,64},{64,96},{96,128},{128,160},{160,192},{192,224},{1,3... | collective-permute-start | bytes 1327112 | tf_op jit(solution)/shard_map/ppermute | solution.py:211
  31.1 0.0 copy-start.2
  31.1 1.2 %copy-done.2 = bf16[1,1,512,1024]{3,2,1,0:T(8,128)(2,1)S(1)} copy-done((bf16[1,1,512,1024]{3,2,1,0:T(8,128)(2,1)S(1)}, bf16[1,1,512,1024]{3,2,1,0:T(8,128)(2,1)}, u32[]{:S(2)}) %copy-start.2) | copy-done | bytes 1048600
  32.3 0.4 shard_map.84
  32.7 16.5 %collective-permute-done.3.north_ref = bf16[3,144,512]{2,1,0:T(8,128)(2,1)S(1)} collective-permute-done((bf16[3,144,512]{2,1,0:T(8,128)(2,1)S(1)}, bf16[3,144,512]{2,1,0:T(8,128)(2,1)S(1)}, u32[]{:S(2)}, u32[]{:S(2)}) %collective-permute-start.3) | collective-permute-done | bytes 442400 | tf_op jit(solution)/shard_map/ppermute | solution.py:212
  49.3 1.2 %shard_map.83 = (f32[512,512]{1,0:T(8,128)S(1)}, f32[1,512]{1,0:T(1,128)S(1)}) custom-call(bf16[3,144,512]{2,1,0:T(8,128)(2,1)S(1)} %pad_maximum_fusion.middle_ref, bf16[3,144,512]{2,1,0:T(8,128)(2,1)S(1)} %collective-permute-done.2.south_ref, bf16[3,144,512]{2,1,0:T(8,128)(2,1)S(1)} %collective-permute-done.3.north_ref), custom_call_target="tpu_custom_call" | custom-call | tf_op jit(solution)/shard_map/pallas_call | solution.py:218
  50.4 0.0 copy-start
  50.5 1.0 %copy-done = f32[512,512]{1,0:T(8,128)} copy-done((f32[512,512]{1,0:T(8,128)}, f32[512,512]{1,0:T(8,128)S(1)}, u32[]{:S(2)}) %copy-start) | copy-done | bytes 1048600
  51.4 23.2 %all-to-all-done.slots_ref = bf16[32,272,128]{2,1,0:T(8,128)(2,1)S(1)} async-done(((bf16[32,272,128]{2,1,0:T(8,128)(2,1)}), bf16[32,272,128]{2,1,0:T(8,128)(2,1)S(1)}, u32[]{:S(2)}, u32[]{:S(2)}) %all-to-all-start) | async-done | bytes 2228256 | tf_op jit(solution)/shard_map/all_to_all | solution.py:213
  74.6 1.2 %copy-done.1 = f32[512,512]{1,0:T(8,128)S(1)} copy-done((f32[512,512]{1,0:T(8,128)S(1)}, f32[512,512]{1,0:T(8,128)}, u32[]{:S(2)}) %copy-start.1) | copy-done | bytes 1048600
  75.8 6.1 %shard_map.85 = f32[512,1024]{1,0:T(8,128)} custom-call(bf16[32,272,128]{2,1,0:T(8,128)(2,1)S(1)} %all-to-all-done.slots_ref, f32[512,512]{1,0:T(8,128)S(1)} %copy-done.1, f32[1,512]{1,0:T(1,128)S(1)} %get-tuple-element.16.drive_ref, f32[1,1024]{1,0:T(1,128)S(1)} %get-tuple-element.17.mean_ref, bf16[512,1024]{1,0:T(8,128)(2,1)S(1)} %get-tuple-element.18.anomaly_ref), custom_call_target="tpu_custom_call" | custom-call | tf_op jit(solution)/shard_map/pallas_call | solution.py:224
  (8 shorter events, 0.0 us)
Async XLA Ops:
  2.2 13.7 %collective-permute-start.1 = (bf16[144,512]{1,0:T(8,128)(2,1)S(1)}, bf16[144,512]{1,0:T(8,128)(2,1)S(1)}, u32[]{:S(2)}, u32[]{:S(2)}) collective-permute-start(bf16[144,512]{1,0:T(8,128)(2,1)S(1)} %get-tuple-element.20), channel_id=1, source_target_pairs={{1,0},{2,1},{3,2},{4,3},{5,4},{6,5},{7,6},{8,7},{9,8},{10,9},{11,1... | collective-permute-start | bytes 442376 | tf_op jit(solution)/shard_map/ppermute | solution.py:198
  8.5 7.4 %collective-permute-start = (bf16[144,512]{1,0:T(8,128)(2,1)S(1)}, bf16[144,512]{1,0:T(8,128)(2,1)S(1)}, u32[]{:S(2)}, u32[]{:S(2)}) collective-permute-start(bf16[144,512]{1,0:T(8,128)(2,1)S(1)} %get-tuple-element.20), channel_id=1, source_target_pairs={{0,1},{1,2},{2,3},{3,4},{4,5},{5,6},{6,7},{7,8},{8,9},{9,10},{10,1... | collective-permute-start | bytes 442376 | tf_op jit(solution)/shard_map/ppermute | solution.py:197
  9.4 1.0 %copy-start.3 = (bf16[1,16,32,512]{3,2,1,0:T(8,128)(2,1)S(1)}, bf16[1,16,32,512]{3,2,1,0:T(8,128)(2,1)}, u32[]{:S(2)}) copy-start(bf16[1,16,32,512]{3,2,1,0:T(8,128)(2,1)} %param.12) | copy-start | bytes 1572868
  10.4 0.7 copy-start.4
  11.1 0.7 copy-start.5
  15.9 58.7 %all-to-all-start = ((bf16[32,272,128]{2,1,0:T(8,128)(2,1)}), bf16[32,272,128]{2,1,0:T(8,128)(2,1)S(1)}, u32[]{:S(2)}, u32[]{:S(2)}) async-start(bf16[32,272,128]{2,1,0:T(8,128)(2,1)} %shard_map.82), calls=%async_computation | async-start | bytes 4456448 | tf_op jit(solution)/shard_map/all_to_all | solution.py:213
  21.6 27.6 %collective-permute-start.3 = (bf16[3,144,512]{2,1,0:T(8,128)(2,1)S(1)}, bf16[3,144,512]{2,1,0:T(8,128)(2,1)S(1)}, u32[]{:S(2)}, u32[]{:S(2)}) collective-permute-start(bf16[3,144,512]{2,1,0:T(8,128)(2,1)S(1)} %pad_maximum_fusion.middle_ref), channel_id=1, source_target_pairs={{32,0},{64,32},{96,64},{128,96},{160,128},{192,160},{224,192},{33,... | collective-permute-start | bytes 1327112 | tf_op jit(solution)/shard_map/ppermute | solution.py:212
  24.3 25.0 %collective-permute-start.2 = (bf16[3,144,512]{2,1,0:T(8,128)(2,1)S(1)}, bf16[3,144,512]{2,1,0:T(8,128)(2,1)S(1)}, u32[]{:S(2)}, u32[]{:S(2)}) collective-permute-start(bf16[3,144,512]{2,1,0:T(8,128)(2,1)S(1)} %pad_maximum_fusion.middle_ref), channel_id=1, source_target_pairs={{0,32},{32,64},{64,96},{96,128},{128,160},{160,192},{192,224},{1,3... | collective-permute-start | bytes 1327112 | tf_op jit(solution)/shard_map/ppermute | solution.py:211
  31.1 1.2 %copy-start.2 = (bf16[1,1,512,1024]{3,2,1,0:T(8,128)(2,1)S(1)}, bf16[1,1,512,1024]{3,2,1,0:T(8,128)(2,1)}, u32[]{:S(2)}) copy-start(bf16[1,1,512,1024]{3,2,1,0:T(8,128)(2,1)} %param.8) | copy-start | bytes 3145732
  50.4 1.0 %copy-start = (f32[512,512]{1,0:T(8,128)}, f32[512,512]{1,0:T(8,128)S(1)}, u32[]{:S(2)}) copy-start(f32[512,512]{1,0:T(8,128)S(1)} %get-tuple-element.15.conv_ref) | copy-start | bytes 3145732
  74.6 1.2 %copy-start.1 = (f32[512,512]{1,0:T(8,128)S(1)}, f32[512,512]{1,0:T(8,128)}, u32[]{:S(2)}) copy-start(f32[512,512]{1,0:T(8,128)} %copy-done) | copy-start | bytes 3145732

commit v4 on v1

--- a/solution.py
+++ b/solution.py
@@ -12,6 +12,10 @@
 F32 = jnp.float32
 BF16 = jnp.bfloat16
 PAD = 16
+LANES = 128
+MATES = 3
+OFFSETS = (4, 3, -3, 2, -2, 1, -1, 0)
+CHUNKS = ((0, 1), (1, 3), (3, 8))
 VMEM = pltpu.VMEM
 SMEM = pltpu.SMEM
 LIMIT = 48 * 1024 * 1024
@@ -44,9 +48,34 @@
     anomaly_ref[...] = (values - mean).astype(BF16)
 
 
-def route_body(pert_ref, misfit_ref, rows_ref, targets_ref, slots_ref, drive_ref, entry_ref, count_ref):
+def route_body(
+    pert_hbm, misfit_hbm, rows_hbm, targets_hbm, conv_hbm, conv_misfit_hbm, conv_column_hbm, *refs
+):
+    outs, halo_ref = refs[: 1 + MATES * len(CHUNKS)], refs[1 + MATES * len(CHUNKS)]
+    (
+        pert_ref, misfit_ref, rows_ref, targets_ref, conv_misfit_ref, conv_column_ref,
+        entry_ref, count_ref, sems,
+    ) = refs[2 + MATES * len(CHUNKS) :]
     tiles, obs, members = pert_ref.shape
-    blocks = slots_ref.shape[0]
+    conv = conv_hbm.shape[0]
+    blocks = count_ref.shape[0]
+    planes, columns = blocks // (MATES + 1), MATES + 1
+    copies = [
+        pltpu.make_async_copy(source, place, sems.at[i])
+        for i, (source, place) in enumerate(
+            (
+                (targets_hbm, targets_ref),
+                (rows_hbm, rows_ref),
+                (pert_hbm, pert_ref),
+                (misfit_hbm, misfit_ref),
+                (conv_misfit_hbm, conv_misfit_ref),
+                (conv_column_hbm, conv_column_ref),
+                (conv_hbm, halo_ref.at[0:conv]),
+            )
+        )
+    ]
+    for copy in copies:
+        copy.start()
 
     def clear(block, _):
         count_ref[block] = 0
@@ -54,27 +83,43 @@
         entry_ref[2 * block + 1] = -1
         return 0
 
-    lax.fori_loop(0, blocks, clear, 0)
+    lax.fori_loop(0, blocks, clear, 0, unroll=True)
+    copies[0].wait()
+    copies[1].wait()
     for tile in range(tiles):
         for k in range(LOC):
-            block = targets_ref[LOC * tile + k]
+            block = targets_ref[k, tile]
             used = count_ref[block]
             entry_ref[2 * block + used] = LOC * tile + k
             count_ref[block] = used + 1
+    for copy in copies[2:]:
+        copy.wait()
     row = lax.broadcasted_iota(jnp.int32, (obs, members), 0)
-
-    def fill(slot, _):
-        entry = entry_ref[slot]
-        safe = jnp.maximum(entry, 0)
-        tile = safe // LOC
-        live = jnp.where(entry >= 0, rows_ref[tile], 0)
-        factor = jnp.where(safe % LOC == 0, 1.0, 0.5**0.5).astype(F32)
-        values = pert_ref[tile].astype(F32) * factor
-        start = pl.multiple_of((slot % 2) * obs, obs)
-        slots_ref[slot // 2, pl.ds(start, obs), :] = jnp.where(row < live, values, 0.0).astype(BF16)
-        return 0
-
-    lax.fori_loop(0, 2 * blocks, fill, 0)
+    me = lax.axis_index("lon")
+    plane, column = me // columns, me % columns
+    places = []
+    for mate in range(columns):
+        for at, offset in enumerate(OFFSETS):
+            if mate == 0:
+                ref, index = outs[0], at
+            else:
+                chunk = [at in range(low, high) for low, high in CHUNKS].index(True)
+                ref, index = outs[1 + (mate - 1) * len(CHUNKS) + chunk], at - CHUNKS[chunk][0]
+            there = (plane + offset + planes) % planes
+            places.append((ref, index, there * columns + (column ^ mate)))
+    for ref, index, block in places:
+        for slot in range(2):
+            entry = entry_ref[2 * block + slot]
+            safe = jnp.maximum(entry, 0)
+            tile = safe // LOC
+            live = jnp.where(entry >= 0, rows_ref[0, tile], 0)
+            factor = jnp.where(safe % LOC == 0, 1.0, 0.5**0.5).astype(F32)
+            values = pert_ref[tile].astype(F32) * factor
+            values = jnp.where(row < live, values, 0.0).astype(BF16)
+            for part in range(members // LANES):
+                start = part * 2 * obs + slot * obs
+                ref[index, start : start + obs, :] = values[:, part * LANES : (part + 1) * LANES]
+
     total = tiles * obs
     lane = lax.broadcasted_iota(jnp.int32, (1, total), 1)
     own_tile = lane // obs
@@ -82,9 +127,9 @@
     named = [jnp.zeros((1, total), jnp.int32) for _ in range(LOC)]
     for tile in range(tiles):
         here = own_tile == tile
-        live = jnp.where(here, rows_ref[tile], live)
+        live = jnp.where(here, rows_ref[0, tile], live)
         for k in range(LOC):
-            named[k] = jnp.where(here, targets_ref[LOC * tile + k], named[k])
+            named[k] = jnp.where(here, targets_ref[k, tile], named[k])
     repeat = (
         lax.broadcasted_iota(jnp.int32, (obs, total), 1) % obs
         == lax.broadcasted_iota(jnp.int32, (obs, total), 0)
@@ -95,11 +140,110 @@
     )
     misfit = jnp.sum(jnp.where(pick, spread, 0.0), axis=0, keepdims=True)
     misfit = jnp.where(lane % obs < live, misfit, 0.0)
-    block = lax.broadcasted_iota(jnp.int32, (blocks, total), 0)
+    position = lax.broadcasted_iota(jnp.int32, (blocks, 1), 0)
+    block = jnp.zeros((blocks, 1), jnp.int32)
+    for at, (_, _, there) in enumerate(places):
+        block = jnp.where(position == at, there, block)
     weight = jnp.zeros((blocks, total), F32)
     for k in range(LOC):
         weight = weight + jnp.where(block == named[k], 0.5**k, 0.0)
-    drive_ref[...] = dot((weight * misfit).astype(BF16), pert_ref[...].reshape(total, members))
+    drive = dot((weight * misfit).astype(BF16), pert_ref[...].reshape(total, members))
+    upper = drive.astype(BF16).astype(F32)
+    empty = jnp.zeros((PAD - 2 * (members // LANES), LANES), F32)
+    for at, (ref, index, _) in enumerate(places):
+        parts = [
+            piece[at : at + 1, part * LANES : (part + 1) * LANES]
+            for piece in (upper, drive - upper)
+            for part in range(members // LANES)
+        ]
+        ref[index, members // LANES * 2 * obs :, :] = jnp.concatenate(parts + [empty]).astype(BF16)
+    first = lax.broadcasted_iota(jnp.int32, (PAD, conv), 0) == 0
+    halo_ref[conv:, :] = jnp.zeros((PAD, members), BF16)
+    halo_ref[conv:, 0:conv] = jnp.where(first, conv_misfit_ref[...].astype(F32), 0.0).astype(BF16)
+    halo_ref[conv:, conv : 2 * conv] = jnp.where(
+        first, conv_column_ref[...].astype(F32), 0.0
+    ).astype(BF16)
+
+
+def gather_rows(own_ref, at, mates, index, rows_ref):
+    sources = [(own_ref, at)] + [(ref, index) for ref in mates]
+    pieces = rows_ref.shape[1] // LANES
+    count = (own_ref.shape[1] - PAD) // pieces
+    drive = jnp.zeros((PAD, LANES), F32)
+    for number, (ref, place) in enumerate(sources):
+        for part in range(pieces):
+            rows_ref[number * count : (number + 1) * count, part * LANES : (part + 1) * LANES] = ref[
+                place, part * count : (part + 1) * count, :
+            ]
+        drive = drive + ref[place, pieces * count :, :].astype(F32)
+    return drive
+
+
+def triangle(size=LANES):
+    across = lax.broadcasted_iota(jnp.int32, (size, size), 1)
+    down = lax.broadcasted_iota(jnp.int32, (size, size), 0)
+    return down, across
+
+
+def packed(rows_ref, drive):
+    down, across = triangle()
+    pieces = rows_ref.shape[1] // LANES
+    bands = []
+    for part in range(pieces):
+        left = rows_ref[:, part * LANES : (part + 1) * LANES]
+        bands.append(transposed_dot(left, rows_ref[:, part * LANES :]))
+    blocks, diagonals = [], []
+    for part in range(0, pieces, 2):
+        lower = bands[part + 1][:, 0:LANES]
+        blocks.append(jnp.where(down <= across, bands[part][:, 0:LANES], lower))
+        diagonals.append(jnp.sum(jnp.where(down == across, lower, 0.0), axis=0, keepdims=True))
+    for part in range(pieces):
+        for other in range(1, pieces - part):
+            blocks.append(bands[part][:, other * LANES : (other + 1) * LANES])
+    total = drive[0:pieces] + drive[pieces : 2 * pieces]
+    empty = jnp.zeros((PAD - 2 * pieces - len(diagonals), LANES), F32)
+    return blocks, total, jnp.concatenate(diagonals), empty
+
+
+def split_drive(total, diagonals, empty):
+    upper = total.astype(BF16).astype(F32)
+    return jnp.concatenate([upper, total - upper, diagonals, empty]).astype(BF16)
+
+
+def extra_of(extra, pieces):
+    extra = extra.astype(F32)
+    return extra[0:pieces] + extra[pieces : 2 * pieces], extra[2 * pieces : 2 * pieces + pieces // 2]
+
+
+def open_body(own_ref, mate1_ref, mate2_ref, mate3_ref, up_ref, down_ref, rows_ref):
+    drive = gather_rows(own_ref, 0, (mate1_ref, mate2_ref, mate3_ref), 0, rows_ref)
+    blocks, total, diagonals, empty = packed(rows_ref, drive)
+    half = len(blocks) // 2
+    for number, block in enumerate(blocks):
+        ref, place = (up_ref, number) if number < half else (down_ref, number - half)
+        ref[place * LANES : (place + 1) * LANES, :] = block.astype(BF16)
+    down_ref[half * LANES :, :] = split_drive(total, diagonals, empty)
+
+
+def step_body(at, index, own_ref, mate1_ref, mate2_ref, mate3_ref, up_in, down_in, up_ref, down_ref, rows_ref):
+    mates = (mate1_ref, mate2_ref, mate3_ref)
+    pieces = rows_ref.shape[1] // LANES
+    for which, (came, out) in enumerate(((up_in, up_ref), (down_in, down_ref))):
+        drive = gather_rows(own_ref, at + which, mates, index + which, rows_ref)
+        blocks, total, diagonals, empty = packed(rows_ref, drive)
+        skip = 0
+        whole = came.shape == out.shape
+        if not whole and which == 1:
+            skip = len(blocks) - came.shape[0] // LANES
+        for number, block in enumerate(blocks):
+            place = (number - skip) * LANES
+            if 0 <= place and place + LANES <= came.shape[0]:
+                block = block + came[place : place + LANES, :].astype(F32)
+            out[number * LANES : (number + 1) * LANES, :] = block.astype(BF16)
+        if whole or which == 1:
+            more, more_diagonals = extra_of(came[came.shape[0] - PAD :, :], pieces)
+            total, diagonals = total + more, diagonals + more_diagonals
+        out[len(blocks) * LANES :, :] = split_drive(total, diagonals, empty)
 
 
 def conv_body(middle_ref, south_ref, north_ref, gram_ref, drive_ref, scaled_ref, spread_ref):
@@ -155,10 +299,46 @@
     out_ref[...] = mean_ref[...] + dot(transform, anomaly_ref[...])
 
 
-def final_body(rows_ref, conv_ref, drive1_ref, drive2_ref, mean_ref, anomaly_ref, out_ref):
+def final_body(
+    at, index, own_ref, mate1_ref, mate2_ref, mate3_ref, up_ref, down_ref,
+    conv_ref, drive_ref, mean_ref, anomaly_ref, out_ref, rows_ref, gram_ref,
+):
+    pieces = rows_ref.shape[1] // LANES
+    drive = gather_rows(own_ref, at, (mate1_ref, mate2_ref, mate3_ref), index, rows_ref)
     rows = rows_ref[...]
-    gram = conv_ref[...] + transposed_dot(rows, rows)
-    root_and_apply(gram, drive1_ref[...] + drive2_ref[...], mean_ref, anomaly_ref, out_ref)
+    gram_ref[...] = conv_ref[...] + transposed_dot(rows, rows)
+    total = drive[0:pieces] + drive[pieces : 2 * pieces]
+    diagonals = jnp.zeros((pieces // 2, LANES), F32)
+    for ref in (up_ref, down_ref):
+        more, more_diagonals = extra_of(ref[ref.shape[0] - PAD :, :], pieces)
+        total, diagonals = total + more, diagonals + more_diagonals
+    down, across = triangle()
+
+    def add(part, other, block):
+        place = (slice(part * LANES, (part + 1) * LANES), slice(other * LANES, (other + 1) * LANES))
+        gram_ref[place] = gram_ref[place] + block
+
+    number = 0
+
+    def block_of(number):
+        place = slice(number * LANES, (number + 1) * LANES)
+        return up_ref[place, :].astype(F32) + down_ref[place, :].astype(F32)
+
+    for part in range(0, pieces, 2):
+        block = block_of(number)
+        turned = block.T
+        add(part, part, jnp.where(down <= across, block, turned))
+        middle = jnp.where(down == across, diagonals[number : number + 1], turned)
+        add(part + 1, part + 1, jnp.where(down > across, block, middle))
+        number += 1
+    for part in range(pieces):
+        for other in range(part + 1, pieces):
+            block = block_of(number)
+            add(part, other, block)
+            add(other, part, block.T)
+            number += 1
+    total = jnp.concatenate([total[part : part + 1] for part in range(pieces)], axis=1)
+    root_and_apply(gram_ref[...], drive_ref[...] + total, mean_ref, anomaly_ref, out_ref)
 
 
 def shards(
@@ -170,28 +350,73 @@
     blocks, bands = lax.axis_size("lon"), lax.axis_size("lat")
     shape = jax.ShapeDtypeStruct
 
-    extra = jnp.concatenate([conv_misfit[0], conv_column[0].astype(BF16)], axis=1)
-    extra = jnp.pad(extra, ((0, PAD - 1), (0, members - 2 * conv)))
-    own = jnp.concatenate([conv_pert[0, 0], extra], axis=0)
+    pieces = members // LANES
+    packet = pieces * 2 * obs + PAD
+    triangles = pieces * pieces // 2
+    full = triangles * LANES + PAD
+    half = triangles // 2 * LANES
+    columns = MATES + 1
+
+    def ring(values, step):
+        return lax.ppermute(values, "lon", [(i, (i + step * columns) % blocks) for i in range(blocks)])
+
+    def trade(values, mate):
+        return lax.ppermute(values, "lon", [(i, i ^ mate) for i in range(blocks)])
+
+    outs = [shape((len(OFFSETS), packet, LANES), BF16)]
+    for mate in range(MATES):
+        outs += [shape((high - low, packet, LANES), BF16) for low, high in CHUNKS]
+    outs.append(shape((conv + PAD, members), BF16))
+    own, *sends, halo = call(
+        route_body,
+        tuple(outs),
+        [pl.ANY] * 7,
+        [
+            pltpu.VMEM((tiles, obs, members), BF16),
+            pltpu.VMEM((tiles, obs), BF16),
+            pltpu.SMEM((1, tiles), jnp.int32),
+            pltpu.SMEM((LOC, tiles), jnp.int32),
+            pltpu.VMEM((1, conv), BF16),
+            pltpu.VMEM((1, conv), jnp.int32),
+            pltpu.SMEM((2 * blocks,), jnp.int32),
+            pltpu.SMEM((blocks,), jnp.int32),
+            pltpu.SemaphoreType.DMA((7,)),
+        ],
+    )(
+        sat_pert[0], sat_misfit[0], sat_rows, jnp.swapaxes(sat_targets[0], 0, 1),
+        conv_pert[0, 0], conv_misfit[0], conv_column[0],
+    )
+    chunked = [[sends[mate * len(CHUNKS) + c] for mate in range(MATES)] for c in range(len(CHUNKS))]
+    got = []
+    for c, chunk in enumerate(chunked):
+        if c:
+            tied = lax.optimization_barrier(tuple(got[-1]) + tuple(chunk))
+            got[-1], chunk = tied[:MATES], tied[MATES:]
+        got.append([trade(values, mate + 1) for mate, values in enumerate(chunk)])
+
     east = [(i, (i + 1) % blocks) for i in range(blocks)]
     west = [(target, source) for source, target in east]
-    low = lax.ppermute(own, "lon", east)
-    high = lax.ppermute(own, "lon", west)
-
-    slots, drive = call(
-        route_body,
-        (shape((blocks, 2 * obs, members), BF16), shape((blocks, members), F32)),
-        [VMEM, VMEM, SMEM, SMEM],
-        [pltpu.SMEM((2 * blocks,), jnp.int32), pltpu.SMEM((blocks,), jnp.int32)],
-    )(sat_pert[0], sat_misfit[0], sat_rows[0], sat_targets.reshape(-1))
-
-    middle = jnp.stack([low, own, high])
-    up = [(i, i + 1) for i in range(bands - 1)]
-    down = [(target, source) for source, target in up]
-    south = lax.ppermute(middle, "lat", up)
-    north = lax.ppermute(middle, "lat", down)
-    drive_sat = lax.psum_scatter(drive, "lon", scatter_dimension=0, tiled=True)
-    rows = lax.all_to_all(slots, "lon", 0, 0, tiled=True).reshape(blocks * 2 * obs, members)
+    low = lax.ppermute(halo, "lon", east)
+    high = lax.ppermute(halo, "lon", west)
+    middle = jnp.stack([low, halo, high])
+    north = [(i, i + 1) for i in range(bands - 1)]
+    south = [(target, source) for source, target in north]
+    below = lax.ppermute(middle, "lat", north)
+    above = lax.ppermute(middle, "lat", south)
+
+    scratch = [pltpu.VMEM((2 * obs * columns, members), BF16)]
+    up, down = call(
+        open_body, (shape((half, LANES), BF16), shape((full - half, LANES), BF16)), [VMEM] * 4, scratch
+    )(own, *got[0])
+    for step, (at, c) in enumerate(((1, 1), (3, 2), (5, 2))):
+        up, down = ring(up, 1), ring(down, -1)
+        up, down = call(
+            functools.partial(step_body, at, at - CHUNKS[c][0]),
+            (shape((full, LANES), BF16), shape((full, LANES), BF16)),
+            [VMEM] * 6,
+            scratch,
+        )(own, *got[c], up, down)
+    up, down = ring(up, 1), ring(down, -1)
 
     anomaly, mean = call(
         background_body, (shape((members, cells), BF16), shape((1, cells), F32)), [VMEM]
@@ -201,10 +426,13 @@
         (shape((members, members), F32), shape((1, members), F32)),
         [VMEM] * 3,
         [pltpu.VMEM((9 * conv, members), BF16), pltpu.VMEM((9 * conv, members), BF16)],
-    )(middle, south, north)
-    result = call(final_body, shape((members, cells), F32), [VMEM] * 6)(
-        rows, gram_conv, drive_conv, drive_sat, mean, anomaly
-    )
+    )(middle, below, above)
+    result = call(
+        functools.partial(final_body, 7, 7 - CHUNKS[2][0]),
+        shape((members, cells), F32),
+        [VMEM] * 10,
+        scratch + [pltpu.VMEM((members, members), F32)],
+    )(own, *got[2], up, down, gram_conv, drive_conv, mean, anomaly)
     return result[None, None]
 
 

time: 294 us -> 84.6 us (0.29)
  the two profiles are of different devices: /device:TPU:24 before, /device:TPU:6 now
where the time goes in v4:
time: 84.6 us; the launch traced here: 84.4 us
  waiting for transfers between devices  39 us (46%)
  starting transfers between devices  29.9 us (35%)
  Pallas kernels  10 us (12%)
  local copies, waits for them, and re-layouts  5.28 us (6%)
    ppermute x9, waiting for transfers between devices, trade(): return lax.ppermute(values, 'lon', [(i, i ^ mate) for i in range(blocks)])  16.9 us
    ppermute x8, starting transfers between devices, ring(): lax.ppermute(values, 'lon', [(i, (i + step * columns) % blocks) for i in...  16 us
    ppermute x8, waiting for transfers between devices, ring(): lax.ppermute(values, 'lon', [(i, (i + step * columns) % blocks) for i in...  10.6 us
    ppermute x1, waiting for transfers between devices, shards(): below = lax.ppermute(middle, 'lat', north)  7.73 us
    ppermute x1, starting transfers between devices, shards(): above = lax.ppermute(middle, 'lat', south)  5.76 us
    ppermute x9, starting transfers between devices, trade(): return lax.ppermute(values, 'lon', [(i, i ^ mate) for i in range(blocks)])  5.68 us
    unnamed x16, local copies, waits for them, and re-layouts  5.28 us
    pallas_call x1, Pallas kernels, shards(): call(functools.partial(final_body, 7, 7 - CHUNKS[2][0]), shape((members,...  5.11 us
  transfers between devices with their start and end apart: 21, of which 9 were waited for; matrix products, arithmetic and copies ran while one was open for 0% of the time, Pallas kernels for 3%

profile of v4, /device:TPU:6, one launch (start us, length us, event | category | flops | bytes accessed | tf_op | source)
XLA Modules:
  0.0 84.4 jit_solution(16376203750845853017)
XLA Ops:
  0.0 1.0 %copy-done.1 = bf16[1,16,32,512]{3,2,1,0:T(8,128)(2,1)S(1)} copy-done((bf16[1,16,32,512]{3,2,1,0:T(8,128)(2,1)S(1)}, bf16[1,16,32,512]{3,2,1,0:T(8,128)(2,1)}, u32[]{:S(2)}) %copy-start.1) | copy-done | bytes 524312
  1.0 0.9 %copy-done.2 = bf16[1,1,128,512]{3,2,1,0:T(8,128)(2,1)S(1)} copy-done((bf16[1,1,128,512]{3,2,1,0:T(8,128)(2,1)S(1)}, bf16[1,1,128,512]{3,2,1,0:T(8,128)(2,1)}, u32[]{:S(2)}) %copy-start.2) | copy-done | bytes 131096
  5.3 1.6 %shard_map.82 = (bf16[8,272,128]{2,1,0:T(8,128)(2,1)S(1)}, bf16[1,272,128]{2,1,0:T(8,128)(2,1)S(1)}, bf16[2,272,128]{2,1,0:T(8,128)(2,1)S(1)}, bf16[5,272,128]{2...) custom-call(bf16[16,32,512]{2,1,0:T(8,128)(2,1)S(1)} %bitcast.14, ...), custom_call_target="tpu_custom_call" | custom-call | tf_op jit(solution)/shard_map/pallas_call | solution.py:370
  7.0 0.9 %collective-permute-start.1 = (bf16[1,272,128]{2,1,0:T(8,128)(2,1)S(1)}, bf16[1,272,128]{2,1,0:T(8,128)(2,1)S(1)}, u32[]{:S(2)}, u32[]{:S(2)}) collective-permute-start(bf16[1,272,128]{2,1,0:T(8,128)(2,1)S(1)} %get-tuple-element.42), channel_id=1, source_target_pairs={{0,2},{1,3},{2,0},{3,1},{4,6},{5,7},{6,4},{7,5},{8,10},{9,11},{10,... | collective-permute-start | bytes 208904 | tf_op jit(solution)/shard_map/ppermute | solution.py:364
  7.9 1.0 %collective-permute-start.2 = (bf16[1,272,128]{2,1,0:T(8,128)(2,1)S(1)}, bf16[1,272,128]{2,1,0:T(8,128)(2,1)S(1)}, u32[]{:S(2)}, u32[]{:S(2)}) collective-permute-start(bf16[1,272,128]{2,1,0:T(8,128)(2,1)S(1)} %get-tuple-element.43), channel_id=1, source_target_pairs={{0,3},{1,2},{2,1},{3,0},{4,7},{5,6},{6,5},{7,4},{8,11},{9,10},{10,... | collective-permute-start | bytes 208904 | tf_op jit(solution)/shard_map/ppermute | solution.py:364
  8.8 3.2 %collective-permute-done.1.mate2_ref = bf16[1,272,128]{2,1,0:T(8,128)(2,1)S(1)} collective-permute-done((bf16[1,272,128]{2,1,0:T(8,128)(2,1)S(1)}, bf16[1,272,128]{2,1,0:T(8,128)(2,1)S(1)}, u32[]{:S(2)}, u32[]{:S(2)}) %collective-permute-start.1) | collective-permute-done | bytes 69664 | tf_op jit(solution)/shard_map/ppermute | solution.py:364
  12.9 0.8 collective-permute-start.4
  13.7 0.7 collective-permute-start.5
  14.8 5.9 %collective-permute-start.10 = (bf16[528,128]{1,0:T(8,128)(2,1)S(1)}, bf16[528,128]{1,0:T(8,128)(2,1)S(1)}, u32[]{:S(2)}, u32[]{:S(2)}) collective-permute-start(bf16[528,128]{1,0:T(8,128)(2,1)S(1)} %get-tuple-element.63), channel_id=1, source_target_pairs={{0,28},{1,29},{2,30},{3,31},{4,0},{5,1},{6,2},{7,3},{8,4},{9,5},{1... | collective-permute-start | bytes 405512 | tf_op jit(solution)/shard_map/ppermute | solution.py:361
  20.9 6.7 %collective-permute-done.9.up_in = bf16[512,128]{1,0:T(8,128)(2,1)S(1)} collective-permute-done((bf16[512,128]{1,0:T(8,128)(2,1)S(1)}, bf16[512,128]{1,0:T(8,128)(2,1)S(1)}, u32[]{:S(2)}, u32[]{:S(2)}) %collective-permute-start.9) | collective-permute-done | bytes 131104 | tf_op jit(solution)/shard_map/ppermute | solution.py:361
  28.2 3.2 %collective-permute-start.12 = (bf16[1040,128]{1,0:T(8,128)(2,1)S(1)}, bf16[1040,128]{1,0:T(8,128)(2,1)S(1)}, u32[]{:S(2)}, u32[]{:S(2)}) collective-permute-start(bf16[1040,128]{1,0:T(8,128)(2,1)S(1)} %get-tuple-element.65), channel_id=1, source_target_pairs={{0,28},{1,29},{2,30},{3,31},{4,0},{5,1},{6,2},{7,3},{8,4},{9,5},{1... | collective-permute-start | bytes 798728 | tf_op jit(solution)/shard_map/ppermute | solution.py:361
  31.4 0.8 collective-permute-start.7
  32.2 1.0 %collective-permute-start.8 = (bf16[5,272,128]{2,1,0:T(8,128)(2,1)S(1)}, bf16[5,272,128]{2,1,0:T(8,128)(2,1)S(1)}, u32[]{:S(2)}, u32[]{:S(2)}) collective-permute-start(bf16[5,272,128]{2,1,0:T(8,128)(2,1)S(1)} %get-tuple-element.55), channel_id=1, source_target_pairs={{0,3},{1,2},{2,1},{3,0},{4,7},{5,6},{6,5},{7,4},{8,11},{9,10},{10,... | collective-permute-start | bytes 1044488 | tf_op jit(solution)/shard_map/ppermute | solution.py:364
  33.3 3.9 %collective-permute-done.11.up_in = bf16[1040,128]{1,0:T(8,128)(2,1)S(1)} collective-permute-done((bf16[1040,128]{1,0:T(8,128)(2,1)S(1)}, bf16[1040,128]{1,0:T(8,128)(2,1)S(1)}, u32[]{:S(2)}, u32[]{:S(2)}) %collective-permute-start.11) | collective-permute-done | bytes 266272 | tf_op jit(solution)/shard_map/ppermute | solution.py:361
  37.7 6.2 %collective-permute-done.7.mate2_ref = bf16[5,272,128]{2,1,0:T(8,128)(2,1)S(1)} collective-permute-done((bf16[5,272,128]{2,1,0:T(8,128)(2,1)S(1)}, bf16[5,272,128]{2,1,0:T(8,128)(2,1)S(1)}, u32[]{:S(2)}, u32[]{:S(2)}) %collective-permute-start.7) | collective-permute-done | bytes 348192 | tf_op jit(solution)/shard_map/ppermute | solution.py:364
  43.9 6.7 %collective-permute-done.8.mate3_ref = bf16[5,272,128]{2,1,0:T(8,128)(2,1)S(1)} collective-permute-done((bf16[5,272,128]{2,1,0:T(8,128)(2,1)S(1)}, bf16[5,272,128]{2,1,0:T(8,128)(2,1)S(1)}, u32[]{:S(2)}, u32[]{:S(2)}) %collective-permute-start.8) | collective-permute-done | bytes 348192 | tf_op jit(solution)/shard_map/ppermute | solution.py:364
  51.4 3.2 %collective-permute-start.14 = (bf16[1040,128]{1,0:T(8,128)(2,1)S(1)}, bf16[1040,128]{1,0:T(8,128)(2,1)S(1)}, u32[]{:S(2)}, u32[]{:S(2)}) collective-permute-start(bf16[1040,128]{1,0:T(8,128)(2,1)S(1)} %get-tuple-element.67), channel_id=1, source_target_pairs={{0,28},{1,29},{2,30},{3,31},{4,0},{5,1},{6,2},{7,3},{8,4},{9,5},{1... | collective-permute-start | bytes 798728 | tf_op jit(solution)/shard_map/ppermute | solution.py:361
  54.7 5.8 %collective-permute-start.20 = (bf16[3,144,512]{2,1,0:T(8,128)(2,1)S(1)}, bf16[3,144,512]{2,1,0:T(8,128)(2,1)S(1)}, u32[]{:S(2)}, u32[]{:S(2)}) collective-permute-start(bf16[3,144,512]{2,1,0:T(8,128)(2,1)S(1)} %pad_maximum_fusion.middle_ref), channel_id=1, source_target_pairs={{32,0},{64,32},{96,64},{128,96},{160,128},{192,160},{224,192},{33,... | collective-permute-start | bytes 1327112 | tf_op jit(solution)/shard_map/ppermute | solution.py:405
  60.4 1.9 %collective-permute-start.19 = (bf16[3,144,512]{2,1,0:T(8,128)(2,1)S(1)}, bf16[3,144,512]{2,1,0:T(8,128)(2,1)S(1)}, u32[]{:S(2)}, u32[]{:S(2)}) collective-permute-start(bf16[3,144,512]{2,1,0:T(8,128)(2,1)S(1)} %pad_maximum_fusion.middle_ref), channel_id=1, source_target_pairs={{0,32},{32,64},{64,96},{96,128},{128,160},{160,192},{192,224},{1,3... | collective-permute-start | bytes 1327112 | tf_op jit(solution)/shard_map/ppermute | solution.py:404
  62.9 3.2 %collective-permute-start.16 = (bf16[1040,128]{1,0:T(8,128)(2,1)S(1)}, bf16[1040,128]{1,0:T(8,128)(2,1)S(1)}, u32[]{:S(2)}, u32[]{:S(2)}) collective-permute-start(bf16[1040,128]{1,0:T(8,128)(2,1)S(1)} %get-tuple-element.69), channel_id=1, source_target_pairs={{0,28},{1,29},{2,30},{3,31},{4,0},{5,1},{6,2},{7,3},{8,4},{9,5},{1... | collective-permute-start | bytes 798728 | tf_op jit(solution)/shard_map/ppermute | solution.py:361
  66.6 3.7 %collective-permute-done.20.north_ref = bf16[3,144,512]{2,1,0:T(8,128)(2,1)S(1)} collective-permute-done((bf16[3,144,512]{2,1,0:T(8,128)(2,1)S(1)}, bf16[3,144,512]{2,1,0:T(8,128)(2,1)S(1)}, u32[]{:S(2)}, u32[]{:S(2)}) %collective-permute-start.20) | collective-permute-done | bytes 442400 | tf_op jit(solution)/shard_map/ppermute | solution.py:405
  70.3 7.7 %collective-permute-done.19.south_ref = bf16[3,144,512]{2,1,0:T(8,128)(2,1)S(1)} collective-permute-done((bf16[3,144,512]{2,1,0:T(8,128)(2,1)S(1)}, bf16[3,144,512]{2,1,0:T(8,128)(2,1)S(1)}, u32[]{:S(2)}, u32[]{:S(2)}) %collective-permute-start.19) | collective-permute-done | bytes 442400 | tf_op jit(solution)/shard_map/ppermute | solution.py:404
  78.1 1.2 %shard_map.87 = (f32[512,512]{1,0:T(8,128)S(1)}, f32[1,512]{1,0:T(1,128)S(1)}) custom-call(bf16[3,144,512]{2,1,0:T(8,128)(2,1)S(1)} %pad_maximum_fusion.middle_ref, bf16[3,144,512]{2,1,0:T(8,128)(2,1)S(1)} %collective-permute-done.19.south_ref, bf16[3,144,512]{2,1,0:T(8,128)(2,1)S(1)} %collective-permute-done.20.north_ref), custom_call_target="tpu_custom_call" | custom-call | tf_op jit(solution)/shard_map/pallas_call | solution.py:424
  79.2 5.1 %shard_map.89 = f32[512,1024]{1,0:T(8,128)} custom-call(bf16[8,272,128]{2,1,0:T(8,128)(2,1)S(1)} %get-tuple-element.40.own_ref, bf16[5,272,128]{2,1,0:T(8,128)(2,1)S(1)} %collective-permute-done.6.mate1_ref, bf16[5,272,128]{2,1,0:T(8,128)(2,1)S(1)} %collective-permute-done.7.mate2_ref, bf16[5,272,128]{2,1,0:T(8,128)(2,1)S(1)} %collective-permute-done.8.mate3_ref, ...), custom_call_target="tpu_custom_call" | custom-call | tf_op jit(solution)/shard_map/pallas_call | solution.py:430
  (43 shorter events, 7.7 us)
Async XLA Ops:
  0.0 1.0 %copy-start.1 = (bf16[1,16,32,512]{3,2,1,0:T(8,128)(2,1)S(1)}, bf16[1,16,32,512]{3,2,1,0:T(8,128)(2,1)}, u32[]{:S(2)}) copy-start(bf16[1,16,32,512]{3,2,1,0:T(8,128)(2,1)} %param.12) | copy-start | bytes 1572868
  1.0 0.9 %copy-start.2 = (bf16[1,1,128,512]{3,2,1,0:T(8,128)(2,1)S(1)}, bf16[1,1,128,512]{3,2,1,0:T(8,128)(2,1)}, u32[]{:S(2)}) copy-start(bf16[1,1,128,512]{3,2,1,0:T(8,128)(2,1)} %param.9) | copy-start | bytes 393220
  6.9 2.0 %collective-permute-start = (bf16[1,272,128]{2,1,0:T(8,128)(2,1)S(1)}, bf16[1,272,128]{2,1,0:T(8,128)(2,1)S(1)}, u32[]{:S(2)}, u32[]{:S(2)}) collective-permute-start(bf16[1,272,128]{2,1,0:T(8,128)(2,1)S(1)} %get-tuple-element.41), channel_id=1, source_target_pairs={{0,1},{1,0},{2,3},{3,2},{4,5},{5,4},{6,7},{7,6},{8,9},{9,8},{10,11... | collective-permute-start | bytes 208904 | tf_op jit(solution)/shard_map/ppermute | solution.py:364
  7.0 5.1 %collective-permute-start.1 = (bf16[1,272,128]{2,1,0:T(8,128)(2,1)S(1)}, bf16[1,272,128]{2,1,0:T(8,128)(2,1)S(1)}, u32[]{:S(2)}, u32[]{:S(2)}) collective-permute-start(bf16[1,272,128]{2,1,0:T(8,128)(2,1)S(1)} %get-tuple-element.42), channel_id=1, source_target_pairs={{0,2},{1,3},{2,0},{3,1},{4,6},{5,7},{6,4},{7,5},{8,10},{9,11},{10,... | collective-permute-start | bytes 208904 | tf_op jit(solution)/shard_map/ppermute | solution.py:364
  7.9 4.7 %collective-permute-start.2 = (bf16[1,272,128]{2,1,0:T(8,128)(2,1)S(1)}, bf16[1,272,128]{2,1,0:T(8,128)(2,1)S(1)}, u32[]{:S(2)}, u32[]{:S(2)}) collective-permute-start(bf16[1,272,128]{2,1,0:T(8,128)(2,1)S(1)} %get-tuple-element.43), channel_id=1, source_target_pairs={{0,3},{1,2},{2,1},{3,0},{4,7},{5,6},{6,5},{7,4},{8,11},{9,10},{10,... | collective-permute-start | bytes 208904 | tf_op jit(solution)/shard_map/ppermute | solution.py:364
  12.6 8.1 %collective-permute-start.3 = (bf16[2,272,128]{2,1,0:T(8,128)(2,1)S(1)}, bf16[2,272,128]{2,1,0:T(8,128)(2,1)S(1)}, u32[]{:S(2)}, u32[]{:S(2)}) collective-permute-start(bf16[2,272,128]{2,1,0:T(8,128)(2,1)S(1)} %get-tuple-element.47), channel_id=1, source_target_pairs={{0,1},{1,0},{2,3},{3,2},{4,5},{5,4},{6,7},{7,6},{8,9},{9,8},{10,11... | collective-permute-start | bytes 417800 | tf_op jit(solution)/shard_map/ppermute | solution.py:364
  12.9 7.8 %collective-permute-start.4 = (bf16[2,272,128]{2,1,0:T(8,128)(2,1)S(1)}, bf16[2,272,128]{2,1,0:T(8,128)(2,1)S(1)}, u32[]{:S(2)}, u32[]{:S(2)}) collective-permute-start(bf16[2,272,128]{2,1,0:T(8,128)(2,1)S(1)} %get-tuple-element.48), channel_id=1, source_target_pairs={{0,2},{1,3},{2,0},{3,1},{4,6},{5,7},{6,4},{7,5},{8,10},{9,11},{10,... | collective-permute-start | bytes 417800 | tf_op jit(solution)/shard_map/ppermute | solution.py:364
  13.7 7.2 %collective-permute-start.5 = (bf16[2,272,128]{2,1,0:T(8,128)(2,1)S(1)}, bf16[2,272,128]{2,1,0:T(8,128)(2,1)S(1)}, u32[]{:S(2)}, u32[]{:S(2)}) collective-permute-start(bf16[2,272,128]{2,1,0:T(8,128)(2,1)S(1)} %get-tuple-element.49), channel_id=1, source_target_pairs={{0,3},{1,2},{2,1},{3,0},{4,7},{5,6},{6,5},{7,4},{8,11},{9,10},{10,... | collective-permute-start | bytes 417800 | tf_op jit(solution)/shard_map/ppermute | solution.py:364
  14.8 12.8 %collective-permute-start.10 = (bf16[528,128]{1,0:T(8,128)(2,1)S(1)}, bf16[528,128]{1,0:T(8,128)(2,1)S(1)}, u32[]{:S(2)}, u32[]{:S(2)}) collective-permute-start(bf16[528,128]{1,0:T(8,128)(2,1)S(1)} %get-tuple-element.63), channel_id=1, source_target_pairs={{0,28},{1,29},{2,30},{3,31},{4,0},{5,1},{6,2},{7,3},{8,4},{9,5},{1... | collective-permute-start | bytes 405512 | tf_op jit(solution)/shard_map/ppermute | solution.py:361
  20.7 6.9 %collective-permute-start.9 = (bf16[512,128]{1,0:T(8,128)(2,1)S(1)}, bf16[512,128]{1,0:T(8,128)(2,1)S(1)}, u32[]{:S(2)}, u32[]{:S(2)}) collective-permute-start(bf16[512,128]{1,0:T(8,128)(2,1)S(1)} %get-tuple-element.62), channel_id=1, source_target_pairs={{0,4},{1,5},{2,6},{3,7},{4,8},{5,9},{6,10},{7,11},{8,12},{9,13},{1... | collective-permute-start | bytes 393224 | tf_op jit(solution)/shard_map/ppermute | solution.py:361
  28.1 9.1 %collective-permute-start.11 = (bf16[1040,128]{1,0:T(8,128)(2,1)S(1)}, bf16[1040,128]{1,0:T(8,128)(2,1)S(1)}, u32[]{:S(2)}, u32[]{:S(2)}) collective-permute-start(bf16[1040,128]{1,0:T(8,128)(2,1)S(1)} %get-tuple-element.64), channel_id=1, source_target_pairs={{0,4},{1,5},{2,6},{3,7},{4,8},{5,9},{6,10},{7,11},{8,12},{9,13},{1... | collective-permute-start | bytes 798728 | tf_op jit(solution)/shard_map/ppermute | solution.py:361
  28.2 9.0 %collective-permute-start.12 = (bf16[1040,128]{1,0:T(8,128)(2,1)S(1)}, bf16[1040,128]{1,0:T(8,128)(2,1)S(1)}, u32[]{:S(2)}, u32[]{:S(2)}) collective-permute-start(bf16[1040,128]{1,0:T(8,128)(2,1)S(1)} %get-tuple-element.65), channel_id=1, source_target_pairs={{0,28},{1,29},{2,30},{3,31},{4,0},{5,1},{6,2},{7,3},{8,4},{9,5},{1... | collective-permute-start | bytes 798728 | tf_op jit(solution)/shard_map/ppermute | solution.py:361
  31.4 6.3 %collective-permute-start.6 = (bf16[5,272,128]{2,1,0:T(8,128)(2,1)S(1)}, bf16[5,272,128]{2,1,0:T(8,128)(2,1)S(1)}, u32[]{:S(2)}, u32[]{:S(2)}) collective-permute-start(bf16[5,272,128]{2,1,0:T(8,128)(2,1)S(1)} %get-tuple-element.53), channel_id=1, source_target_pairs={{0,1},{1,0},{2,3},{3,2},{4,5},{5,4},{6,7},{7,6},{8,9},{9,8},{10,11... | collective-permute-start | bytes 1044488 | tf_op jit(solution)/shard_map/ppermute | solution.py:364
  31.4 12.5 %collective-permute-start.7 = (bf16[5,272,128]{2,1,0:T(8,128)(2,1)S(1)}, bf16[5,272,128]{2,1,0:T(8,128)(2,1)S(1)}, u32[]{:S(2)}, u32[]{:S(2)}) collective-permute-start(bf16[5,272,128]{2,1,0:T(8,128)(2,1)S(1)} %get-tuple-element.54), channel_id=1, source_target_pairs={{0,2},{1,3},{2,0},{3,1},{4,6},{5,7},{6,4},{7,5},{8,10},{9,11},{10,... | collective-permute-start | bytes 1044488 | tf_op jit(solution)/shard_map/ppermute | solution.py:364
  32.2 18.4 %collective-permute-start.8 = (bf16[5,272,128]{2,1,0:T(8,128)(2,1)S(1)}, bf16[5,272,128]{2,1,0:T(8,128)(2,1)S(1)}, u32[]{:S(2)}, u32[]{:S(2)}) collective-permute-start(bf16[5,272,128]{2,1,0:T(8,128)(2,1)S(1)} %get-tuple-element.55), channel_id=1, source_target_pairs={{0,3},{1,2},{2,1},{3,0},{4,7},{5,6},{6,5},{7,4},{8,11},{9,10},{10,... | collective-permute-start | bytes 1044488 | tf_op jit(solution)/shard_map/ppermute | solution.py:364
  37.2 29.0 %copy-start = (bf16[1,1,512,1024]{3,2,1,0:T(8,128)(2,1)S(1)}, bf16[1,1,512,1024]{3,2,1,0:T(8,128)(2,1)}, u32[]{:S(2)}) copy-start(bf16[1,1,512,1024]{3,2,1,0:T(8,128)(2,1)} %param.8) | copy-start | bytes 3145732
  37.2 17.4 %collective-permute-start.18 = (bf16[144,512]{1,0:T(8,128)(2,1)S(1)}, bf16[144,512]{1,0:T(8,128)(2,1)S(1)}, u32[]{:S(2)}, u32[]{:S(2)}) collective-permute-start(bf16[144,512]{1,0:T(8,128)(2,1)S(1)} %get-tuple-element.70), channel_id=1, source_target_pairs={{1,0},{2,1},{3,2},{4,3},{5,4},{6,5},{7,6},{8,7},{9,8},{10,9},{11,1... | collective-permute-start | bytes 442376 | tf_op jit(solution)/shard_map/ppermute | solution.py:400
  37.2 17.4 %collective-permute-start.17 = (bf16[144,512]{1,0:T(8,128)(2,1)S(1)}, bf16[144,512]{1,0:T(8,128)(2,1)S(1)}, u32[]{:S(2)}, u32[]{:S(2)}) collective-permute-start(bf16[144,512]{1,0:T(8,128)(2,1)S(1)} %get-tuple-element.70), channel_id=1, source_target_pairs={{0,1},{1,2},{2,3},{3,4},{4,5},{5,6},{6,7},{7,8},{8,9},{9,10},{10,1... | collective-permute-start | bytes 442376 | tf_op jit(solution)/shard_map/ppermute | solution.py:399
  51.1 11.3 %collective-permute-start.13 = (bf16[1040,128]{1,0:T(8,128)(2,1)S(1)}, bf16[1040,128]{1,0:T(8,128)(2,1)S(1)}, u32[]{:S(2)}, u32[]{:S(2)}) collective-permute-start(bf16[1040,128]{1,0:T(8,128)(2,1)S(1)} %get-tuple-element.66), channel_id=1, source_target_pairs={{0,4},{1,5},{2,6},{3,7},{4,8},{5,9},{6,10},{7,11},{8,12},{9,13},{1... | collective-permute-start | bytes 798728 | tf_op jit(solution)/shard_map/ppermute | solution.py:361
  51.4 11.0 %collective-permute-start.14 = (bf16[1040,128]{1,0:T(8,128)(2,1)S(1)}, bf16[1040,128]{1,0:T(8,128)(2,1)S(1)}, u32[]{:S(2)}, u32[]{:S(2)}) collective-permute-start(bf16[1040,128]{1,0:T(8,128)(2,1)S(1)} %get-tuple-element.67), channel_id=1, source_target_pairs={{0,28},{1,29},{2,30},{3,31},{4,0},{5,1},{6,2},{7,3},{8,4},{9,5},{1... | collective-permute-start | bytes 798728 | tf_op jit(solution)/shard_map/ppermute | solution.py:361
  54.7 15.7 %collective-permute-start.20 = (bf16[3,144,512]{2,1,0:T(8,128)(2,1)S(1)}, bf16[3,144,512]{2,1,0:T(8,128)(2,1)S(1)}, u32[]{:S(2)}, u32[]{:S(2)}) collective-permute-start(bf16[3,144,512]{2,1,0:T(8,128)(2,1)S(1)} %pad_maximum_fusion.middle_ref), channel_id=1, source_target_pairs={{32,0},{64,32},{96,64},{128,96},{160,128},{192,160},{224,192},{33,... | collective-permute-start | bytes 1327112 | tf_op jit(solution)/shard_map/ppermute | solution.py:405
  60.4 17.6 %collective-permute-start.19 = (bf16[3,144,512]{2,1,0:T(8,128)(2,1)S(1)}, bf16[3,144,512]{2,1,0:T(8,128)(2,1)S(1)}, u32[]{:S(2)}, u32[]{:S(2)}) collective-permute-start(bf16[3,144,512]{2,1,0:T(8,128)(2,1)S(1)} %pad_maximum_fusion.middle_ref), channel_id=1, source_target_pairs={{0,32},{32,64},{64,96},{96,128},{128,160},{160,192},{192,224},{1,3... | collective-permute-start | bytes 1327112 | tf_op jit(solution)/shard_map/ppermute | solution.py:404
  62.9 16.4 %collective-permute-start.15 = (bf16[1040,128]{1,0:T(8,128)(2,1)S(1)}, bf16[1040,128]{1,0:T(8,128)(2,1)S(1)}, u32[]{:S(2)}, u32[]{:S(2)}) collective-permute-start(bf16[1040,128]{1,0:T(8,128)(2,1)S(1)} %get-tuple-element.68), channel_id=1, source_target_pairs={{0,4},{1,5},{2,6},{3,7},{4,8},{5,9},{6,10},{7,11},{8,12},{9,13},{1... | collective-permute-start | bytes 798728 | tf_op jit(solution)/shard_map/ppermute | solution.py:361
  62.9 16.3 %collective-permute-start.16 = (bf16[1040,128]{1,0:T(8,128)(2,1)S(1)}, bf16[1040,128]{1,0:T(8,128)(2,1)S(1)}, u32[]{:S(2)}, u32[]{:S(2)}) collective-permute-start(bf16[1040,128]{1,0:T(8,128)(2,1)S(1)} %get-tuple-element.69), channel_id=1, source_target_pairs={{0,28},{1,29},{2,30},{3,31},{4,0},{5,1},{6,2},{7,3},{8,4},{9,5},{1... | collective-permute-start | bytes 798728 | tf_op jit(solution)/shard_map/ppermute | solution.py:361
  (5 other events, 3.3 us)

commit v5 on v4

v5 whole, which is shorter than its diff:
```python
import functools

import jax
import jax.numpy as jnp
from jax import lax
from jax.experimental import pallas as pl
from jax.experimental.pallas import tpu as pltpu
from jax.sharding import PartitionSpec as P

BLK = 16
LOC = 2
F32 = jnp.float32
BF16 = jnp.bfloat16
PAD = 16
LANES = 128
COLUMNS = 4
OFFSETS = (4, 3, -3, 2, -2, 1, -1, 0)
CHUNKS = ((0, 1), (1, 8))
VMEM = pltpu.VMEM
SMEM = pltpu.SMEM
LIMIT = 48 * 1024 * 1024


def call(body, outs, in_spaces, scratch=(), limit=LIMIT, flops=0, moved=0):
    return pl.pallas_call(
        body,
        out_shape=outs,
        in_specs=[pl.BlockSpec(memory_space=space) for space in in_spaces],
        out_specs=jax.tree.map(lambda _: pl.BlockSpec(memory_space=VMEM), outs),
        scratch_shapes=list(scratch),
        compiler_params=pltpu.CompilerParams(vmem_limit_bytes=limit),
        cost_estimate=pl.CostEstimate(flops=flops, bytes_accessed=moved, transcendentals=0),
    )


def transposed_dot(left, right):
    return lax.dot_general(left, right, (((0,), (0,)), ((), ())), preferred_element_type=F32)


def dot(left, right):
    return jnp.dot(left, right, preferred_element_type=F32)


def background_body(ensemble_ref, anomaly_ref, mean_ref):
    values = ensemble_ref[...].astype(F32)
    mean = jnp.mean(values, axis=0, keepdims=True)
    mean_ref[...] = mean
    anomaly_ref[...] = (values - mean).astype(BF16)


def halo_body(conv_hbm, misfit_hbm, column_hbm, halo_ref, misfit_ref, column_ref, sems):
    conv, members = conv_hbm.shape
    copies = [
        pltpu.make_async_copy(misfit_hbm, misfit_ref, sems.at[0]),
        pltpu.make_async_copy(column_hbm, column_ref, sems.at[1]),
        pltpu.make_async_copy(conv_hbm, halo_ref.at[0:conv], sems.at[2]),
    ]
    for copy in copies:
        copy.start()
    first = lax.broadcasted_iota(jnp.int32, (PAD, conv), 0) == 0
    halo_ref[conv:, :] = jnp.zeros((PAD, members), BF16)
    copies[0].wait()
    copies[1].wait()
    halo_ref[conv:, 0:conv] = jnp.where(first, misfit_ref[...].astype(F32), 0.0).astype(BF16)
    halo_ref[conv:, conv : 2 * conv] = jnp.where(first, column_ref[...].astype(F32), 0.0).astype(BF16)
    copies[2].wait()


def route_body(
    pert0_hbm, pert1_hbm, misfit0_hbm, misfit1_hbm, lists0_hbm, lists1_hbm, own_ref, *refs
):
    sends = refs[: len(CHUNKS)]
    pert_ref, misfit_ref, lists_ref, entry_ref, count_ref, sems = refs[len(CHUNKS) :]
    tiles, obs, members = pert0_hbm.shape
    blocks = count_ref.shape[0]
    copies = []
    for source, (pert, misfit, lists) in enumerate(
        ((pert0_hbm, misfit0_hbm, lists0_hbm), (pert1_hbm, misfit1_hbm, lists1_hbm))
    ):
        span = pl.ds(source * tiles, tiles)
        copies.append(pltpu.make_async_copy(lists, lists_ref.at[source], sems.at[3 * source]))
        copies.append(pltpu.make_async_copy(misfit, misfit_ref.at[span], sems.at[3 * source + 1]))
        copies.append(pltpu.make_async_copy(pert, pert_ref.at[span], sems.at[3 * source + 2]))
    for copy in copies:
        copy.start()

    def clear(block, _):
        count_ref[block] = 0
        for slot in range(4):
            entry_ref[4 * block + slot] = -1
        return 0

    lax.fori_loop(0, blocks, clear, 0, unroll=True)
    copies[0].wait()
    copies[3].wait()
    for source in range(2):
        for tile in range(tiles):
            for k in range(LOC):
                block = lists_ref[source, k, tile]
                used = count_ref[block]
                entry_ref[4 * block + used] = LOC * (tiles * source + tile) + k
                count_ref[block] = used + 1
    for at in (1, 2, 4, 5):
        copies[at].wait()
    row = lax.broadcasted_iota(jnp.int32, (obs, members), 0)
    me = lax.axis_index("lon")
    planes = blocks // COLUMNS
    plane, column = me // COLUMNS, me % COLUMNS
    places = []
    for mate in range(2):
        for at, offset in enumerate(OFFSETS):
            ref, index = own_ref, at
            if mate:
                chunk = [at in range(low, high) for low, high in CHUNKS].index(True)
                ref, index = sends[chunk], at - CHUNKS[chunk][0]
            there = (plane + offset + planes) % planes
            places.append((ref, index, there * COLUMNS + (column ^ mate)))
    pieces = members // LANES
    for ref, index, block in places:
        for slot in range(4):
            entry = entry_ref[4 * block + slot]
            safe = jnp.maximum(entry, 0)
            tile = safe // LOC
            source = jnp.where(tile >= tiles, 1, 0)
            live = jnp.where(entry >= 0, lists_ref[source, LOC, tile - tiles * source], 0)
            factor = jnp.where(safe % LOC == 0, 1.0, 0.5**0.5).astype(F32)
            values = pert_ref[tile].astype(F32) * factor
            values = jnp.where(row < live, values, 0.0).astype(BF16)
            for part in range(pieces):
                start = (part * 4 + slot) * obs
                ref[index, start : start + obs, :] = values[:, part * LANES : (part + 1) * LANES]

    total = 2 * tiles * obs
    lane = lax.broadcasted_iota(jnp.int32, (1, total), 1)
    own_tile = lane // obs
    live = jnp.zeros((1, total), jnp.int32)
    named = [jnp.zeros((1, total), jnp.int32) for _ in range(LOC)]
    for source in range(2):
        for tile in range(tiles):
            here = own_tile == source * tiles + tile
            live = jnp.where(here, lists_ref[source, LOC, tile], live)
            for k in range(LOC):
                named[k] = jnp.where(here, lists_ref[source, k, tile], named[k])
    repeat = (
        lax.broadcasted_iota(jnp.int32, (obs, total), 1) % obs
        == lax.broadcasted_iota(jnp.int32, (obs, total), 0)
    )
    spread = dot(misfit_ref[...], jnp.where(repeat, 1.0, 0.0).astype(BF16))
    pick = lax.broadcasted_iota(jnp.int32, (2 * tiles, total), 1) // obs == lax.broadcasted_iota(
        jnp.int32, (2 * tiles, total), 0
    )
    misfit = jnp.sum(jnp.where(pick, spread, 0.0), axis=0, keepdims=True)
    misfit = jnp.where(lane % obs < live, misfit, 0.0)
    position = lax.broadcasted_iota(jnp.int32, (len(places), 1), 0)
    block = jnp.zeros((len(places), 1), jnp.int32)
    for at, (_, _, there) in enumerate(places):
        block = jnp.where(position == at, there, block)
    weight = jnp.zeros((len(places), total), F32)
    for k in range(LOC):
        weight = weight + jnp.where(block == named[k], 0.5**k, 0.0)
    drive = dot((weight * misfit).astype(BF16), pert_ref[...].reshape(total, members))
    upper = drive.astype(BF16).astype(F32)
    empty = jnp.zeros((PAD - 2 * pieces, LANES), F32)
    for at, (ref, index, _) in enumerate(places):
        parts = [
            piece[at : at + 1, part * LANES : (part + 1) * LANES]
            for piece in (upper, drive - upper)
            for part in range(pieces)
        ]
        ref[index, 4 * obs * pieces :, :] = jnp.concatenate(parts + [empty]).astype(BF16)


def gather_rows(own_ref, at, mate_ref, index, rows_ref):
    sources = [(own_ref, at), (mate_ref, index)]
    pieces = rows_ref.shape[1] // LANES
    count = (own_ref.shape[1] - PAD) // pieces
    drive = jnp.zeros((PAD, LANES), F32)
    for number, (ref, place) in enumerate(sources):
        for part in range(pieces):
            rows_ref[number * count : (number + 1) * count, part * LANES : (part + 1) * LANES] = ref[
                place, part * count : (part + 1) * count, :
            ]
        drive = drive + ref[place, pieces * count :, :].astype(F32)
    return drive


def triangle(size=LANES):
    across = lax.broadcasted_iota(jnp.int32, (size, size), 1)
    down = lax.broadcasted_iota(jnp.int32, (size, size), 0)
    return down, across


def packed(rows_ref, drive, right_ref=None):
    down, across = triangle()
    right_ref = rows_ref if right_ref is None else right_ref
    pieces = rows_ref.shape[1] // LANES
    bands = []
    for part in range(pieces):
        left = rows_ref[:, part * LANES : (part + 1) * LANES]
        bands.append(transposed_dot(left, right_ref[:, part * LANES :]))
    blocks, diagonals = [], []
    for part in range(0, pieces, 2):
        lower = bands[part + 1][:, 0:LANES]
        blocks.append(jnp.where(down <= across, bands[part][:, 0:LANES], lower))
        diagonals.append(jnp.sum(jnp.where(down == across, lower, 0.0), axis=0, keepdims=True))
    for part in range(pieces):
        for other in range(1, pieces - part):
            blocks.append(bands[part][:, other * LANES : (other + 1) * LANES])
    total = drive[0:pieces] + drive[pieces : 2 * pieces]
    empty = jnp.zeros((PAD - 2 * pieces - len(diagonals), LANES), F32)
    return blocks, total, jnp.concatenate(diagonals), empty


def split_drive(total, diagonals, empty):
    upper = total.astype(BF16).astype(F32)
    return jnp.concatenate([upper, total - upper, diagonals, empty]).astype(BF16)


def extra_of(extra, pieces):
    extra = extra.astype(F32)
    return extra[0:pieces] + extra[pieces : 2 * pieces], extra[2 * pieces : 2 * pieces + pieces // 2]


def open_body(own_ref, mate_ref, up_ref, down_ref, rows_ref):
    drive = gather_rows(own_ref, 0, mate_ref, 0, rows_ref)
    blocks, total, diagonals, empty = packed(rows_ref, drive)
    half = len(blocks) // 2
    for number, block in enumerate(blocks):
        ref, place = (up_ref, number) if number < half else (down_ref, number - half)
        ref[place * LANES : (place + 1) * LANES, :] = block.astype(BF16)
    down_ref[half * LANES :, :] = split_drive(total, diagonals, empty)


def step_body(at, index, own_ref, mate_ref, up_in, down_in, up_ref, down_ref, rows_ref):
    pieces = rows_ref.shape[1] // LANES
    for which, (came, out) in enumerate(((up_in, up_ref), (down_in, down_ref))):
        drive = gather_rows(own_ref, at + which, mate_ref, index + which, rows_ref)
        blocks, total, diagonals, empty = packed(rows_ref, drive)
        skip = 0
        whole = came.shape == out.shape
        if not whole and which == 1:
            skip = len(blocks) - came.shape[0] // LANES
        for number, block in enumerate(blocks):
            place = (number - skip) * LANES
            if 0 <= place and place + LANES <= came.shape[0]:
                block = block + came[place : place + LANES, :].astype(F32)
            out[number * LANES : (number + 1) * LANES, :] = block.astype(BF16)
        if whole or which == 1:
            more, more_diagonals = extra_of(came[came.shape[0] - PAD :, :], pieces)
            total, diagonals = total + more, diagonals + more_diagonals
        out[len(blocks) * LANES :, :] = split_drive(total, diagonals, empty)


def conv_body(
    low_ref, halo_ref, high_ref, gram_ref, drive_ref, north_ref, south_ref, scaled_ref, spread_ref
):
    conv, members = halo_ref.shape[0] - PAD, halo_ref.shape[1]
    pieces = members // LANES
    eye = lax.broadcasted_iota(jnp.int32, (conv, conv), 0) == lax.broadcasted_iota(
        jnp.int32, (conv, conv), 1
    )
    refs = ((-1, low_ref), (0, halo_ref), (1, high_ref))
    for b, ref in refs:
        spread_ref[(b + 1) * conv : (b + 2) * conv, :] = ref[0:conv, :]
    for a, out_ref in ((-1, north_ref), (1, south_ref), (0, gram_ref)):
        drive = jnp.zeros((8, members), F32)
        for b, ref in refs:
            misfit = ref[conv : conv + 1, 0:conv]
            column = ref[conv : conv + 1, conv : 2 * conv].astype(F32)
            lat_cell = jnp.floor(column * (1.0 / BLK))
            lon_cell = column - BLK * lat_cell
            lat_place = BLK * a + lat_cell + 0.5 - 0.5 * BLK
            lon_place = BLK * b + lon_cell + 0.5 - 0.5 * BLK
            weight = jnp.exp(-(lat_place * lat_place + lon_place * lon_place) / (2.0 * BLK * BLK))
            weight = jnp.sum(jnp.where(eye, weight, 0.0), axis=1, keepdims=True)
            scaled = (weight * ref[0:conv, :].astype(F32)).astype(BF16)
            scaled_ref[(b + 1) * conv : (b + 2) * conv, :] = scaled
            drive = drive + dot(jnp.broadcast_to(misfit, (8, conv)), scaled)
        if a == 0:
            drive_ref[...] = drive[0:1]
            gram_ref[...] = transposed_dot(scaled_ref[...], spread_ref[...])
            continue
        total = jnp.concatenate(
            [drive[0:1, part * LANES : (part + 1) * LANES] for part in range(pieces)]
            + [jnp.zeros((PAD - pieces, LANES), F32)]
        )
        blocks, total, diagonals, empty = packed(scaled_ref, total, spread_ref)
        for number, block in enumerate(blocks):
            out_ref[number * LANES : (number + 1) * LANES, :] = block.astype(BF16)
        out_ref[len(blocks) * LANES :, :] = split_drive(total, diagonals, empty)


def root_and_apply(gram, drive, mean_ref, anomaly_ref, out_ref):
    members = gram.shape[0]
    eye = lax.broadcasted_iota(jnp.int32, gram.shape, 0) == lax.broadcasted_iota(
        jnp.int32, gram.shape, 1
    )
    system = gram + jnp.where(eye, members - 1.0, 0.0)
    square = jnp.sum(jnp.sum(system * system, axis=0, keepdims=True), axis=1, keepdims=True)
    inverse_scale = lax.rsqrt(square)
    power1 = system * inverse_scale
    half1 = power1.astype(BF16)
    power2 = dot(half1, half1)
    half2 = power2.astype(BF16)
    power3 = dot(half1, half2)
    power4 = dot(half2, half2)
    product = 2.25 * power1 - 1.5 * power2 + 0.25 * power3
    excess = -0.75 * (power1 + product) + 0.25 * (2.25 * power2 - 1.5 * power3 + 0.25 * power4)
    half_excess = excess.astype(BF16)
    lifted = 4.5 * excess + dot(half_excess, half_excess)
    product = 5.0625 * power1 + dot(half1, lifted.astype(BF16))
    inverse_root = 1.5 * excess - 1.125 * product - 0.5 * dot(product.astype(BF16), half_excess)
    inverse_root = inverse_root + jnp.where(eye, 3.375, 0.0)
    first = jnp.sum(inverse_root * drive, axis=1, keepdims=True)
    weight = jnp.sum(inverse_root * first, axis=0, keepdims=True) * inverse_scale
    transform = (jnp.sqrt((members - 1.0) * inverse_scale) * inverse_root + weight).astype(BF16)
    out_ref[...] = mean_ref[...] + dot(transform, anomaly_ref[...])


def final_body(
    at, index, own_ref, mate_ref, up_ref, down_ref, below_ref, above_ref,
    conv_ref, drive_ref, mean_ref, anomaly_ref, out_ref, rows_ref, gram_ref,
):
    pieces = rows_ref.shape[1] // LANES
    drive = gather_rows(own_ref, at, mate_ref, index, rows_ref)
    rows = rows_ref[...]
    gram_ref[...] = conv_ref[...] + transposed_dot(rows, rows)
    total = drive[0:pieces] + drive[pieces : 2 * pieces]
    diagonals = jnp.zeros((pieces // 2, LANES), F32)
    arrived = (up_ref, down_ref, below_ref, above_ref)
    for ref in arrived:
        more, more_diagonals = extra_of(ref[ref.shape[0] - PAD :, :], pieces)
        total, diagonals = total + more, diagonals + more_diagonals
    down, across = triangle()

    def add(part, other, block):
        place = (slice(part * LANES, (part + 1) * LANES), slice(other * LANES, (other + 1) * LANES))
        gram_ref[place] = gram_ref[place] + block

    number = 0

    def block_of(number):
        place = slice(number * LANES, (number + 1) * LANES)
        return sum(ref[place, :].astype(F32) for ref in arrived)

    for part in range(0, pieces, 2):
        block = block_of(number)
        turned = block.T
        add(part, part, jnp.where(down <= across, block, turned))
        middle = jnp.where(down == across, diagonals[number : number + 1], turned)
        add(part + 1, part + 1, jnp.where(down > across, block, middle))
        number += 1
    for part in range(pieces):
        for other in range(part + 1, pieces):
            block = block_of(number)
            add(part, other, block)
            add(other, part, block.T)
            number += 1
    total = jnp.concatenate([total[part : part + 1] for part in range(pieces)], axis=1)
    root_and_apply(gram_ref[...], drive_ref[...] + total, mean_ref, anomaly_ref, out_ref)


def shards(
    background, conv_pert, conv_misfit, conv_column, sat_pert, sat_misfit, sat_rows, sat_targets
):
    members, cells = background.shape[2:]
    conv = conv_pert.shape[2]
    tiles, obs = sat_pert.shape[1:3]
    blocks, bands = lax.axis_size("lon"), lax.axis_size("lat")
    shape = jax.ShapeDtypeStruct

    pieces = members // LANES
    packet = pieces * 4 * obs + PAD
    triangles = pieces * pieces // 2
    full = triangles * LANES + PAD
    half = triangles // 2 * LANES
    message = shape((full, LANES), BF16)

    def ring(values, step):
        return lax.ppermute(values, "lon", [(i, (i + step * COLUMNS) % blocks) for i in range(blocks)])

    def trade(values, mate):
        return lax.ppermute(values, "lon", [(i, i ^ mate) for i in range(blocks)])

    lists = jnp.concatenate([jnp.swapaxes(sat_targets[0], 0, 1), sat_rows])
    pert1, misfit1, lists1 = trade(sat_pert[0], 2), trade(sat_misfit[0], 2), trade(lists, 2)
    halo = call(
        halo_body,
        shape((conv + PAD, members), BF16),
        [pltpu.HBM] * 3,
        [pltpu.VMEM((1, conv), BF16), pltpu.VMEM((1, conv), jnp.int32), pltpu.SemaphoreType.DMA((3,))],
        limit=None,
    )(conv_pert[0, 0], conv_misfit[0], conv_column[0])
    east = [(i, (i + 1) % blocks) for i in range(blocks)]
    west = [(target, source) for source, target in east]
    low = lax.ppermute(halo, "lon", east)
    high = lax.ppermute(halo, "lon", west)
    gram_conv, drive_conv, to_north, to_south = call(
        conv_body,
        (shape((members, members), F32), shape((1, members), F32), message, message),
        [VMEM] * 3,
        [pltpu.VMEM((3 * conv, members), BF16), pltpu.VMEM((3 * conv, members), BF16)],
    )(low, halo, high)
    to_north, to_south, pert1 = lax.optimization_barrier((to_north, to_south, pert1))
    north = [(i, i + 1) for i in range(bands - 1)]
    south = [(target, source) for source, target in north]
    below = lax.ppermute(to_north, "lat", north)
    above = lax.ppermute(to_south, "lat", south)
    own, *sends = call(
        route_body,
        tuple(
            shape((count, packet, LANES), BF16)
            for count in [len(OFFSETS)] + [high - low for low, high in CHUNKS]
        ),
        [pltpu.HBM] * 6,
        [
            pltpu.VMEM((2 * tiles, obs, members), BF16),
            pltpu.VMEM((2 * tiles, obs), BF16),
            pltpu.SMEM((2, LOC + 1, tiles), jnp.int32),
            pltpu.SMEM((4 * blocks,), jnp.int32),
            pltpu.SMEM((blocks,), jnp.int32),
            pltpu.SemaphoreType.DMA((6,)),
        ],
        limit=None,
    )(sat_pert[0], pert1, sat_misfit[0], misfit1, lists, lists1)
    got = [trade(values, 1) for values in sends]
    scratch = [pltpu.VMEM((8 * obs, members), BF16)]
    up, down = call(
        open_body, (shape((half, LANES), BF16), shape((full - half, LANES), BF16)), [VMEM] * 2, scratch
    )(own, got[0])
    for step, at in enumerate((1, 3, 5)):
        up, down = ring(up, 1), ring(down, -1)
        if step == 2:
            up, down, below, above = lax.optimization_barrier((up, down, below, above))
        up, down = call(
            functools.partial(step_body, at, at - CHUNKS[1][0]), (message, message), [VMEM] * 4, scratch
        )(own, got[1], up, down)
    up, down = ring(up, 1), ring(down, -1)

    anomaly, mean = call(
        background_body, (shape((members, cells), BF16), shape((1, cells), F32)), [VMEM]
    )(background[0, 0])
    result = call(
        functools.partial(final_body, 7, 7 - CHUNKS[1][0]),
        shape((members, cells), F32),
        [VMEM] * 10,
        scratch + [pltpu.VMEM((members, members), F32)],
    )(own, got[1], up, down, below, above, gram_conv, drive_conv, mean, anomaly)
    return result[None, None]


def solution(mesh):
    placed = (
        P("lat", "lon", None, None),
        P("lat", "lon", None, None),
        P("lat", "lon", None),
        P("lat", "lon", None),
        P("lat", "lon", None, None),
        P("lat", "lon", None),
        P("lat", "lon"),
        P("lat", "lon", None),
    )
    return jax.shard_map(
        shards, mesh=mesh, in_specs=placed, out_specs=P("lat", "lon", None, None), check_vma=False
    )
```

time: 84.6 us -> 76.3 us (0.902)
  the two profiles are of different devices: /device:TPU:6 before, /device:TPU:24 now
where the time goes in v5:
time: 76.3 us; the launch traced here: 74.8 us
  starting transfers between devices  32.9 us (43%)
  waiting for transfers between devices  23.7 us (31%)
  Pallas kernels  13.7 us (18%)
  local copies, waits for them, and re-layouts  3.51 us (5%)
    ppermute x8, starting transfers between devices, ring(): lax.ppermute(values, 'lon', [(i, (i + step * COLUMNS) % blocks) for i in...  15.9 us
    ppermute x8, waiting for transfers between devices, ring(): lax.ppermute(values, 'lon', [(i, (i + step * COLUMNS) % blocks) for i in...  10.7 us
    ppermute x1, waiting for transfers between devices, shards(): above = lax.ppermute(to_south, 'lat', south)  6.43 us
    ppermute x5, starting transfers between devices, trade(): return lax.ppermute(values, 'lon', [(i, i ^ mate) for i in range(blocks)])  5.53 us
    pallas_call x1, Pallas kernels, shards(): call(functools.partial(final_body, 7, 7 - CHUNKS[1][0]), shape((members,...  5.12 us
    ppermute x1, starting transfers between devices, shards(): high = lax.ppermute(halo, 'lon', west)  5.06 us
    ppermute x1, starting transfers between devices, shards(): below = lax.ppermute(to_north, 'lat', north)  4.57 us
    ppermute x1, waiting for transfers between devices, shards(): low = lax.ppermute(halo, 'lon', east)  4 us
  transfers between devices with their start and end apart: 17, of which 6 were waited for; matrix products, arithmetic and copies ran while one was open for 1% of the time, Pallas kernels for 5%

profile of v5, /device:TPU:24, one launch (start us, length us, event | category | flops | bytes accessed | tf_op | source)
XLA Modules:
  0.0 74.8 jit_solution(6929694887655306740)
XLA Ops:
  0.0 1.5 %collective-permute-start.2 = (bf16[16,32,512]{2,1,0:T(8,128)(2,1)}, bf16[16,32,512]{2,1,0:T(8,128)(2,1)S(1)}, u32[]{:S(2)}, u32[]{:S(2)}) collective-permute-start(bf16[16,32,512]{2,1,0:T(8,128)(2,1)} %bitcast.11), channel_id=1, source_target_pairs={{0,2},{1,3},{2,0},{3,1},{4,6},{5,7},{6,4},{7,5},{8,10},{9,11},{10,... | collective-permute-start | bytes 1572872 | tf_op jit(solution)/shard_map/ppermute | solution.py:383
  1.5 1.6 %shard_map.82.halo_ref = bf16[144,512]{1,0:T(8,128)(2,1)} custom-call(bf16[128,512]{1,0:T(8,128)(2,1)} %bitcast.13, bf16[1,128]{1,0:T(2,128)(2,1)} %bitcast.17, s32[1,128]{1,0:T(1,128)} %bitcast.18), custom_call_target="tpu_custom_call" | custom-call | tf_op jit(solution)/shard_map/pallas_call | solution.py:387
  3.1 5.1 %collective-permute-start.1 = (bf16[144,512]{1,0:T(8,128)(2,1)}, bf16[144,512]{1,0:T(8,128)(2,1)S(1)}, u32[]{:S(2)}, u32[]{:S(2)}) collective-permute-start(bf16[144,512]{1,0:T(8,128)(2,1)} %shard_map.82.halo_ref), channel_id=1, source_target_pairs={{1,0},{2,1},{3,2},{4,3},{5,4},{6,5},{7,6},{8,7},{9,8},{10,9},{11,1... | collective-permute-start | bytes 442376 | tf_op jit(solution)/shard_map/ppermute | solution.py:397
  8.2 0.7 pad_add_fusion.lists0_hbm
  8.9 2.1 %collective-permute-start.4 = (s32[3,16]{1,0:T(4,128)S(1)}, s32[3,16]{1,0:T(4,128)S(1)}, u32[]{:S(2)}, u32[]{:S(2)}) collective-permute-start(s32[3,16]{1,0:T(4,128)S(1)} %pad_add_fusion.lists0_hbm), channel_id=1, source_target_pairs={{0,2},{1,3},{2,0},{3,1},{4,6},{5,7},{6,4},{7,5},{8,10},{9,11},{10,... | collective-permute-start | bytes 584 | tf_op jit(solution)/shard_map/ppermute | solution.py:383
  11.2 4.0 %collective-permute-done.low_ref = bf16[144,512]{1,0:T(8,128)(2,1)S(1)} collective-permute-done((bf16[144,512]{1,0:T(8,128)(2,1)}, bf16[144,512]{1,0:T(8,128)(2,1)S(1)}, u32[]{:S(2)}, u32[]{:S(2)}) %collective-permute-start) | collective-permute-done | bytes 147488 | tf_op jit(solution)/shard_map/ppermute | solution.py:396
  15.2 0.9 %copy-done.3 = bf16[144,512]{1,0:T(8,128)(2,1)S(1)} copy-done((bf16[144,512]{1,0:T(8,128)(2,1)S(1)}, bf16[144,512]{1,0:T(8,128)(2,1)}, u32[]{:S(2)}) %copy-start.3) | copy-done | bytes 147480
  16.1 1.2 %shard_map.83 = (f32[512,512]{1,0:T(8,128)S(1)}, f32[1,512]{1,0:T(1,128)S(1)}, bf16[1040,128]{1,0:T(8,128)(2,1)S(1)}, bf16[1040,128]{1,0:T(8,128)(2,1)S(1)}) custom-call(bf16[144,512]{1,0:T(8,128)(2,1)S(1)} %collective-permute-done.low_ref, bf16[144,512]{1,0:T(8,128)(2,1)S(1)} %copy-done.3, bf16[144,512]{1,0:T(8,128)(2,1)S(1)} %collective-permute-done.1.high_ref), custom_call_target="tpu_custom_call" | custom-call | tf_op jit(solution)/shard_map/pallas_call | solution.py:398
  17.4 0.8 %copy-done.4 = bf16[16,32,512]{2,1,0:T(8,128)(2,1)} copy-done((bf16[16,32,512]{2,1,0:T(8,128)(2,1)}, bf16[16,32,512]{2,1,0:T(8,128)(2,1)S(1)}, u32[]{:S(2)}) %copy-start.4) | copy-done | bytes 524312
  18.1 0.6 copy-done.6
  18.7 3.6 %shard_map.84 = (bf16[8,528,128]{2,1,0:T(8,128)(2,1)}, bf16[1,528,128]{2,1,0:T(8,128)(2,1)}, bf16[7,528,128]{2,1,0:T(8,128)(2,1)}) custom-call(bf16[16,32,512]{2,1,0:T(8,128)(2,1)} %bitcast.12, bf16[16,32,512]{2,1,0:T(8,128)(2,1)} %copy-done.4, bf16[16,32]{1,0:T(8,128)(2,1)} %bitcast.15, bf16[16,32]{1,0:T(8,128)(2,1)} %copy-done.6, s32[3,16]{1,0:T(4,128)} %copy-done.5, ...), custom_call_target="tpu_custom_call" | custom-call | tf_op jit(solution)/shard_map/pallas_call | solution.py:409
  22.3 1.8 %collective-permute-start.5 = (bf16[7,528,128]{2,1,0:T(8,128)(2,1)}, bf16[7,528,128]{2,1,0:T(8,128)(2,1)S(1)}, u32[]{:S(2)}, u32[]{:S(2)}) collective-permute-start(bf16[7,528,128]{2,1,0:T(8,128)(2,1)} %get-tuple-element.33), channel_id=1, source_target_pairs={{0,1},{1,0},{2,3},{3,2},{4,5},{5,4},{6,7},{7,6},{8,9},{9,8},{10,11... | collective-permute-start | bytes 2838536 | tf_op jit(solution)/shard_map/ppermute | solution.py:383
  24.2 2.4 %collective-permute-done.6.mate_ref = bf16[1,528,128]{2,1,0:T(8,128)(2,1)S(1)} collective-permute-done((bf16[1,528,128]{2,1,0:T(8,128)(2,1)}, bf16[1,528,128]{2,1,0:T(8,128)(2,1)S(1)}, u32[]{:S(2)}, u32[]{:S(2)}) %collective-permute-start.6) | collective-permute-done | bytes 135200 | tf_op jit(solution)/shard_map/ppermute | solution.py:383
  26.7 1.2 %copy-done = bf16[8,528,128]{2,1,0:T(8,128)(2,1)S(1)} copy-done((bf16[8,528,128]{2,1,0:T(8,128)(2,1)S(1)}, bf16[8,528,128]{2,1,0:T(8,128)(2,1)}, u32[]{:S(2)}) %copy-start) | copy-done | bytes 1081368
  28.3 5.9 %collective-permute-start.8 = (bf16[528,128]{1,0:T(8,128)(2,1)S(1)}, bf16[528,128]{1,0:T(8,128)(2,1)S(1)}, u32[]{:S(2)}, u32[]{:S(2)}) collective-permute-start(bf16[528,128]{1,0:T(8,128)(2,1)S(1)} %get-tuple-element.36), channel_id=1, source_target_pairs={{0,28},{1,29},{2,30},{3,31},{4,0},{5,1},{6,2},{7,3},{8,4},{9,5},{1... | collective-permute-start | bytes 405512 | tf_op jit(solution)/shard_map/ppermute | solution.py:380
  34.2 6.7 %collective-permute-done.7.up_in = bf16[512,128]{1,0:T(8,128)(2,1)S(1)} collective-permute-done((bf16[512,128]{1,0:T(8,128)(2,1)S(1)}, bf16[512,128]{1,0:T(8,128)(2,1)S(1)}, u32[]{:S(2)}, u32[]{:S(2)}) %collective-permute-start.7) | collective-permute-done | bytes 131104 | tf_op jit(solution)/shard_map/ppermute | solution.py:380
  41.5 3.2 %collective-permute-start.10 = (bf16[1040,128]{1,0:T(8,128)(2,1)S(1)}, bf16[1040,128]{1,0:T(8,128)(2,1)S(1)}, u32[]{:S(2)}, u32[]{:S(2)}) collective-permute-start(bf16[1040,128]{1,0:T(8,128)(2,1)S(1)} %get-tuple-element.38), channel_id=1, source_target_pairs={{0,28},{1,29},{2,30},{3,31},{4,0},{5,1},{6,2},{7,3},{8,4},{9,5},{1... | collective-permute-start | bytes 798728 | tf_op jit(solution)/shard_map/ppermute | solution.py:380
  44.7 4.6 %collective-permute-start.13 = (bf16[1040,128]{1,0:T(8,128)(2,1)S(1)}, bf16[1040,128]{1,0:T(8,128)(2,1)S(1)}, u32[]{:S(2)}, u32[]{:S(2)}) collective-permute-start(bf16[1040,128]{1,0:T(8,128)(2,1)S(1)} %get-tuple-element.41), channel_id=1, source_target_pairs={{0,32},{32,64},{64,96},{96,128},{128,160},{160,192},{192,224},{1,3... | collective-permute-start | bytes 798728 | tf_op jit(solution)/shard_map/ppermute | solution.py:407
  49.3 1.9 %collective-permute-start.14 = (bf16[1040,128]{1,0:T(8,128)(2,1)S(1)}, bf16[1040,128]{1,0:T(8,128)(2,1)S(1)}, u32[]{:S(2)}, u32[]{:S(2)}) collective-permute-start(bf16[1040,128]{1,0:T(8,128)(2,1)S(1)} %get-tuple-element.42), channel_id=1, source_target_pairs={{32,0},{64,32},{96,64},{128,96},{160,128},{192,160},{224,192},{33,... | collective-permute-start | bytes 798728 | tf_op jit(solution)/shard_map/ppermute | solution.py:408
  51.8 3.2 %collective-permute-start.12 = (bf16[1040,128]{1,0:T(8,128)(2,1)S(1)}, bf16[1040,128]{1,0:T(8,128)(2,1)S(1)}, u32[]{:S(2)}, u32[]{:S(2)}) collective-permute-start(bf16[1040,128]{1,0:T(8,128)(2,1)S(1)} %get-tuple-element.40), channel_id=1, source_target_pairs={{0,28},{1,29},{2,30},{3,31},{4,0},{5,1},{6,2},{7,3},{8,4},{9,5},{1... | collective-permute-start | bytes 798728 | tf_op jit(solution)/shard_map/ppermute | solution.py:380
  55.1 6.4 %collective-permute-done.14.above_ref = bf16[1040,128]{1,0:T(8,128)(2,1)S(1)} collective-permute-done((bf16[1040,128]{1,0:T(8,128)(2,1)S(1)}, bf16[1040,128]{1,0:T(8,128)(2,1)S(1)}, u32[]{:S(2)}, u32[]{:S(2)}) %collective-permute-start.14) | collective-permute-done | bytes 266272 | tf_op jit(solution)/shard_map/ppermute | solution.py:408
  62.1 3.2 %collective-permute-start.16 = (bf16[1040,128]{1,0:T(8,128)(2,1)S(1)}, bf16[1040,128]{1,0:T(8,128)(2,1)S(1)}, u32[]{:S(2)}, u32[]{:S(2)}) collective-permute-start(bf16[1040,128]{1,0:T(8,128)(2,1)S(1)} %get-tuple-element.46), channel_id=1, source_target_pairs={{0,28},{1,29},{2,30},{3,31},{4,0},{5,1},{6,2},{7,3},{8,4},{9,5},{1... | collective-permute-start | bytes 798728 | tf_op jit(solution)/shard_map/ppermute | solution.py:380
  65.7 4.0 %collective-permute-done.15.up_ref = bf16[1040,128]{1,0:T(8,128)(2,1)S(1)} collective-permute-done((bf16[1040,128]{1,0:T(8,128)(2,1)S(1)}, bf16[1040,128]{1,0:T(8,128)(2,1)S(1)}, u32[]{:S(2)}, u32[]{:S(2)}) %collective-permute-start.15) | collective-permute-done | bytes 266272 | tf_op jit(solution)/shard_map/ppermute | solution.py:380
  69.7 5.1 %shard_map.90 = f32[512,1024]{1,0:T(8,128)} custom-call(bf16[8,528,128]{2,1,0:T(8,128)(2,1)S(1)} %copy-done.1, bf16[7,528,128]{2,1,0:T(8,128)(2,1)S(1)} %collective-permute-done.5.mate_ref, bf16[1040,128]{1,0:T(8,128)(2,1)S(1)} %collective-permute-done.15.up_ref, bf16[1040,128]{1,0:T(8,128)(2,1)S(1)} %collective-permute-done.16.down_ref, ...), custom_call_target="tpu_custom_call" | custom-call | tf_op jit(solution)/shard_map/pallas_call | solution.py:443
  (36 shorter events, 2.8 us)
Async XLA Ops:
  0.0 17.3 %collective-permute-start.2 = (bf16[16,32,512]{2,1,0:T(8,128)(2,1)}, bf16[16,32,512]{2,1,0:T(8,128)(2,1)S(1)}, u32[]{:S(2)}, u32[]{:S(2)}) collective-permute-start(bf16[16,32,512]{2,1,0:T(8,128)(2,1)} %bitcast.11), channel_id=1, source_target_pairs={{0,2},{1,3},{2,0},{3,1},{4,6},{5,7},{6,4},{7,5},{8,10},{9,11},{10,... | collective-permute-start | bytes 1572872 | tf_op jit(solution)/shard_map/ppermute | solution.py:383
  3.1 8.1 %collective-permute-start.1 = (bf16[144,512]{1,0:T(8,128)(2,1)}, bf16[144,512]{1,0:T(8,128)(2,1)S(1)}, u32[]{:S(2)}, u32[]{:S(2)}) collective-permute-start(bf16[144,512]{1,0:T(8,128)(2,1)} %shard_map.82.halo_ref), channel_id=1, source_target_pairs={{1,0},{2,1},{3,2},{4,3},{5,4},{6,5},{7,6},{8,7},{9,8},{10,9},{11,1... | collective-permute-start | bytes 442376 | tf_op jit(solution)/shard_map/ppermute | solution.py:397
  8.2 7.0 %collective-permute-start = (bf16[144,512]{1,0:T(8,128)(2,1)}, bf16[144,512]{1,0:T(8,128)(2,1)S(1)}, u32[]{:S(2)}, u32[]{:S(2)}) collective-permute-start(bf16[144,512]{1,0:T(8,128)(2,1)} %shard_map.82.halo_ref), channel_id=1, source_target_pairs={{0,1},{1,2},{2,3},{3,4},{4,5},{5,6},{6,7},{7,8},{8,9},{9,10},{10,1... | collective-permute-start | bytes 442376 | tf_op jit(solution)/shard_map/ppermute | solution.py:396
  8.2 9.2 %collective-permute-start.3 = (bf16[16,32]{1,0:T(8,128)(2,1)}, bf16[16,32]{1,0:T(8,128)(2,1)S(1)}, u32[]{:S(2)}, u32[]{:S(2)}) collective-permute-start(bf16[16,32]{1,0:T(8,128)(2,1)} %bitcast.14), channel_id=1, source_target_pairs={{0,2},{1,3},{2,0},{3,1},{4,6},{5,7},{6,4},{7,5},{8,10},{9,11},{10,... | collective-permute-start | bytes 3080 | tf_op jit(solution)/shard_map/ppermute | solution.py:383
  8.9 8.5 %copy-start.5 = (s32[3,16]{1,0:T(4,128)}, s32[3,16]{1,0:T(4,128)S(1)}, u32[]{:S(2)}) copy-start(s32[3,16]{1,0:T(4,128)S(1)} %pad_add_fusion.lists0_hbm) | copy-start | bytes 580
  8.9 8.4 %collective-permute-start.4 = (s32[3,16]{1,0:T(4,128)S(1)}, s32[3,16]{1,0:T(4,128)S(1)}, u32[]{:S(2)}, u32[]{:S(2)}) collective-permute-start(s32[3,16]{1,0:T(4,128)S(1)} %pad_add_fusion.lists0_hbm), channel_id=1, source_target_pairs={{0,2},{1,3},{2,0},{3,1},{4,6},{5,7},{6,4},{7,5},{8,10},{9,11},{10,... | collective-permute-start | bytes 584 | tf_op jit(solution)/shard_map/ppermute | solution.py:383
  15.2 0.9 %copy-start.3 = (bf16[144,512]{1,0:T(8,128)(2,1)S(1)}, bf16[144,512]{1,0:T(8,128)(2,1)}, u32[]{:S(2)}) copy-start(bf16[144,512]{1,0:T(8,128)(2,1)} %shard_map.82.halo_ref) | copy-start | bytes 442372
  17.3 0.8 %copy-start.4 = (bf16[16,32,512]{2,1,0:T(8,128)(2,1)}, bf16[16,32,512]{2,1,0:T(8,128)(2,1)S(1)}, u32[]{:S(2)}) copy-start(bf16[16,32,512]{2,1,0:T(8,128)(2,1)S(1)} %collective-permute-done.2.pert1_hbm) | copy-start | bytes 1572868
  17.4 0.8 %copy-start.7 = (s32[3,16]{1,0:T(4,128)}, s32[3,16]{1,0:T(4,128)S(1)}, u32[]{:S(2)}) copy-start(s32[3,16]{1,0:T(4,128)S(1)} %collective-permute-done.4.lists1_hbm) | copy-start | bytes 580
  22.3 18.6 %collective-permute-start.5 = (bf16[7,528,128]{2,1,0:T(8,128)(2,1)}, bf16[7,528,128]{2,1,0:T(8,128)(2,1)S(1)}, u32[]{:S(2)}, u32[]{:S(2)}) collective-permute-start(bf16[7,528,128]{2,1,0:T(8,128)(2,1)} %get-tuple-element.33), channel_id=1, source_target_pairs={{0,1},{1,0},{2,3},{3,2},{4,5},{5,4},{6,7},{7,6},{8,9},{9,8},{10,11... | collective-permute-start | bytes 2838536 | tf_op jit(solution)/shard_map/ppermute | solution.py:383
  24.1 2.5 %collective-permute-start.6 = (bf16[1,528,128]{2,1,0:T(8,128)(2,1)}, bf16[1,528,128]{2,1,0:T(8,128)(2,1)S(1)}, u32[]{:S(2)}, u32[]{:S(2)}) collective-permute-start(bf16[1,528,128]{2,1,0:T(8,128)(2,1)} %get-tuple-element.34), channel_id=1, source_target_pairs={{0,1},{1,0},{2,3},{3,2},{4,5},{5,4},{6,7},{7,6},{8,9},{9,8},{10,11... | collective-permute-start | bytes 405512 | tf_op jit(solution)/shard_map/ppermute | solution.py:383
  26.7 1.2 %copy-start = (bf16[8,528,128]{2,1,0:T(8,128)(2,1)S(1)}, bf16[8,528,128]{2,1,0:T(8,128)(2,1)}, u32[]{:S(2)}) copy-start(bf16[8,528,128]{2,1,0:T(8,128)(2,1)} %get-tuple-element.32.own_ref) | copy-start | bytes 3244036
  28.3 12.6 %collective-permute-start.8 = (bf16[528,128]{1,0:T(8,128)(2,1)S(1)}, bf16[528,128]{1,0:T(8,128)(2,1)S(1)}, u32[]{:S(2)}, u32[]{:S(2)}) collective-permute-start(bf16[528,128]{1,0:T(8,128)(2,1)S(1)} %get-tuple-element.36), channel_id=1, source_target_pairs={{0,28},{1,29},{2,30},{3,31},{4,0},{5,1},{6,2},{7,3},{8,4},{9,5},{1... | collective-permute-start | bytes 405512 | tf_op jit(solution)/shard_map/ppermute | solution.py:380
  34.2 6.7 %collective-permute-start.7 = (bf16[512,128]{1,0:T(8,128)(2,1)S(1)}, bf16[512,128]{1,0:T(8,128)(2,1)S(1)}, u32[]{:S(2)}, u32[]{:S(2)}) collective-permute-start(bf16[512,128]{1,0:T(8,128)(2,1)S(1)} %get-tuple-element.35), channel_id=1, source_target_pairs={{0,4},{1,5},{2,6},{3,7},{4,8},{5,9},{6,10},{7,11},{8,12},{9,13},{1... | collective-permute-start | bytes 393224 | tf_op jit(solution)/shard_map/ppermute | solution.py:380
  41.4 9.8 %collective-permute-start.9 = (bf16[1040,128]{1,0:T(8,128)(2,1)S(1)}, bf16[1040,128]{1,0:T(8,128)(2,1)S(1)}, u32[]{:S(2)}, u32[]{:S(2)}) collective-permute-start(bf16[1040,128]{1,0:T(8,128)(2,1)S(1)} %get-tuple-element.37), channel_id=1, source_target_pairs={{0,4},{1,5},{2,6},{3,7},{4,8},{5,9},{6,10},{7,11},{8,12},{9,13},{1... | collective-permute-start | bytes 798728 | tf_op jit(solution)/shard_map/ppermute | solution.py:380
  41.5 23.8 %copy-start.2 = (bf16[1,1,512,1024]{3,2,1,0:T(8,128)(2,1)S(1)}, bf16[1,1,512,1024]{3,2,1,0:T(8,128)(2,1)}, u32[]{:S(2)}) copy-start(bf16[1,1,512,1024]{3,2,1,0:T(8,128)(2,1)} %param.8) | copy-start | bytes 3145732
  41.5 9.7 %collective-permute-start.10 = (bf16[1040,128]{1,0:T(8,128)(2,1)S(1)}, bf16[1040,128]{1,0:T(8,128)(2,1)S(1)}, u32[]{:S(2)}, u32[]{:S(2)}) collective-permute-start(bf16[1040,128]{1,0:T(8,128)(2,1)S(1)} %get-tuple-element.38), channel_id=1, source_target_pairs={{0,28},{1,29},{2,30},{3,31},{4,0},{5,1},{6,2},{7,3},{8,4},{9,5},{1... | collective-permute-start | bytes 798728 | tf_op jit(solution)/shard_map/ppermute | solution.py:380
  44.7 10.4 %collective-permute-start.13 = (bf16[1040,128]{1,0:T(8,128)(2,1)S(1)}, bf16[1040,128]{1,0:T(8,128)(2,1)S(1)}, u32[]{:S(2)}, u32[]{:S(2)}) collective-permute-start(bf16[1040,128]{1,0:T(8,128)(2,1)S(1)} %get-tuple-element.41), channel_id=1, source_target_pairs={{0,32},{32,64},{64,96},{96,128},{128,160},{160,192},{192,224},{1,3... | collective-permute-start | bytes 798728 | tf_op jit(solution)/shard_map/ppermute | solution.py:407
  49.3 12.2 %collective-permute-start.14 = (bf16[1040,128]{1,0:T(8,128)(2,1)S(1)}, bf16[1040,128]{1,0:T(8,128)(2,1)S(1)}, u32[]{:S(2)}, u32[]{:S(2)}) collective-permute-start(bf16[1040,128]{1,0:T(8,128)(2,1)S(1)} %get-tuple-element.42), channel_id=1, source_target_pairs={{32,0},{64,32},{96,64},{128,96},{160,128},{192,160},{224,192},{33,... | collective-permute-start | bytes 798728 | tf_op jit(solution)/shard_map/ppermute | solution.py:408
  51.7 18.0 %copy-start.1 = (bf16[8,528,128]{2,1,0:T(8,128)(2,1)S(1)}, bf16[8,528,128]{2,1,0:T(8,128)(2,1)}, u32[]{:S(2)}) copy-start(bf16[8,528,128]{2,1,0:T(8,128)(2,1)} %get-tuple-element.32.own_ref) | copy-start | bytes 3244036
  51.7 9.8 %collective-permute-start.11 = (bf16[1040,128]{1,0:T(8,128)(2,1)S(1)}, bf16[1040,128]{1,0:T(8,128)(2,1)S(1)}, u32[]{:S(2)}, u32[]{:S(2)}) collective-permute-start(bf16[1040,128]{1,0:T(8,128)(2,1)S(1)} %get-tuple-element.39), channel_id=1, source_target_pairs={{0,4},{1,5},{2,6},{3,7},{4,8},{5,9},{6,10},{7,11},{8,12},{9,13},{1... | collective-permute-start | bytes 798728 | tf_op jit(solution)/shard_map/ppermute | solution.py:380
  51.8 9.7 %collective-permute-start.12 = (bf16[1040,128]{1,0:T(8,128)(2,1)S(1)}, bf16[1040,128]{1,0:T(8,128)(2,1)S(1)}, u32[]{:S(2)}, u32[]{:S(2)}) collective-permute-start(bf16[1040,128]{1,0:T(8,128)(2,1)S(1)} %get-tuple-element.40), channel_id=1, source_target_pairs={{0,28},{1,29},{2,30},{3,31},{4,0},{5,1},{6,2},{7,3},{8,4},{9,5},{1... | collective-permute-start | bytes 798728 | tf_op jit(solution)/shard_map/ppermute | solution.py:380
  62.0 7.7 %collective-permute-start.15 = (bf16[1040,128]{1,0:T(8,128)(2,1)S(1)}, bf16[1040,128]{1,0:T(8,128)(2,1)S(1)}, u32[]{:S(2)}, u32[]{:S(2)}) collective-permute-start(bf16[1040,128]{1,0:T(8,128)(2,1)S(1)} %get-tuple-element.45), channel_id=1, source_target_pairs={{0,4},{1,5},{2,6},{3,7},{4,8},{5,9},{6,10},{7,11},{8,12},{9,13},{1... | collective-permute-start | bytes 798728 | tf_op jit(solution)/shard_map/ppermute | solution.py:380
  62.1 7.6 %collective-permute-start.16 = (bf16[1040,128]{1,0:T(8,128)(2,1)S(1)}, bf16[1040,128]{1,0:T(8,128)(2,1)S(1)}, u32[]{:S(2)}, u32[]{:S(2)}) collective-permute-start(bf16[1040,128]{1,0:T(8,128)(2,1)S(1)} %get-tuple-element.46), channel_id=1, source_target_pairs={{0,28},{1,29},{2,30},{3,31},{4,0},{5,1},{6,2},{7,3},{8,4},{9,5},{1... | collective-permute-start | bytes 798728 | tf_op jit(solution)/shard_map/ppermute | solution.py:380
  (1 other events, 0.6 us)

commit v6 on v5

v6 whole, which is shorter than its diff:
```python
import functools

import jax
import jax.numpy as jnp
from jax import lax
from jax.experimental import pallas as pl
from jax.experimental.pallas import tpu as pltpu
from jax.sharding import PartitionSpec as P

BLK = 16
LOC = 2
F32 = jnp.float32
BF16 = jnp.bfloat16
PAD = 16
LANES = 128
COLUMNS = 4
OFFSETS = (4, 3, -3, 2, -2, 1, -1, 0)
CHUNKS = ((0, 1), (1, 8))
VMEM = pltpu.VMEM
SMEM = pltpu.SMEM
LIMIT = 48 * 1024 * 1024


def call(body, outs, in_spaces, scratch=(), limit=LIMIT, flops=0, moved=0, out_space=VMEM):
    return pl.pallas_call(
        body,
        out_shape=outs,
        in_specs=[pl.BlockSpec(memory_space=space) for space in in_spaces],
        out_specs=jax.tree.map(lambda _: pl.BlockSpec(memory_space=out_space), outs),
        scratch_shapes=list(scratch),
        compiler_params=pltpu.CompilerParams(vmem_limit_bytes=limit),
        cost_estimate=pl.CostEstimate(flops=flops, bytes_accessed=moved, transcendentals=0),
    )


def transposed_dot(left, right):
    return lax.dot_general(left, right, (((0,), (0,)), ((), ())), preferred_element_type=F32)


def dot(left, right):
    return jnp.dot(left, right, preferred_element_type=F32)


def background_body(ensemble_ref, anomaly_ref, mean_ref):
    values = ensemble_ref[...].astype(F32)
    mean = jnp.mean(values, axis=0, keepdims=True)
    mean_ref[...] = mean
    anomaly_ref[...] = (values - mean).astype(BF16)


def halo_body(conv_hbm, misfit_hbm, column_hbm, halo_ref, misfit_ref, column_ref, sems):
    conv, members = conv_hbm.shape
    copies = [
        pltpu.make_async_copy(misfit_hbm, misfit_ref, sems.at[0]),
        pltpu.make_async_copy(column_hbm, column_ref, sems.at[1]),
        pltpu.make_async_copy(conv_hbm, halo_ref.at[0:conv], sems.at[2]),
    ]
    for copy in copies:
        copy.start()
    first = lax.broadcasted_iota(jnp.int32, (PAD, conv), 0) == 0
    halo_ref[conv:, :] = jnp.zeros((PAD, members), BF16)
    copies[0].wait()
    copies[1].wait()
    halo_ref[conv:, 0:conv] = jnp.where(first, misfit_ref[...].astype(F32), 0.0).astype(BF16)
    halo_ref[conv:, conv : 2 * conv] = jnp.where(first, column_ref[...].astype(F32), 0.0).astype(BF16)
    copies[2].wait()


def route_body(
    pert0_ref, pert1_ref, misfit0_ref, misfit1_ref, lists0_hbm, lists1_hbm, *refs
):
    outs = refs[: 2 * len(CHUNKS)]
    lists_ref, entry_ref, count_ref, sems = refs[2 * len(CHUNKS) :]
    tiles, obs, members = pert0_ref.shape
    blocks = count_ref.shape[0] // 2
    copies = [
        pltpu.make_async_copy(lists0_hbm, lists_ref.at[0], sems.at[0]),
        pltpu.make_async_copy(lists1_hbm, lists_ref.at[1], sems.at[1]),
    ]
    for copy in copies:
        copy.start()

    def clear(place, _):
        count_ref[place] = 0
        entry_ref[2 * place] = -1
        entry_ref[2 * place + 1] = -1
        return 0

    lax.fori_loop(0, 2 * blocks, clear, 0, unroll=True)
    for copy in copies:
        copy.wait()
    for source in range(2):
        for tile in range(tiles):
            for k in range(LOC):
                place = 2 * lists_ref[source, k, tile] + source
                used = count_ref[place]
                entry_ref[2 * place + used] = LOC * tile + k
                count_ref[place] = used + 1
    row = lax.broadcasted_iota(jnp.int32, (obs, members), 0)
    me = lax.axis_index("lon")
    planes = blocks // COLUMNS
    plane, column = me // COLUMNS, me % COLUMNS
    places = []
    for mate in range(2):
        there_column = column ^ mate
        sign = 1 - 2 * (there_column % 2)
        for at, offset in enumerate(OFFSETS):
            chunk = [at in range(low, high) for low, high in CHUNKS].index(True)
            there = (plane + sign * offset + planes) % planes
            places.append(
                (outs[mate * len(CHUNKS) + chunk], at - CHUNKS[chunk][0], there * COLUMNS + there_column)
            )
    pieces = members // LANES
    for ref, index, block in places:
        for source, pert_ref in enumerate((pert0_ref, pert1_ref)):
            for turn in range(2):
                entry = entry_ref[4 * block + 2 * source + turn]
                safe = jnp.maximum(entry, 0)
                tile = safe // LOC
                live = jnp.where(entry >= 0, lists_ref[source, LOC, tile], 0)
                factor = jnp.where(safe % LOC == 0, 1.0, 0.5**0.5).astype(F32)
                values = pert_ref[tile].astype(F32) * factor
                values = jnp.where(row < live, values, 0.0).astype(BF16)
                for part in range(pieces):
                    start = (part * 4 + 2 * source + turn) * obs
                    ref[index, start : start + obs, :] = values[:, part * LANES : (part + 1) * LANES]

    total = tiles * obs
    lane = lax.broadcasted_iota(jnp.int32, (1, total), 1)
    own_tile = lane // obs
    repeat = (
        lax.broadcasted_iota(jnp.int32, (obs, total), 1) % obs
        == lax.broadcasted_iota(jnp.int32, (obs, total), 0)
    )
    repeat = jnp.where(repeat, 1.0, 0.0).astype(BF16)
    pick = lax.broadcasted_iota(jnp.int32, (tiles, total), 1) // obs == lax.broadcasted_iota(
        jnp.int32, (tiles, total), 0
    )
    position = lax.broadcasted_iota(jnp.int32, (len(places), 1), 0)
    block = jnp.zeros((len(places), 1), jnp.int32)
    for at, (_, _, there) in enumerate(places):
        block = jnp.where(position == at, there, block)
    drive = jnp.zeros((len(places), members), F32)
    for source, (pert_ref, misfit_ref) in enumerate(
        ((pert0_ref, misfit0_ref), (pert1_ref, misfit1_ref))
    ):
        live = jnp.zeros((1, total), jnp.int32)
        named = [jnp.zeros((1, total), jnp.int32) for _ in range(LOC)]
        for tile in range(tiles):
            here = own_tile == tile
            live = jnp.where(here, lists_ref[source, LOC, tile], live)
            for k in range(LOC):
                named[k] = jnp.where(here, lists_ref[source, k, tile], named[k])
        spread = dot(misfit_ref[...], repeat)
        misfit = jnp.sum(jnp.where(pick, spread, 0.0), axis=0, keepdims=True)
        misfit = jnp.where(lane % obs < live, misfit, 0.0)
        weight = jnp.zeros((len(places), total), F32)
        for k in range(LOC):
            weight = weight + jnp.where(block == named[k], 0.5**k, 0.0)
        drive = drive + dot((weight * misfit).astype(BF16), pert_ref[...].reshape(total, members))
    upper = drive.astype(BF16).astype(F32)
    empty = jnp.zeros((PAD - 2 * pieces, LANES), F32)
    for at, (ref, index, _) in enumerate(places):
        parts = [
            piece[at : at + 1, part * LANES : (part + 1) * LANES]
            for piece in (upper, drive - upper)
            for part in range(pieces)
        ]
        ref[index, 4 * obs * pieces :, :] = jnp.concatenate(parts + [empty]).astype(BF16)


def gather_rows(own_ref, at, mate_ref, index, rows_ref):
    sources = [(own_ref, at), (mate_ref, index)]
    pieces = rows_ref.shape[1] // LANES
    count = (own_ref.shape[1] - PAD) // pieces
    drive = jnp.zeros((PAD, LANES), F32)
    for number, (ref, place) in enumerate(sources):
        for part in range(pieces):
            rows_ref[number * count : (number + 1) * count, part * LANES : (part + 1) * LANES] = ref[
                place, part * count : (part + 1) * count, :
            ]
        drive = drive + ref[place, pieces * count :, :].astype(F32)
    return drive


def triangle(size=LANES):
    across = lax.broadcasted_iota(jnp.int32, (size, size), 1)
    down = lax.broadcasted_iota(jnp.int32, (size, size), 0)
    return down, across


def packed(rows_ref, drive, right_ref=None):
    down, across = triangle()
    right_ref = rows_ref if right_ref is None else right_ref
    pieces = rows_ref.shape[1] // LANES
    bands = []
    for part in range(pieces):
        left = rows_ref[:, part * LANES : (part + 1) * LANES]
        bands.append(transposed_dot(left, right_ref[:, part * LANES :]))
    blocks, diagonals = [], []
    for part in range(0, pieces, 2):
        lower = bands[part + 1][:, 0:LANES]
        blocks.append(jnp.where(down <= across, bands[part][:, 0:LANES], lower))
        diagonals.append(jnp.sum(jnp.where(down == across, lower, 0.0), axis=0, keepdims=True))
    for part in range(pieces):
        for other in range(1, pieces - part):
            blocks.append(bands[part][:, other * LANES : (other + 1) * LANES])
    total = drive[0:pieces] + drive[pieces : 2 * pieces]
    empty = jnp.zeros((PAD - 2 * pieces - len(diagonals), LANES), F32)
    return blocks, total, jnp.concatenate(diagonals), empty


def split_drive(total, diagonals, empty):
    upper = total.astype(BF16).astype(F32)
    return jnp.concatenate([upper, total - upper, diagonals, empty]).astype(BF16)


def extra_of(extra, pieces):
    extra = extra.astype(F32)
    return extra[0:pieces] + extra[pieces : 2 * pieces], extra[2 * pieces : 2 * pieces + pieces // 2]


def open_body(own_ref, mate_ref, up_ref, down_ref, rows_ref):
    drive = gather_rows(own_ref, 0, mate_ref, 0, rows_ref)
    blocks, total, diagonals, empty = packed(rows_ref, drive)
    half = len(blocks) // 4
    for number, block in enumerate(blocks):
        ref, place = (up_ref, number) if number < half else (down_ref, number - half)
        ref[place * LANES : (place + 1) * LANES, :] = block.astype(BF16)
    down_ref[(len(blocks) - half) * LANES :, :] = split_drive(total, diagonals, empty)


def step_body(at, skip, own_ref, mate_ref, came, out, rows_ref):
    pieces = rows_ref.shape[1] // LANES
    drive = gather_rows(own_ref, at, mate_ref, at, rows_ref)
    blocks, total, diagonals, empty = packed(rows_ref, drive)
    for number, block in enumerate(blocks):
        place = (number - skip) * LANES
        if 0 <= place and place + LANES <= came.shape[0]:
            block = block + came[place : place + LANES, :].astype(F32)
        out[number * LANES : (number + 1) * LANES, :] = block.astype(BF16)
    if came.shape[0] % LANES:
        more, more_diagonals = extra_of(came[came.shape[0] - PAD :, :], pieces)
        total, diagonals = total + more, diagonals + more_diagonals
    out[len(blocks) * LANES :, :] = split_drive(total, diagonals, empty)


def conv_body(
    low_ref, halo_ref, high_ref, gram_ref, drive_ref, north_ref, south_ref, scaled_ref, spread_ref
):
    conv, members = halo_ref.shape[0] - PAD, halo_ref.shape[1]
    pieces = members // LANES
    eye = lax.broadcasted_iota(jnp.int32, (conv, conv), 0) == lax.broadcasted_iota(
        jnp.int32, (conv, conv), 1
    )
    refs = ((-1, low_ref), (0, halo_ref), (1, high_ref))
    for b, ref in refs:
        spread_ref[(b + 1) * conv : (b + 2) * conv, :] = ref[0:conv, :]
    for a, out_ref in ((-1, north_ref), (1, south_ref), (0, gram_ref)):
        drive = jnp.zeros((8, members), F32)
        for b, ref in refs:
            misfit = ref[conv : conv + 1, 0:conv]
            column = ref[conv : conv + 1, conv : 2 * conv].astype(F32)
            lat_cell = jnp.floor(column * (1.0 / BLK))
            lon_cell = column - BLK * lat_cell
            lat_place = BLK * a + lat_cell + 0.5 - 0.5 * BLK
            lon_place = BLK * b + lon_cell + 0.5 - 0.5 * BLK
            weight = jnp.exp(-(lat_place * lat_place + lon_place * lon_place) / (2.0 * BLK * BLK))
            weight = jnp.sum(jnp.where(eye, weight, 0.0), axis=1, keepdims=True)
            scaled = (weight * ref[0:conv, :].astype(F32)).astype(BF16)
            scaled_ref[(b + 1) * conv : (b + 2) * conv, :] = scaled
            drive = drive + dot(jnp.broadcast_to(misfit, (8, conv)), scaled)
        if a == 0:
            drive_ref[...] = drive[0:1]
            gram_ref[...] = transposed_dot(scaled_ref[...], spread_ref[...])
            continue
        total = jnp.concatenate(
            [drive[0:1, part * LANES : (part + 1) * LANES] for part in range(pieces)]
            + [jnp.zeros((PAD - pieces, LANES), F32)]
        )
        blocks, total, diagonals, empty = packed(scaled_ref, total, spread_ref)
        for number, block in enumerate(blocks):
            out_ref[number * LANES : (number + 1) * LANES, :] = block.astype(BF16)
        out_ref[len(blocks) * LANES :, :] = split_drive(total, diagonals, empty)


def root(system, drive):
    members = system.shape[0]
    eye = lax.broadcasted_iota(jnp.int32, system.shape, 0) == lax.broadcasted_iota(
        jnp.int32, system.shape, 1
    )
    square = jnp.sum(jnp.sum(system * system, axis=0, keepdims=True), axis=1, keepdims=True)
    inverse_scale = lax.rsqrt(square)
    power1 = system * inverse_scale
    half1 = power1.astype(BF16)
    power2 = dot(half1, half1)
    half2 = power2.astype(BF16)
    power3 = dot(half1, half2)
    power4 = dot(half2, half2)
    product = 2.25 * power1 - 1.5 * power2 + 0.25 * power3
    excess = -0.75 * (power1 + product) + 0.25 * (2.25 * power2 - 1.5 * power3 + 0.25 * power4)
    half_excess = excess.astype(BF16)
    lifted = 4.5 * excess + dot(half_excess, half_excess)
    product = 5.0625 * power1 + dot(half1, lifted.astype(BF16))
    inverse_root = 1.5 * excess - 1.125 * product - 0.5 * dot(product.astype(BF16), half_excess)
    inverse_root = inverse_root + jnp.where(eye, 3.375, 0.0)
    first = jnp.sum(inverse_root * drive, axis=1, keepdims=True)
    weight = jnp.sum(inverse_root * first, axis=0, keepdims=True) * inverse_scale
    return (jnp.sqrt((members - 1.0) * inverse_scale) * inverse_root + weight).astype(BF16)


def unpack_into(gram_ref, arrived, factors):
    pieces = gram_ref.shape[0] // LANES
    total, diagonals = 0.0, 0.0
    for ref, factor in zip(arrived, factors):
        more, more_diagonals = extra_of(ref[ref.shape[0] - PAD :, :], pieces)
        total, diagonals = total + factor * more, diagonals + factor * more_diagonals
    down, across = triangle()

    def add(part, other, block):
        place = (slice(part * LANES, (part + 1) * LANES), slice(other * LANES, (other + 1) * LANES))
        gram_ref[place] = gram_ref[place] + block

    def block_of(number):
        place = slice(number * LANES, (number + 1) * LANES)
        return sum(factor * ref[place, :].astype(F32) for ref, factor in zip(arrived, factors))

    number = 0
    for part in range(0, pieces, 2):
        block = block_of(number)
        turned = block.T
        add(part, part, jnp.where(down <= across, block, turned))
        middle = jnp.where(down == across, diagonals[number : number + 1], turned)
        add(part + 1, part + 1, jnp.where(down > across, block, middle))
        number += 1
    for part in range(pieces):
        for other in range(part + 1, pieces):
            block = block_of(number)
            add(part, other, block)
            add(other, part, block.T)
            number += 1
    return jnp.concatenate([total[part : part + 1] for part in range(pieces)], axis=1)


def base_body(
    at, own_ref, mate_ref, below_ref, above_ref, conv_ref, conv_drive_ref, gram_ref, drive_ref, rows_ref
):
    members = gram_ref.shape[0]
    pieces = members // LANES
    drive = gather_rows(own_ref, at, mate_ref, at, rows_ref)
    rows = rows_ref[...]
    eye = lax.broadcasted_iota(jnp.int32, gram_ref.shape, 0) == lax.broadcasted_iota(
        jnp.int32, gram_ref.shape, 1
    )
    gram_ref[...] = conv_ref[...] + transposed_dot(rows, rows) + jnp.where(eye, members - 1.0, 0.0)
    band = lax.axis_index("lat")
    from_below = jnp.where(band > 0, 1.0, 0.0).astype(F32)
    from_above = jnp.where(band < lax.axis_size("lat") - 1, 1.0, 0.0).astype(F32)
    total = unpack_into(gram_ref, (below_ref, above_ref), (from_below, from_above))
    own = drive[0:pieces] + drive[pieces : 2 * pieces]
    own = jnp.concatenate([own[part : part + 1] for part in range(pieces)], axis=1)
    drive_ref[...] = conv_drive_ref[...] + total + own


def final_body(up_ref, down_ref, base_ref, drive_ref, mean_ref, anomaly_ref, out_hbm, gram_ref, out_ref, sems):
    gram_ref[...] = base_ref[...]
    drive = drive_ref[...] + unpack_into(gram_ref, (up_ref, down_ref), (1.0, 1.0))
    transform = root(gram_ref[...], drive)
    members = gram_ref.shape[0]
    copies = []
    for part in range(members // LANES):
        rows = slice(part * LANES, (part + 1) * LANES)
        out_ref[rows, :] = mean_ref[...] + dot(transform[rows], anomaly_ref[...])
        copies.append(pltpu.make_async_copy(out_ref.at[rows], out_hbm.at[rows], sems.at[part]))
        copies[-1].start()
    for copy in copies:
        copy.wait()


def shards(
    background, conv_pert, conv_misfit, conv_column, sat_pert, sat_misfit, sat_rows, sat_targets
):
    members, cells = background.shape[2:]
    conv = conv_pert.shape[2]
    tiles, obs = sat_pert.shape[1:3]
    blocks, bands = lax.axis_size("lon"), lax.axis_size("lat")
    shape = jax.ShapeDtypeStruct

    pieces = members // LANES
    packet = pieces * 4 * obs + PAD
    triangles = pieces * pieces // 2
    full = triangles * LANES + PAD
    half = triangles // 4 * LANES
    message = shape((full, LANES), BF16)

    def ring(values, step):
        def target(i):
            sign = 1 - 2 * (i % 2)
            return (i + step * sign * COLUMNS) % blocks

        return lax.ppermute(values, "lon", [(i, target(i)) for i in range(blocks)])

    def trade(values, mate):
        return lax.ppermute(values, "lon", [(i, i ^ mate) for i in range(blocks)])

    halo = call(
        halo_body,
        shape((conv + PAD, members), BF16),
        [pltpu.HBM] * 3,
        [pltpu.VMEM((1, conv), BF16), pltpu.VMEM((1, conv), jnp.int32), pltpu.SemaphoreType.DMA((3,))],
        limit=None,
    )(conv_pert[0, 0], conv_misfit[0], conv_column[0])
    east = [(i, (i + 1) % blocks) for i in range(blocks)]
    west = [(target, source) for source, target in east]
    lists = jnp.concatenate([jnp.swapaxes(sat_targets[0], 0, 1), sat_rows])
    pert1, misfit1, lists1 = trade(sat_pert[0], 2), trade(sat_misfit[0], 2), trade(lists, 2)
    anomaly, mean = call(
        background_body, (shape((members, cells), BF16), shape((1, cells), F32)), [VMEM], flops=4 * members * cells, moved=4 * members * cells
    )(background[0, 0])
    halo, anomaly, mean, pert1 = lax.optimization_barrier((halo, anomaly, mean, pert1))
    counts = [high - low for low, high in CHUNKS]
    routed = call(
        route_body,
        tuple(shape((count, packet, LANES), BF16) for count in counts + counts),
        [VMEM] * 4 + [pl.ANY] * 2,
        [
            pltpu.SMEM((2, LOC + 1, tiles), jnp.int32),
            pltpu.SMEM((4 * blocks,), jnp.int32),
            pltpu.SMEM((2 * blocks,), jnp.int32),
            pltpu.SemaphoreType.DMA((2,)),
        ],
    )(sat_pert[0], pert1, sat_misfit[0], misfit1, lists, lists1)
    own, sends = routed[: len(CHUNKS)], routed[len(CHUNKS) :]
    got = [trade(values, 1) for values in sends]
    halo, _ = lax.optimization_barrier((halo, routed[-1]))
    low = lax.ppermute(halo, "lon", east)
    high = lax.ppermute(halo, "lon", west)
    def conv_halo(low, halo, high):
        gram_conv, drive_conv, to_north, to_south = call(
            conv_body,
            (shape((members, members), F32), shape((1, members), F32), message, message),
            [VMEM] * 3,
            [pltpu.VMEM((3 * conv, members), BF16), pltpu.VMEM((3 * conv, members), BF16)],
            flops=18 * conv * members * members,
            moved=8 * members * members,
        )(low, halo, high)
        return gram_conv, drive_conv, to_north, to_south

    north = [(i, (i + 1) % bands) for i in range(bands)]
    south = [(target, source) for source, target in north]
    scratch = [pltpu.VMEM((8 * obs, members), BF16)]
    step_flops, step_bytes = 16 * obs * members * members, 4 * full * LANES
    first, second = call(
        open_body, (shape((half, LANES), BF16), shape((full - half, LANES), BF16)), [VMEM] * 2, scratch
    )(own[0], got[0])
    for step in range(3):
        first = ring(first, 1)
        second = ring(second, -1)
        if step == 0:
            second, low, high = lax.optimization_barrier((second, low, high))
            gram_conv, drive_conv, to_north, to_south = conv_halo(low, halo, high)
        if step == 1:
            first, to_north, to_south = lax.optimization_barrier((first, to_north, to_south))
            below = lax.ppermute(to_north, "lat", north)
            above = lax.ppermute(to_south, "lat", south)
        if step == 2:
            first, below = lax.optimization_barrier((first, below))
            second, above = lax.optimization_barrier((second, above))
        first = call(functools.partial(step_body, 2 * step, 0), message, [VMEM] * 3, scratch, flops=step_flops, moved=step_bytes)(
            own[1], got[1], first
        )
        skip = triangles // 4 if step == 0 else 0
        second = call(functools.partial(step_body, 2 * step + 1, skip), message, [VMEM] * 3, scratch, flops=step_flops, moved=step_bytes)(
            own[1], got[1], second
        )
    first, second = ring(first, 1), ring(second, -1)

    base, drive = call(
        functools.partial(base_body, 6),
        (shape((members, members), F32), shape((1, members), F32)),
        [VMEM] * 6,
        scratch,
        flops=16 * obs * members * members,
        moved=8 * members * members,
    )(own[1], got[1], below, above, gram_conv, drive_conv)
    result = call(
        final_body,
        shape((members, cells), F32),
        [VMEM] * 6,
        [
            pltpu.VMEM((members, members), F32),
            pltpu.VMEM((members, cells), F32),
            pltpu.SemaphoreType.DMA((members // LANES,)),
        ],
        out_space=pl.ANY,
    )(first, second, base, drive, mean, anomaly)
    return result[None, None]


def solution(mesh):
    placed = (
        P("lat", "lon", None, None),
        P("lat", "lon", None, None),
        P("lat", "lon", None),
        P("lat", "lon", None),
        P("lat", "lon", None, None),
        P("lat", "lon", None),
        P("lat", "lon"),
        P("lat", "lon", None),
    )
    return jax.shard_map(
        shards, mesh=mesh, in_specs=placed, out_specs=P("lat", "lon", None, None), check_vma=False
    )
```

time: 76.3 us -> 71.1 us (0.932); the launches traced: 74.8 us -> 70.9 us
  starting transfers between devices: 32.9 us -> 18.7 us
  waiting for transfers between devices: 23.7 us -> 36 us
  Pallas kernels: 13.7 us -> 12.2 us
    ppermute x8, waiting for transfers between devices: 10.7 us -> 22 us  [ring(): return lax.ppermute(values, 'lon', [(i, target(i)) for i in range(blocks)])]
    ppermute x5, waiting for transfers between devices: 2.45 us -> 8.69 us  [trade(): return lax.ppermute(values, 'lon', [(i, i ^ mate) for i in range(blocks)])]
    ppermute x8, starting transfers between devices: 15.9 us -> 11.2 us  [ring(): return lax.ppermute(values, 'lon', [(i, target(i)) for i in range(blocks)])]
    ppermute x1, starting transfers between devices: 5.06 us -> 0.77 us  [shards(): high = lax.ppermute(halo, 'lon', west)]
    ppermute x1, waiting for transfers between devices: 6.43 us -> 3.86 us  [shards(): above = lax.ppermute(to_south, 'lat', south)]
    ppermute x1, waiting for transfers between devices: 4 us -> 1.45 us  [shards(): low = lax.ppermute(halo, 'lon', east)]
    ppermute x1, starting transfers between devices: 4.57 us -> 2.56 us  [shards(): below = lax.ppermute(to_north, 'lat', north)]
    ppermute x1, starting transfers between devices: 1.92 us -> 0.01 us  [shards(): above = lax.ppermute(to_south, 'lat', south)]
  transfers between devices with their start and end apart: 17 -> 17, of which waited for: 6 -> 11; matrix products, arithmetic and copies ran while one was open for 1% -> 1% of each run, Pallas kernels for 5% -> 8%
where the time goes in v6:
time: 71.1 us; the launch traced here: 70.9 us
  waiting for transfers between devices  36 us (51%)
  starting transfers between devices  18.7 us (26%)
  Pallas kernels  12.2 us (17%)
  local copies, waits for them, and re-layouts  2.95 us (4%)
    ppermute x8, waiting for transfers between devices, ring(): return lax.ppermute(values, 'lon', [(i, target(i)) for i in range(blocks)])  22 us
    ppermute x8, starting transfers between devices, ring(): return lax.ppermute(values, 'lon', [(i, target(i)) for i in range(blocks)])  11.2 us
    ppermute x5, waiting for transfers between devices, trade(): return lax.ppermute(values, 'lon', [(i, i ^ mate) for i in range(blocks)])  8.69 us
    pallas_call x1, Pallas kernels, shards(): call(final_body, shape((members, cells), F32), [VMEM] * 6, [pltpu.VMEM((m...  4.51 us
    ppermute x5, starting transfers between devices, trade(): return lax.ppermute(values, 'lon', [(i, i ^ mate) for i in range(blocks)])  4.11 us
    ppermute x1, waiting for transfers between devices, shards(): above = lax.ppermute(to_south, 'lat', south)  3.86 us
    unnamed x8, local copies, waits for them, and re-layouts  2.95 us
    ppermute x1, starting transfers between devices, shards(): below = lax.ppermute(to_north, 'lat', north)  2.56 us
  transfers between devices with their start and end apart: 17, of which 11 were waited for; matrix products, arithmetic and copies ran while one was open for 1% of the time, Pallas kernels for 8%

profile of v6, /device:TPU:24, one launch (start us, length us, event | category | flops | bytes accessed | tf_op | source)
XLA Modules:
  0.0 70.9 jit_solution(10366775322021428731)
XLA Ops:
  0.0 1.5 %collective-permute-start = (bf16[16,32,512]{2,1,0:T(8,128)(2,1)}, bf16[16,32,512]{2,1,0:T(8,128)(2,1)S(1)}, u32[]{:S(2)}, u32[]{:S(2)}) collective-permute-start(bf16[16,32,512]{2,1,0:T(8,128)(2,1)} %bitcast.11), channel_id=1, source_target_pairs={{0,2},{1,3},{2,0},{3,1},{4,6},{5,7},{6,4},{7,5},{8,10},{9,11},{10,... | collective-permute-start | bytes 1572872 | tf_op jit(solution)/shard_map/ppermute | solution.py:404
  2.0 0.7 pad_add_fusion.lists0_hbm
  2.7 1.5 %collective-permute-start.2 = (s32[3,16]{1,0:T(4,128)S(1)}, s32[3,16]{1,0:T(4,128)S(1)}, u32[]{:S(2)}, u32[]{:S(2)}) collective-permute-start(s32[3,16]{1,0:T(4,128)S(1)} %pad_add_fusion.lists0_hbm), channel_id=1, source_target_pairs={{0,2},{1,3},{2,0},{3,1},{4,6},{5,7},{6,4},{7,5},{8,10},{9,11},{10,... | collective-permute-start | bytes 584 | tf_op jit(solution)/shard_map/ppermute | solution.py:404
  4.2 1.6 %shard_map.82.halo_ref = bf16[144,512]{1,0:T(8,128)(2,1)} custom-call(bf16[128,512]{1,0:T(8,128)(2,1)} %bitcast.15, bf16[1,128]{1,0:T(2,128)(2,1)} %bitcast.17, s32[1,128]{1,0:T(1,128)} %bitcast.18), custom_call_target="tpu_custom_call" | custom-call | tf_op jit(solution)/shard_map/pallas_call | solution.py:406
  5.9 1.2 %copy-done = bf16[1,1,512,1024]{3,2,1,0:T(8,128)(2,1)S(1)} copy-done((bf16[1,1,512,1024]{3,2,1,0:T(8,128)(2,1)S(1)}, bf16[1,1,512,1024]{3,2,1,0:T(8,128)(2,1)}, u32[]{:S(2)}) %copy-start) | copy-done | bytes 1048600
  7.5 6.4 %collective-permute-done.pert1_ref = bf16[16,32,512]{2,1,0:T(8,128)(2,1)S(1)} collective-permute-done((bf16[16,32,512]{2,1,0:T(8,128)(2,1)}, bf16[16,32,512]{2,1,0:T(8,128)(2,1)S(1)}, u32[]{:S(2)}, u32[]{:S(2)}) %collective-permute-start) | collective-permute-done | bytes 524320 | tf_op jit(solution)/shard_map/ppermute | solution.py:404
  14.0 1.0 %copy-done.1 = bf16[1,16,32,512]{3,2,1,0:T(8,128)(2,1)S(1)} copy-done((bf16[1,16,32,512]{3,2,1,0:T(8,128)(2,1)S(1)}, bf16[1,16,32,512]{3,2,1,0:T(8,128)(2,1)}, u32[]{:S(2)}) %copy-start.1) | copy-done | bytes 524312
  15.7 1.8 %shard_map.84 = (bf16[1,528,128]{2,1,0:T(8,128)(2,1)S(1)}, bf16[7,528,128]{2,1,0:T(8,128)(2,1)S(1)}, bf16[1,528,128]{2,1,0:T(8,128)(2,1)S(1)}, bf16[7,528,128]{2,1,0:T(8,128)(2,1)S(1)}) custom-call(bf16[16,32,512]{2,1,0:T(8,128)(2,1)S(1)} %bitcast.12, bf16[16,32,512]{2,1,0:T(8,128)(2,1)S(1)} %collective-permute-done.pert1_ref, bf16[16,32]{1,0:T(8,128)(2,1)S(1)} %bitcast.14, ...), custom_call_target="tpu_custom_call" | custom-call | tf_op jit(solution)/shard_map/pallas_call | solution.py:422
  18.1 2.2 %collective-permute-done.4.mate_ref = bf16[1,528,128]{2,1,0:T(8,128)(2,1)S(1)} collective-permute-done((bf16[1,528,128]{2,1,0:T(8,128)(2,1)S(1)}, bf16[1,528,128]{2,1,0:T(8,128)(2,1)S(1)}, u32[]{:S(2)}, u32[]{:S(2)}) %collective-permute-start.4) | collective-permute-done | bytes 135200 | tf_op jit(solution)/shard_map/ppermute | solution.py:404
  20.6 5.9 %collective-permute-start.7 = (bf16[784,128]{1,0:T(8,128)(2,1)S(1)}, bf16[784,128]{1,0:T(8,128)(2,1)S(1)}, u32[]{:S(2)}, u32[]{:S(2)}) collective-permute-start(bf16[784,128]{1,0:T(8,128)(2,1)S(1)} %get-tuple-element.42), channel_id=1, source_target_pairs={{0,28},{1,5},{2,30},{3,7},{4,0},{5,9},{6,2},{7,11},{8,4},{9,13},{1... | collective-permute-start | bytes 602120 | tf_op jit(solution)/shard_map/ppermute | solution.py:401
  26.6 0.8 %collective-permute-start.9 = (bf16[144,512]{1,0:T(8,128)(2,1)S(1)}, bf16[144,512]{1,0:T(8,128)(2,1)S(1)}, u32[]{:S(2)}, u32[]{:S(2)}) collective-permute-start(bf16[144,512]{1,0:T(8,128)(2,1)S(1)} %copy-done.2), channel_id=1, source_target_pairs={{1,0},{2,1},{3,2},{4,3},{5,4},{6,5},{7,6},{8,7},{9,8},{10,9},{11,1... | collective-permute-start | bytes 442376 | tf_op jit(solution)/shard_map/ppermute | solution.py:437
  27.3 5.5 %collective-permute-done.5.came = bf16[256,128]{1,0:T(8,128)(2,1)S(1)} collective-permute-done((bf16[256,128]{1,0:T(8,128)(2,1)S(1)}, bf16[256,128]{1,0:T(8,128)(2,1)S(1)}, u32[]{:S(2)}, u32[]{:S(2)}) %collective-permute-start.5) | collective-permute-done | bytes 65568 | tf_op jit(solution)/shard_map/ppermute | solution.py:401
  33.3 1.5 %collective-permute-done.8.low_ref = bf16[144,512]{1,0:T(8,128)(2,1)S(1)} collective-permute-done((bf16[144,512]{1,0:T(8,128)(2,1)S(1)}, bf16[144,512]{1,0:T(8,128)(2,1)S(1)}, u32[]{:S(2)}, u32[]{:S(2)}) %collective-permute-start.8) | collective-permute-done | bytes 147488 | tf_op jit(solution)/shard_map/ppermute | solution.py:436
  35.1 1.9 %collective-permute-start.13 = (bf16[1040,128]{1,0:T(8,128)(2,1)S(1)}, bf16[1040,128]{1,0:T(8,128)(2,1)S(1)}, u32[]{:S(2)}, u32[]{:S(2)}) collective-permute-start(bf16[1040,128]{1,0:T(8,128)(2,1)S(1)} %shard_map.90), channel_id=1, source_target_pairs={{0,28},{1,5},{2,30},{3,7},{4,0},{5,9},{6,2},{7,11},{8,4},{9,13},{1... | collective-permute-start | bytes 798728 | tf_op jit(solution)/shard_map/ppermute | solution.py:401
  36.9 1.2 %shard_map.87 = (f32[512,512]{1,0:T(8,128)S(1)}, f32[1,512]{1,0:T(1,128)S(1)}, bf16[1040,128]{1,0:T(8,128)(2,1)S(1)}, bf16[1040,128]{1,0:T(8,128)(2,1)S(1)}) custom-call(bf16[144,512]{1,0:T(8,128)(2,1)S(1)} %collective-permute-done.8.low_ref, bf16[144,512]{1,0:T(8,128)(2,1)S(1)} %copy-done.2, bf16[144,512]{1,0:T(8,128)(2,1)S(1)} %collective-permute-done.9.high_ref), custom_call_target="tpu_custom_call" | custom-call | flops 603979776 | bytes 2097152 | tf_op jit(solution)/shard_map/pallas_call | solution.py:439
  38.1 4.9 %collective-permute-done.6.came = bf16[1040,128]{1,0:T(8,128)(2,1)S(1)} collective-permute-done((bf16[1040,128]{1,0:T(8,128)(2,1)S(1)}, bf16[1040,128]{1,0:T(8,128)(2,1)S(1)}, u32[]{:S(2)}, u32[]{:S(2)}) %collective-permute-start.6) | collective-permute-done | bytes 266272 | tf_op jit(solution)/shard_map/ppermute | solution.py:401
  43.4 2.6 %collective-permute-start.11 = (bf16[1040,128]{1,0:T(8,128)(2,1)S(1)}, bf16[1040,128]{1,0:T(8,128)(2,1)S(1)}, u32[]{:S(2)}, u32[]{:S(2)}) collective-permute-start(bf16[1040,128]{1,0:T(8,128)(2,1)S(1)} %get-tuple-element.50), channel_id=1, source_target_pairs={{0,32},{32,64},{64,96},{96,128},{128,160},{160,192},{192,224},{224... | collective-permute-start | bytes 798728 | tf_op jit(solution)/shard_map/ppermute | solution.py:464
  46.3 3.0 %collective-permute-start.14 = (bf16[1040,128]{1,0:T(8,128)(2,1)S(1)}, bf16[1040,128]{1,0:T(8,128)(2,1)S(1)}, u32[]{:S(2)}, u32[]{:S(2)}) collective-permute-start(bf16[1040,128]{1,0:T(8,128)(2,1)S(1)} %shard_map.91), channel_id=1, source_target_pairs={{0,28},{1,5},{2,30},{3,7},{4,0},{5,9},{6,2},{7,11},{8,4},{9,13},{1... | collective-permute-start | bytes 798728 | tf_op jit(solution)/shard_map/ppermute | solution.py:401
  49.4 4.3 %collective-permute-done.10.came = bf16[1040,128]{1,0:T(8,128)(2,1)S(1)} collective-permute-done((bf16[1040,128]{1,0:T(8,128)(2,1)S(1)}, bf16[1040,128]{1,0:T(8,128)(2,1)S(1)}, u32[]{:S(2)}, u32[]{:S(2)}) %collective-permute-start.10) | collective-permute-done | bytes 266272 | tf_op jit(solution)/shard_map/ppermute | solution.py:401
  54.1 1.5 %collective-permute-done.14.came = bf16[1040,128]{1,0:T(8,128)(2,1)S(1)} collective-permute-done((bf16[1040,128]{1,0:T(8,128)(2,1)S(1)}, bf16[1040,128]{1,0:T(8,128)(2,1)S(1)}, u32[]{:S(2)}, u32[]{:S(2)}) %collective-permute-start.14) | collective-permute-done | bytes 266272 | tf_op jit(solution)/shard_map/ppermute | solution.py:401
  55.5 3.9 %collective-permute-done.15.above_ref = bf16[1040,128]{1,0:T(8,128)(2,1)S(1)} collective-permute-done((bf16[1040,128]{1,0:T(8,128)(2,1)S(1)}, bf16[1040,128]{1,0:T(8,128)(2,1)S(1)}, u32[]{:S(2)}, u32[]{:S(2)}) %collective-permute-start.15) | collective-permute-done | bytes 266272 | tf_op jit(solution)/shard_map/ppermute | solution.py:465
  60.3 3.2 %collective-permute-done.12.up_ref = bf16[1040,128]{1,0:T(8,128)(2,1)S(1)} collective-permute-done((bf16[1040,128]{1,0:T(8,128)(2,1)S(1)}, bf16[1040,128]{1,0:T(8,128)(2,1)S(1)}, u32[]{:S(2)}, u32[]{:S(2)}) %collective-permute-start.12) | collective-permute-done | bytes 266272 | tf_op jit(solution)/shard_map/ppermute | solution.py:401
  63.5 2.7 %collective-permute-done.16.down_ref = bf16[1040,128]{1,0:T(8,128)(2,1)S(1)} collective-permute-done((bf16[1040,128]{1,0:T(8,128)(2,1)S(1)}, bf16[1040,128]{1,0:T(8,128)(2,1)S(1)}, u32[]{:S(2)}, u32[]{:S(2)}) %collective-permute-start.16) | collective-permute-done | bytes 266272 | tf_op jit(solution)/shard_map/ppermute | solution.py:401
  66.2 4.5 %shard_map.94 = f32[512,1024]{1,0:T(8,128)} custom-call(bf16[1040,128]{1,0:T(8,128)(2,1)S(1)} %collective-permute-done.12.up_ref, bf16[1040,128]{1,0:T(8,128)(2,1)S(1)} %collective-permute-done.16.down_ref, f32[512,512]{1,0:T(8,128)S(1)} %get-tuple-element.59.base_ref, f32[1,512]{1,0:T(1,128)S(1)} %get-tuple-element.60.drive_ref, ...), custom_call_target="tpu_custom_call" | custom-call | tf_op jit(solution)/shard_map/pallas_call | solution.py:486
  (32 shorter events, 5.5 us)
Async XLA Ops:
  0.0 13.9 %collective-permute-start = (bf16[16,32,512]{2,1,0:T(8,128)(2,1)}, bf16[16,32,512]{2,1,0:T(8,128)(2,1)S(1)}, u32[]{:S(2)}, u32[]{:S(2)}) collective-permute-start(bf16[16,32,512]{2,1,0:T(8,128)(2,1)} %bitcast.11), channel_id=1, source_target_pairs={{0,2},{1,3},{2,0},{3,1},{4,6},{5,7},{6,4},{7,5},{8,10},{9,11},{10,... | collective-permute-start | bytes 1572872 | tf_op jit(solution)/shard_map/ppermute | solution.py:404
  1.5 12.5 %collective-permute-start.1 = (bf16[16,32]{1,0:T(8,128)(2,1)}, bf16[16,32]{1,0:T(8,128)(2,1)S(1)}, u32[]{:S(2)}, u32[]{:S(2)}) collective-permute-start(bf16[16,32]{1,0:T(8,128)(2,1)} %bitcast.13), channel_id=1, source_target_pairs={{0,2},{1,3},{2,0},{3,1},{4,6},{5,7},{6,4},{7,5},{8,10},{9,11},{10,... | collective-permute-start | bytes 3080 | tf_op jit(solution)/shard_map/ppermute | solution.py:404
  2.7 11.3 %collective-permute-start.2 = (s32[3,16]{1,0:T(4,128)S(1)}, s32[3,16]{1,0:T(4,128)S(1)}, u32[]{:S(2)}, u32[]{:S(2)}) collective-permute-start(s32[3,16]{1,0:T(4,128)S(1)} %pad_add_fusion.lists0_hbm), channel_id=1, source_target_pairs={{0,2},{1,3},{2,0},{3,1},{4,6},{5,7},{6,4},{7,5},{8,10},{9,11},{10,... | collective-permute-start | bytes 584 | tf_op jit(solution)/shard_map/ppermute | solution.py:404
  5.9 1.2 %copy-start = (bf16[1,1,512,1024]{3,2,1,0:T(8,128)(2,1)S(1)}, bf16[1,1,512,1024]{3,2,1,0:T(8,128)(2,1)}, u32[]{:S(2)}) copy-start(bf16[1,1,512,1024]{3,2,1,0:T(8,128)(2,1)} %param.8) | copy-start | bytes 3145732
  7.1 19.5 %copy-start.2 = (bf16[144,512]{1,0:T(8,128)(2,1)S(1)}, bf16[144,512]{1,0:T(8,128)(2,1)}, u32[]{:S(2)}) copy-start(bf16[144,512]{1,0:T(8,128)(2,1)} %shard_map.82.halo_ref) | copy-start | bytes 442372
  14.0 1.0 %copy-start.1 = (bf16[1,16,32,512]{3,2,1,0:T(8,128)(2,1)S(1)}, bf16[1,16,32,512]{3,2,1,0:T(8,128)(2,1)}, u32[]{:S(2)}) copy-start(bf16[1,16,32,512]{3,2,1,0:T(8,128)(2,1)} %param.12) | copy-start | bytes 1572868
  15.1 0.7 copy-start.3
  17.5 15.3 %collective-permute-start.3 = (bf16[7,528,128]{2,1,0:T(8,128)(2,1)S(1)}, bf16[7,528,128]{2,1,0:T(8,128)(2,1)S(1)}, u32[]{:S(2)}, u32[]{:S(2)}) collective-permute-start(bf16[7,528,128]{2,1,0:T(8,128)(2,1)S(1)} %get-tuple-element.38), channel_id=1, source_target_pairs={{0,1},{1,0},{2,3},{3,2},{4,5},{5,4},{6,7},{7,6},{8,9},{9,8},{10,11... | collective-permute-start | bytes 2838536 | tf_op jit(solution)/shard_map/ppermute | solution.py:404
  17.6 2.7 %collective-permute-start.4 = (bf16[1,528,128]{2,1,0:T(8,128)(2,1)S(1)}, bf16[1,528,128]{2,1,0:T(8,128)(2,1)S(1)}, u32[]{:S(2)}, u32[]{:S(2)}) collective-permute-start(bf16[1,528,128]{2,1,0:T(8,128)(2,1)S(1)} %get-tuple-element.40), channel_id=1, source_target_pairs={{0,1},{1,0},{2,3},{3,2},{4,5},{5,4},{6,7},{7,6},{8,9},{9,8},{10,11... | collective-permute-start | bytes 405512 | tf_op jit(solution)/shard_map/ppermute | solution.py:404
  20.6 14.1 %collective-permute-start.7 = (bf16[784,128]{1,0:T(8,128)(2,1)S(1)}, bf16[784,128]{1,0:T(8,128)(2,1)S(1)}, u32[]{:S(2)}, u32[]{:S(2)}) collective-permute-start(bf16[784,128]{1,0:T(8,128)(2,1)S(1)} %get-tuple-element.42), channel_id=1, source_target_pairs={{0,28},{1,5},{2,30},{3,7},{4,0},{5,9},{6,2},{7,11},{8,4},{9,13},{1... | collective-permute-start | bytes 602120 | tf_op jit(solution)/shard_map/ppermute | solution.py:401
  26.6 6.7 %collective-permute-start.9 = (bf16[144,512]{1,0:T(8,128)(2,1)S(1)}, bf16[144,512]{1,0:T(8,128)(2,1)S(1)}, u32[]{:S(2)}, u32[]{:S(2)}) collective-permute-start(bf16[144,512]{1,0:T(8,128)(2,1)S(1)} %copy-done.2), channel_id=1, source_target_pairs={{1,0},{2,1},{3,2},{4,3},{5,4},{6,5},{7,6},{8,7},{9,8},{10,9},{11,1... | collective-permute-start | bytes 442376 | tf_op jit(solution)/shard_map/ppermute | solution.py:437
  27.3 7.4 %collective-permute-start.8 = (bf16[144,512]{1,0:T(8,128)(2,1)S(1)}, bf16[144,512]{1,0:T(8,128)(2,1)S(1)}, u32[]{:S(2)}, u32[]{:S(2)}) collective-permute-start(bf16[144,512]{1,0:T(8,128)(2,1)S(1)} %copy-done.2), channel_id=1, source_target_pairs={{0,1},{1,2},{2,3},{3,4},{4,5},{5,6},{6,7},{7,8},{8,9},{9,10},{10,1... | collective-permute-start | bytes 442376 | tf_op jit(solution)/shard_map/ppermute | solution.py:436
  27.3 5.5 %collective-permute-start.5 = (bf16[256,128]{1,0:T(8,128)(2,1)S(1)}, bf16[256,128]{1,0:T(8,128)(2,1)S(1)}, u32[]{:S(2)}, u32[]{:S(2)}) collective-permute-start(bf16[256,128]{1,0:T(8,128)(2,1)S(1)} %get-tuple-element.41), channel_id=1, source_target_pairs={{0,4},{1,29},{2,6},{3,31},{4,8},{5,1},{6,10},{7,3},{8,12},{9,5},{1... | collective-permute-start | bytes 196616 | tf_op jit(solution)/shard_map/ppermute | solution.py:401
  33.2 9.8 %collective-permute-start.6 = (bf16[1040,128]{1,0:T(8,128)(2,1)S(1)}, bf16[1040,128]{1,0:T(8,128)(2,1)S(1)}, u32[]{:S(2)}, u32[]{:S(2)}) collective-permute-start(bf16[1040,128]{1,0:T(8,128)(2,1)S(1)} %shard_map.86), channel_id=1, source_target_pairs={{0,4},{1,29},{2,6},{3,31},{4,8},{5,1},{6,10},{7,3},{8,12},{9,5},{1... | collective-permute-start | bytes 798728 | tf_op jit(solution)/shard_map/ppermute | solution.py:401
  35.1 10.9 %collective-permute-start.13 = (bf16[1040,128]{1,0:T(8,128)(2,1)S(1)}, bf16[1040,128]{1,0:T(8,128)(2,1)S(1)}, u32[]{:S(2)}, u32[]{:S(2)}) collective-permute-start(bf16[1040,128]{1,0:T(8,128)(2,1)S(1)} %shard_map.90), channel_id=1, source_target_pairs={{0,28},{1,5},{2,30},{3,7},{4,0},{5,9},{6,2},{7,11},{8,4},{9,13},{1... | collective-permute-start | bytes 798728 | tf_op jit(solution)/shard_map/ppermute | solution.py:401
  43.3 10.3 %collective-permute-start.10 = (bf16[1040,128]{1,0:T(8,128)(2,1)S(1)}, bf16[1040,128]{1,0:T(8,128)(2,1)S(1)}, u32[]{:S(2)}, u32[]{:S(2)}) collective-permute-start(bf16[1040,128]{1,0:T(8,128)(2,1)S(1)} %shard_map.88), channel_id=1, source_target_pairs={{0,4},{1,29},{2,6},{3,31},{4,8},{5,1},{6,10},{7,3},{8,12},{9,5},{1... | collective-permute-start | bytes 798728 | tf_op jit(solution)/shard_map/ppermute | solution.py:401
  43.4 10.2 %collective-permute-start.11 = (bf16[1040,128]{1,0:T(8,128)(2,1)S(1)}, bf16[1040,128]{1,0:T(8,128)(2,1)S(1)}, u32[]{:S(2)}, u32[]{:S(2)}) collective-permute-start(bf16[1040,128]{1,0:T(8,128)(2,1)S(1)} %get-tuple-element.50), channel_id=1, source_target_pairs={{0,32},{32,64},{64,96},{96,128},{128,160},{160,192},{192,224},{224... | collective-permute-start | bytes 798728 | tf_op jit(solution)/shard_map/ppermute | solution.py:464
  46.3 9.2 %collective-permute-start.14 = (bf16[1040,128]{1,0:T(8,128)(2,1)S(1)}, bf16[1040,128]{1,0:T(8,128)(2,1)S(1)}, u32[]{:S(2)}, u32[]{:S(2)}) collective-permute-start(bf16[1040,128]{1,0:T(8,128)(2,1)S(1)} %shard_map.91), channel_id=1, source_target_pairs={{0,28},{1,5},{2,30},{3,7},{4,0},{5,9},{6,2},{7,11},{8,4},{9,13},{1... | collective-permute-start | bytes 798728 | tf_op jit(solution)/shard_map/ppermute | solution.py:401
  49.4 10.0 %collective-permute-start.15 = (bf16[1040,128]{1,0:T(8,128)(2,1)S(1)}, bf16[1040,128]{1,0:T(8,128)(2,1)S(1)}, u32[]{:S(2)}, u32[]{:S(2)}) collective-permute-start(bf16[1040,128]{1,0:T(8,128)(2,1)S(1)} %get-tuple-element.53), channel_id=1, source_target_pairs={{32,0},{64,32},{96,64},{128,96},{160,128},{192,160},{224,192},{0,2... | collective-permute-start | bytes 798728 | tf_op jit(solution)/shard_map/ppermute | solution.py:465
  54.0 9.5 %collective-permute-start.12 = (bf16[1040,128]{1,0:T(8,128)(2,1)S(1)}, bf16[1040,128]{1,0:T(8,128)(2,1)S(1)}, u32[]{:S(2)}, u32[]{:S(2)}) collective-permute-start(bf16[1040,128]{1,0:T(8,128)(2,1)S(1)} %shard_map.89), channel_id=1, source_target_pairs={{0,4},{1,29},{2,6},{3,31},{4,8},{5,1},{6,10},{7,3},{8,12},{9,5},{1... | collective-permute-start | bytes 798728 | tf_op jit(solution)/shard_map/ppermute | solution.py:401
  59.7 6.5 %collective-permute-start.16 = (bf16[1040,128]{1,0:T(8,128)(2,1)S(1)}, bf16[1040,128]{1,0:T(8,128)(2,1)S(1)}, u32[]{:S(2)}, u32[]{:S(2)}) collective-permute-start(bf16[1040,128]{1,0:T(8,128)(2,1)S(1)} %shard_map.92), channel_id=1, source_target_pairs={{0,28},{1,5},{2,30},{3,7},{4,0},{5,9},{6,2},{7,11},{8,4},{9,13},{1... | collective-permute-start | bytes 798728 | tf_op jit(solution)/shard_map/ppermute | solution.py:401

commit v7 on v6

--- a/solution.py
+++ b/solution.py
@@ -41,7 +41,11 @@
     return jnp.dot(left, right, preferred_element_type=F32)
 
 
-def background_body(ensemble_ref, anomaly_ref, mean_ref):
+def background_body(
+    ensemble_ref, pert_ref, misfit_ref, anomaly_ref, mean_ref, kept_pert_ref, kept_misfit_ref
+):
+    kept_pert_ref[...] = pert_ref[...]
+    kept_misfit_ref[...] = misfit_ref[...]
     values = ensemble_ref[...].astype(F32)
     mean = jnp.mean(values, axis=0, keepdims=True)
     mean_ref[...] = mean
@@ -223,7 +227,7 @@
 def open_body(own_ref, mate_ref, up_ref, down_ref, rows_ref):
     drive = gather_rows(own_ref, 0, mate_ref, 0, rows_ref)
     blocks, total, diagonals, empty = packed(rows_ref, drive)
-    half = len(blocks) // 4
+    half = len(blocks) * 1 // 2
     for number, block in enumerate(blocks):
         ref, place = (up_ref, number) if number < half else (down_ref, number - half)
         ref[place * LANES : (place + 1) * LANES, :] = block.astype(BF16)
@@ -390,7 +394,7 @@
     packet = pieces * 4 * obs + PAD
     triangles = pieces * pieces // 2
     full = triangles * LANES + PAD
-    half = triangles // 4 * LANES
+    half = triangles * 1 // 2 * LANES
     message = shape((full, LANES), BF16)
 
     def ring(values, step):
@@ -414,9 +418,18 @@
     west = [(target, source) for source, target in east]
     lists = jnp.concatenate([jnp.swapaxes(sat_targets[0], 0, 1), sat_rows])
     pert1, misfit1, lists1 = trade(sat_pert[0], 2), trade(sat_misfit[0], 2), trade(lists, 2)
-    anomaly, mean = call(
-        background_body, (shape((members, cells), BF16), shape((1, cells), F32)), [VMEM], flops=4 * members * cells, moved=4 * members * cells
-    )(background[0, 0])
+    anomaly, mean, pert0, misfit0 = call(
+        background_body,
+        (
+            shape((members, cells), BF16),
+            shape((1, cells), F32),
+            shape((tiles, obs, members), BF16),
+            shape((tiles, obs), BF16),
+        ),
+        [VMEM] * 3,
+        flops=4 * members * cells,
+        moved=4 * members * cells,
+    )(background[0, 0], sat_pert[0], sat_misfit[0])
     halo, anomaly, mean, pert1 = lax.optimization_barrier((halo, anomaly, mean, pert1))
     counts = [high - low for low, high in CHUNKS]
     routed = call(
@@ -429,7 +442,7 @@
             pltpu.SMEM((2 * blocks,), jnp.int32),
             pltpu.SemaphoreType.DMA((2,)),
         ],
-    )(sat_pert[0], pert1, sat_misfit[0], misfit1, lists, lists1)
+    )(pert0, pert1, misfit0, misfit1, lists, lists1)
     own, sends = routed[: len(CHUNKS)], routed[len(CHUNKS) :]
     got = [trade(values, 1) for values in sends]
     halo, _ = lax.optimization_barrier((halo, routed[-1]))
@@ -464,15 +477,15 @@
             below = lax.ppermute(to_north, "lat", north)
             above = lax.ppermute(to_south, "lat", south)
         if step == 2:
-            first, below = lax.optimization_barrier((first, below))
-            second, above = lax.optimization_barrier((second, above))
+            second, below = lax.optimization_barrier((second, below))
         first = call(functools.partial(step_body, 2 * step, 0), message, [VMEM] * 3, scratch, flops=step_flops, moved=step_bytes)(
             own[1], got[1], first
         )
-        skip = triangles // 4 if step == 0 else 0
+        skip = triangles * 1 // 2 if step == 0 else 0
         second = call(functools.partial(step_body, 2 * step + 1, skip), message, [VMEM] * 3, scratch, flops=step_flops, moved=step_bytes)(
             own[1], got[1], second
         )
+    second, above = lax.optimization_barrier((second, above))
     first, second = ring(first, 1), ring(second, -1)
 
     base, drive = call(

time: 71.1 us -> 68.6 us (0.965)
  waiting for transfers between devices: 36 us -> 28.4 us
  starting transfers between devices: 18.7 us -> 23.8 us
    ppermute x1, starting transfers between devices: 0.77 us -> 6.49 us  [shards(): high = lax.ppermute(halo, 'lon', west)]
    ppermute x8, waiting for transfers between devices: 22 us -> 18 us  [ring(): return lax.ppermute(values, 'lon', [(i, target(i)) for i in range(blocks)])]
    ppermute x5, waiting for transfers between devices: 8.69 us -> 4.74 us  [trade(): return lax.ppermute(values, 'lon', [(i, i ^ mate) for i in range(blocks)])]
    ppermute x1, waiting for transfers between devices: 3.86 us -> 5.68 us  [shards(): above = lax.ppermute(to_south, 'lat', south)]
    ppermute x1, waiting for transfers between devices: 1.45 us -> 0.01 us  [shards(): low = lax.ppermute(halo, 'lon', east)]
  transfers between devices with their start and end apart: 17 -> 17, of which waited for: 11 -> 9; matrix products, arithmetic and copies ran while one was open for 1% -> 1% of each run, Pallas kernels for 8% -> 9%
where the time goes in v7:
time: 68.6 us; the launch traced here: 68.4 us
  waiting for transfers between devices  28.4 us (41%)
  starting transfers between devices  23.8 us (35%)
  Pallas kernels  12.3 us (18%)
  local copies, waits for them, and re-layouts  2.95 us (4%)
  other arithmetic  0.7 us (1%)
    ppermute x8, waiting for transfers between devices, ring(): return lax.ppermute(values, 'lon', [(i, target(i)) for i in range(blocks)])  18 us
    ppermute x8, starting transfers between devices, ring(): return lax.ppermute(values, 'lon', [(i, target(i)) for i in range(blocks)])  10.8 us
    ppermute x1, starting transfers between devices, shards(): high = lax.ppermute(halo, 'lon', west)  6.49 us
    ppermute x1, waiting for transfers between devices, shards(): above = lax.ppermute(to_south, 'lat', south)  5.68 us
    ppermute x5, waiting for transfers between devices, trade(): return lax.ppermute(values, 'lon', [(i, i ^ mate) for i in range(blocks)])  4.74 us
    pallas_call x1, Pallas kernels, shards(): call(final_body, shape((members, cells), F32), [VMEM] * 6, [pltpu.VMEM((m...  4.51 us
    ppermute x5, starting transfers between devices, trade(): return lax.ppermute(values, 'lon', [(i, i ^ mate) for i in range(blocks)])  4.11 us
    unnamed x8, local copies, waits for them, and re-layouts  2.95 us
  transfers between devices with their start and end apart: 17, of which 9 were waited for; matrix products, arithmetic and copies ran while one was open for 1% of the time, Pallas kernels for 9%

profile of v7, /device:TPU:24, one launch (start us, length us, event | category | flops | bytes accessed | tf_op | source)
XLA Modules:
  0.0 68.4 jit_solution(10798455925163590204)
XLA Ops:
  0.0 1.5 %collective-permute-start = (bf16[16,32,512]{2,1,0:T(8,128)(2,1)}, bf16[16,32,512]{2,1,0:T(8,128)(2,1)S(1)}, u32[]{:S(2)}, u32[]{:S(2)}) collective-permute-start(bf16[16,32,512]{2,1,0:T(8,128)(2,1)} %bitcast.11), channel_id=1, source_target_pairs={{0,2},{1,3},{2,0},{3,1},{4,6},{5,7},{6,4},{7,5},{8,10},{9,11},{10,... | collective-permute-start | bytes 1572872 | tf_op jit(solution)/shard_map/ppermute | solution.py:408
  1.5 0.5 collective-permute-start.1
  2.0 0.7 %pad_add_fusion.lists0_hbm = s32[3,16]{1,0:T(4,128)S(1)} fusion(s32[1,16]{1,0:T(1,128)} %param.14, s32[2,16]{1,0:T(2,128)} %bitcast.16), kind=kLoop, calls=%fused_computation | loop fusion | flops 48 | bytes 384 | tf_op jit(solution)/shard_map/concatenate | solution.py:419
  2.7 1.5 %collective-permute-start.2 = (s32[3,16]{1,0:T(4,128)S(1)}, s32[3,16]{1,0:T(4,128)S(1)}, u32[]{:S(2)}, u32[]{:S(2)}) collective-permute-start(s32[3,16]{1,0:T(4,128)S(1)} %pad_add_fusion.lists0_hbm), channel_id=1, source_target_pairs={{0,2},{1,3},{2,0},{3,1},{4,6},{5,7},{6,4},{7,5},{8,10},{9,11},{10,... | collective-permute-start | bytes 584 | tf_op jit(solution)/shard_map/ppermute | solution.py:408
  4.2 1.6 %shard_map.83.halo_ref = bf16[144,512]{1,0:T(8,128)(2,1)} custom-call(bf16[128,512]{1,0:T(8,128)(2,1)} %bitcast.15, bf16[1,128]{1,0:T(2,128)(2,1)} %bitcast.17, s32[1,128]{1,0:T(1,128)} %bitcast.18), custom_call_target="tpu_custom_call" | custom-call | tf_op jit(solution)/shard_map/pallas_call | solution.py:410
  5.9 1.2 %copy-done = bf16[1,1,512,1024]{3,2,1,0:T(8,128)(2,1)S(1)} copy-done((bf16[1,1,512,1024]{3,2,1,0:T(8,128)(2,1)S(1)}, bf16[1,1,512,1024]{3,2,1,0:T(8,128)(2,1)}, u32[]{:S(2)}) %copy-start) | copy-done | bytes 1048600
  7.1 1.0 %copy-done.1 = bf16[1,16,32,512]{3,2,1,0:T(8,128)(2,1)S(1)} copy-done((bf16[1,16,32,512]{3,2,1,0:T(8,128)(2,1)S(1)}, bf16[1,16,32,512]{3,2,1,0:T(8,128)(2,1)}, u32[]{:S(2)}) %copy-start.1) | copy-done | bytes 524312
  8.1 0.7 %copy-done.3 = bf16[1,16,32]{2,1,0:T(8,128)(2,1)S(1)} copy-done((bf16[1,16,32]{2,1,0:T(8,128)(2,1)S(1)}, bf16[1,16,32]{2,1,0:T(8,128)(2,1)}, u32[]{:S(2)}) %copy-start.3) | copy-done | bytes 1048
  9.3 4.7 %collective-permute-done.pert1_ref = bf16[16,32,512]{2,1,0:T(8,128)(2,1)S(1)} collective-permute-done((bf16[16,32,512]{2,1,0:T(8,128)(2,1)}, bf16[16,32,512]{2,1,0:T(8,128)(2,1)S(1)}, u32[]{:S(2)}, u32[]{:S(2)}) %collective-permute-start) | collective-permute-done | bytes 524320 | tf_op jit(solution)/shard_map/ppermute | solution.py:408
  14.0 1.8 %shard_map.84 = (bf16[1,528,128]{2,1,0:T(8,128)(2,1)S(1)}, bf16[7,528,128]{2,1,0:T(8,128)(2,1)S(1)}, bf16[1,528,128]{2,1,0:T(8,128)(2,1)S(1)}, bf16[7,528,128]{2,1,0:T(8,128)(2,1)S(1)}) custom-call(bf16[16,32,512]{2,1,0:T(8,128)(2,1)S(1)} %get-tuple-element.36.pert0_ref, bf16[16,32,512]{2,1,0:T(8,128)(2,1)S(1)} %collective-permute-done.pert1_ref, ...), custom_call_target="tpu_custom_call" | custom-call | tf_op jit(solution)/shard_map/pallas_call | solution.py:435
  16.4 6.5 %collective-permute-start.9 = (bf16[144,512]{1,0:T(8,128)(2,1)S(1)}, bf16[144,512]{1,0:T(8,128)(2,1)S(1)}, u32[]{:S(2)}, u32[]{:S(2)}) collective-permute-start(bf16[144,512]{1,0:T(8,128)(2,1)S(1)} %copy-done.2), channel_id=1, source_target_pairs={{1,0},{2,1},{3,2},{4,3},{5,4},{6,5},{7,6},{8,7},{9,8},{10,9},{11,1... | collective-permute-start | bytes 442376 | tf_op jit(solution)/shard_map/ppermute | solution.py:450
  23.3 3.2 %collective-permute-start.7 = (bf16[528,128]{1,0:T(8,128)(2,1)S(1)}, bf16[528,128]{1,0:T(8,128)(2,1)S(1)}, u32[]{:S(2)}, u32[]{:S(2)}) collective-permute-start(bf16[528,128]{1,0:T(8,128)(2,1)S(1)} %get-tuple-element.46), channel_id=1, source_target_pairs={{0,28},{1,5},{2,30},{3,7},{4,0},{5,9},{6,2},{7,11},{8,4},{9,13},{1... | collective-permute-start | bytes 405512 | tf_op jit(solution)/shard_map/ppermute | solution.py:405
  26.5 4.0 %collective-permute-done.5.came = bf16[512,128]{1,0:T(8,128)(2,1)S(1)} collective-permute-done((bf16[512,128]{1,0:T(8,128)(2,1)S(1)}, bf16[512,128]{1,0:T(8,128)(2,1)S(1)}, u32[]{:S(2)}, u32[]{:S(2)}) %collective-permute-start.5) | collective-permute-done | bytes 131104 | tf_op jit(solution)/shard_map/ppermute | solution.py:405
  31.3 3.3 %collective-permute-start.12 = (bf16[1040,128]{1,0:T(8,128)(2,1)S(1)}, bf16[1040,128]{1,0:T(8,128)(2,1)S(1)}, u32[]{:S(2)}, u32[]{:S(2)}) collective-permute-start(bf16[1040,128]{1,0:T(8,128)(2,1)S(1)} %shard_map.90), channel_id=1, source_target_pairs={{0,28},{1,5},{2,30},{3,7},{4,0},{5,9},{6,2},{7,11},{8,4},{9,13},{1... | collective-permute-start | bytes 798728 | tf_op jit(solution)/shard_map/ppermute | solution.py:405
  34.6 1.2 %shard_map.87 = (f32[512,512]{1,0:T(8,128)S(1)}, f32[1,512]{1,0:T(1,128)S(1)}, bf16[1040,128]{1,0:T(8,128)(2,1)S(1)}, bf16[1040,128]{1,0:T(8,128)(2,1)S(1)}) custom-call(bf16[144,512]{1,0:T(8,128)(2,1)S(1)} %collective-permute-done.8.low_ref, bf16[144,512]{1,0:T(8,128)(2,1)S(1)} %copy-done.2, bf16[144,512]{1,0:T(8,128)(2,1)S(1)} %collective-permute-done.9.high_ref), custom_call_target="tpu_custom_call" | custom-call | flops 603979776 | bytes 2097152 | tf_op jit(solution)/shard_map/pallas_call | solution.py:452
  35.8 4.8 %collective-permute-done.6.came = bf16[1040,128]{1,0:T(8,128)(2,1)S(1)} collective-permute-done((bf16[1040,128]{1,0:T(8,128)(2,1)S(1)}, bf16[1040,128]{1,0:T(8,128)(2,1)S(1)}, u32[]{:S(2)}, u32[]{:S(2)}) %collective-permute-start.6) | collective-permute-done | bytes 266272 | tf_op jit(solution)/shard_map/ppermute | solution.py:405
  41.6 3.3 %collective-permute-start.13 = (bf16[1040,128]{1,0:T(8,128)(2,1)S(1)}, bf16[1040,128]{1,0:T(8,128)(2,1)S(1)}, u32[]{:S(2)}, u32[]{:S(2)}) collective-permute-start(bf16[1040,128]{1,0:T(8,128)(2,1)S(1)} %shard_map.91), channel_id=1, source_target_pairs={{0,28},{1,5},{2,30},{3,7},{4,0},{5,9},{6,2},{7,11},{8,4},{9,13},{1... | collective-permute-start | bytes 798728 | tf_op jit(solution)/shard_map/ppermute | solution.py:405
  44.9 2.4 %collective-permute-start.14 = (bf16[1040,128]{1,0:T(8,128)(2,1)S(1)}, bf16[1040,128]{1,0:T(8,128)(2,1)S(1)}, u32[]{:S(2)}, u32[]{:S(2)}) collective-permute-start(bf16[1040,128]{1,0:T(8,128)(2,1)S(1)} %get-tuple-element.55), channel_id=1, source_target_pairs={{0,32},{32,64},{64,96},{96,128},{128,160},{160,192},{192,224},{224... | collective-permute-start | bytes 798728 | tf_op jit(solution)/shard_map/ppermute | solution.py:477
  47.3 2.7 %collective-permute-done.10.came = bf16[1040,128]{1,0:T(8,128)(2,1)S(1)} collective-permute-done((bf16[1040,128]{1,0:T(8,128)(2,1)S(1)}, bf16[1040,128]{1,0:T(8,128)(2,1)S(1)}, u32[]{:S(2)}, u32[]{:S(2)}) %collective-permute-start.10) | collective-permute-done | bytes 266272 | tf_op jit(solution)/shard_map/ppermute | solution.py:405
  50.4 0.9 %collective-permute-done.13.came = bf16[1040,128]{1,0:T(8,128)(2,1)S(1)} collective-permute-done((bf16[1040,128]{1,0:T(8,128)(2,1)S(1)}, bf16[1040,128]{1,0:T(8,128)(2,1)S(1)}, u32[]{:S(2)}, u32[]{:S(2)}) %collective-permute-start.13) | collective-permute-done | bytes 266272 | tf_op jit(solution)/shard_map/ppermute | solution.py:405
  51.7 5.7 %collective-permute-done.15.above_ref = bf16[1040,128]{1,0:T(8,128)(2,1)S(1)} collective-permute-done((bf16[1040,128]{1,0:T(8,128)(2,1)S(1)}, bf16[1040,128]{1,0:T(8,128)(2,1)S(1)}, u32[]{:S(2)}, u32[]{:S(2)}) %collective-permute-start.15) | collective-permute-done | bytes 266272 | tf_op jit(solution)/shard_map/ppermute | solution.py:478
  58.2 1.6 %collective-permute-done.11.up_ref = bf16[1040,128]{1,0:T(8,128)(2,1)S(1)} collective-permute-done((bf16[1040,128]{1,0:T(8,128)(2,1)S(1)}, bf16[1040,128]{1,0:T(8,128)(2,1)S(1)}, u32[]{:S(2)}, u32[]{:S(2)}) %collective-permute-start.11) | collective-permute-done | bytes 266272 | tf_op jit(solution)/shard_map/ppermute | solution.py:405
  59.8 4.0 %collective-permute-done.16.down_ref = bf16[1040,128]{1,0:T(8,128)(2,1)S(1)} collective-permute-done((bf16[1040,128]{1,0:T(8,128)(2,1)S(1)}, bf16[1040,128]{1,0:T(8,128)(2,1)S(1)}, u32[]{:S(2)}, u32[]{:S(2)}) %collective-permute-start.16) | collective-permute-done | bytes 266272 | tf_op jit(solution)/shard_map/ppermute | solution.py:405
  63.7 4.5 %shard_map.94 = f32[512,1024]{1,0:T(8,128)} custom-call(bf16[1040,128]{1,0:T(8,128)(2,1)S(1)} %collective-permute-done.11.up_ref, bf16[1040,128]{1,0:T(8,128)(2,1)S(1)} %collective-permute-done.16.down_ref, f32[512,512]{1,0:T(8,128)S(1)} %get-tuple-element.63.base_ref, f32[1,512]{1,0:T(1,128)S(1)} %get-tuple-element.64.drive_ref, ...), custom_call_target="tpu_custom_call" | custom-call | tf_op jit(solution)/shard_map/pallas_call | solution.py:499
  (32 shorter events, 4.9 us)
Async XLA Ops:
  0.0 13.9 %collective-permute-start = (bf16[16,32,512]{2,1,0:T(8,128)(2,1)}, bf16[16,32,512]{2,1,0:T(8,128)(2,1)S(1)}, u32[]{:S(2)}, u32[]{:S(2)}) collective-permute-start(bf16[16,32,512]{2,1,0:T(8,128)(2,1)} %bitcast.11), channel_id=1, source_target_pairs={{0,2},{1,3},{2,0},{3,1},{4,6},{5,7},{6,4},{7,5},{8,10},{9,11},{10,... | collective-permute-start | bytes 1572872 | tf_op jit(solution)/shard_map/ppermute | solution.py:408
  1.5 12.5 %collective-permute-start.1 = (bf16[16,32]{1,0:T(8,128)(2,1)}, bf16[16,32]{1,0:T(8,128)(2,1)S(1)}, u32[]{:S(2)}, u32[]{:S(2)}) collective-permute-start(bf16[16,32]{1,0:T(8,128)(2,1)} %bitcast.13), channel_id=1, source_target_pairs={{0,2},{1,3},{2,0},{3,1},{4,6},{5,7},{6,4},{7,5},{8,10},{9,11},{10,... | collective-permute-start | bytes 3080 | tf_op jit(solution)/shard_map/ppermute | solution.py:408
  2.7 11.3 %collective-permute-start.2 = (s32[3,16]{1,0:T(4,128)S(1)}, s32[3,16]{1,0:T(4,128)S(1)}, u32[]{:S(2)}, u32[]{:S(2)}) collective-permute-start(s32[3,16]{1,0:T(4,128)S(1)} %pad_add_fusion.lists0_hbm), channel_id=1, source_target_pairs={{0,2},{1,3},{2,0},{3,1},{4,6},{5,7},{6,4},{7,5},{8,10},{9,11},{10,... | collective-permute-start | bytes 584 | tf_op jit(solution)/shard_map/ppermute | solution.py:408
  5.9 1.2 %copy-start = (bf16[1,1,512,1024]{3,2,1,0:T(8,128)(2,1)S(1)}, bf16[1,1,512,1024]{3,2,1,0:T(8,128)(2,1)}, u32[]{:S(2)}) copy-start(bf16[1,1,512,1024]{3,2,1,0:T(8,128)(2,1)} %param.8) | copy-start | bytes 3145732
  7.1 1.0 %copy-start.1 = (bf16[1,16,32,512]{3,2,1,0:T(8,128)(2,1)S(1)}, bf16[1,16,32,512]{3,2,1,0:T(8,128)(2,1)}, u32[]{:S(2)}) copy-start(bf16[1,16,32,512]{3,2,1,0:T(8,128)(2,1)} %param.12) | copy-start | bytes 1572868
  8.1 0.7 %copy-start.3 = (bf16[1,16,32]{2,1,0:T(8,128)(2,1)S(1)}, bf16[1,16,32]{2,1,0:T(8,128)(2,1)}, u32[]{:S(2)}) copy-start(bf16[1,16,32]{2,1,0:T(8,128)(2,1)} %param.13) | copy-start | bytes 3076
  8.8 7.6 %copy-start.2 = (bf16[144,512]{1,0:T(8,128)(2,1)S(1)}, bf16[144,512]{1,0:T(8,128)(2,1)}, u32[]{:S(2)}) copy-start(bf16[144,512]{1,0:T(8,128)(2,1)} %shard_map.83.halo_ref) | copy-start | bytes 442372
  15.8 14.7 %collective-permute-start.3 = (bf16[7,528,128]{2,1,0:T(8,128)(2,1)S(1)}, bf16[7,528,128]{2,1,0:T(8,128)(2,1)S(1)}, u32[]{:S(2)}, u32[]{:S(2)}) collective-permute-start(bf16[7,528,128]{2,1,0:T(8,128)(2,1)S(1)} %get-tuple-element.42), channel_id=1, source_target_pairs={{0,1},{1,0},{2,3},{3,2},{4,5},{5,4},{6,7},{7,6},{8,9},{9,8},{10,11... | collective-permute-start | bytes 2838536 | tf_op jit(solution)/shard_map/ppermute | solution.py:408
  15.9 7.0 %collective-permute-start.4 = (bf16[1,528,128]{2,1,0:T(8,128)(2,1)S(1)}, bf16[1,528,128]{2,1,0:T(8,128)(2,1)S(1)}, u32[]{:S(2)}, u32[]{:S(2)}) collective-permute-start(bf16[1,528,128]{2,1,0:T(8,128)(2,1)S(1)} %get-tuple-element.44), channel_id=1, source_target_pairs={{0,1},{1,0},{2,3},{3,2},{4,5},{5,4},{6,7},{7,6},{8,9},{9,8},{10,11... | collective-permute-start | bytes 405512 | tf_op jit(solution)/shard_map/ppermute | solution.py:408
  16.4 14.6 %collective-permute-start.9 = (bf16[144,512]{1,0:T(8,128)(2,1)S(1)}, bf16[144,512]{1,0:T(8,128)(2,1)S(1)}, u32[]{:S(2)}, u32[]{:S(2)}) collective-permute-start(bf16[144,512]{1,0:T(8,128)(2,1)S(1)} %copy-done.2), channel_id=1, source_target_pairs={{1,0},{2,1},{3,2},{4,3},{5,4},{6,5},{7,6},{8,7},{9,8},{10,9},{11,1... | collective-permute-start | bytes 442376 | tf_op jit(solution)/shard_map/ppermute | solution.py:450
  22.9 8.1 %collective-permute-start.8 = (bf16[144,512]{1,0:T(8,128)(2,1)S(1)}, bf16[144,512]{1,0:T(8,128)(2,1)S(1)}, u32[]{:S(2)}, u32[]{:S(2)}) collective-permute-start(bf16[144,512]{1,0:T(8,128)(2,1)S(1)} %copy-done.2), channel_id=1, source_target_pairs={{0,1},{1,2},{2,3},{3,4},{4,5},{5,6},{6,7},{7,8},{8,9},{9,10},{10,1... | collective-permute-start | bytes 442376 | tf_op jit(solution)/shard_map/ppermute | solution.py:449
  23.2 7.3 %collective-permute-start.5 = (bf16[512,128]{1,0:T(8,128)(2,1)S(1)}, bf16[512,128]{1,0:T(8,128)(2,1)S(1)}, u32[]{:S(2)}, u32[]{:S(2)}) collective-permute-start(bf16[512,128]{1,0:T(8,128)(2,1)S(1)} %get-tuple-element.45), channel_id=1, source_target_pairs={{0,4},{1,29},{2,6},{3,31},{4,8},{5,1},{6,10},{7,3},{8,12},{9,5},{1... | collective-permute-start | bytes 393224 | tf_op jit(solution)/shard_map/ppermute | solution.py:405
  23.3 7.7 %collective-permute-start.7 = (bf16[528,128]{1,0:T(8,128)(2,1)S(1)}, bf16[528,128]{1,0:T(8,128)(2,1)S(1)}, u32[]{:S(2)}, u32[]{:S(2)}) collective-permute-start(bf16[528,128]{1,0:T(8,128)(2,1)S(1)} %get-tuple-element.46), channel_id=1, source_target_pairs={{0,28},{1,5},{2,30},{3,7},{4,0},{5,9},{6,2},{7,11},{8,4},{9,13},{1... | collective-permute-start | bytes 405512 | tf_op jit(solution)/shard_map/ppermute | solution.py:405
  30.8 9.8 %collective-permute-start.6 = (bf16[1040,128]{1,0:T(8,128)(2,1)S(1)}, bf16[1040,128]{1,0:T(8,128)(2,1)S(1)}, u32[]{:S(2)}, u32[]{:S(2)}) collective-permute-start(bf16[1040,128]{1,0:T(8,128)(2,1)S(1)} %shard_map.86), channel_id=1, source_target_pairs={{0,4},{1,29},{2,6},{3,31},{4,8},{5,1},{6,10},{7,3},{8,12},{9,5},{1... | collective-permute-start | bytes 798728 | tf_op jit(solution)/shard_map/ppermute | solution.py:405
  31.3 10.0 %collective-permute-start.12 = (bf16[1040,128]{1,0:T(8,128)(2,1)S(1)}, bf16[1040,128]{1,0:T(8,128)(2,1)S(1)}, u32[]{:S(2)}, u32[]{:S(2)}) collective-permute-start(bf16[1040,128]{1,0:T(8,128)(2,1)S(1)} %shard_map.90), channel_id=1, source_target_pairs={{0,28},{1,5},{2,30},{3,7},{4,0},{5,9},{6,2},{7,11},{8,4},{9,13},{1... | collective-permute-start | bytes 798728 | tf_op jit(solution)/shard_map/ppermute | solution.py:405
  41.0 9.0 %collective-permute-start.10 = (bf16[1040,128]{1,0:T(8,128)(2,1)S(1)}, bf16[1040,128]{1,0:T(8,128)(2,1)S(1)}, u32[]{:S(2)}, u32[]{:S(2)}) collective-permute-start(bf16[1040,128]{1,0:T(8,128)(2,1)S(1)} %shard_map.88), channel_id=1, source_target_pairs={{0,4},{1,29},{2,6},{3,31},{4,8},{5,1},{6,10},{7,3},{8,12},{9,5},{1... | collective-permute-start | bytes 798728 | tf_op jit(solution)/shard_map/ppermute | solution.py:405
  41.6 9.7 %collective-permute-start.13 = (bf16[1040,128]{1,0:T(8,128)(2,1)S(1)}, bf16[1040,128]{1,0:T(8,128)(2,1)S(1)}, u32[]{:S(2)}, u32[]{:S(2)}) collective-permute-start(bf16[1040,128]{1,0:T(8,128)(2,1)S(1)} %shard_map.91), channel_id=1, source_target_pairs={{0,28},{1,5},{2,30},{3,7},{4,0},{5,9},{6,2},{7,11},{8,4},{9,13},{1... | collective-permute-start | bytes 798728 | tf_op jit(solution)/shard_map/ppermute | solution.py:405
  44.9 6.4 %collective-permute-start.14 = (bf16[1040,128]{1,0:T(8,128)(2,1)S(1)}, bf16[1040,128]{1,0:T(8,128)(2,1)S(1)}, u32[]{:S(2)}, u32[]{:S(2)}) collective-permute-start(bf16[1040,128]{1,0:T(8,128)(2,1)S(1)} %get-tuple-element.55), channel_id=1, source_target_pairs={{0,32},{32,64},{64,96},{96,128},{128,160},{160,192},{192,224},{224... | collective-permute-start | bytes 798728 | tf_op jit(solution)/shard_map/ppermute | solution.py:477
  47.3 10.0 %collective-permute-start.15 = (bf16[1040,128]{1,0:T(8,128)(2,1)S(1)}, bf16[1040,128]{1,0:T(8,128)(2,1)S(1)}, u32[]{:S(2)}, u32[]{:S(2)}) collective-permute-start(bf16[1040,128]{1,0:T(8,128)(2,1)S(1)} %get-tuple-element.57), channel_id=1, source_target_pairs={{32,0},{64,32},{96,64},{128,96},{160,128},{192,160},{224,192},{0,2... | collective-permute-start | bytes 798728 | tf_op jit(solution)/shard_map/ppermute | solution.py:478
  50.3 9.5 %collective-permute-start.11 = (bf16[1040,128]{1,0:T(8,128)(2,1)S(1)}, bf16[1040,128]{1,0:T(8,128)(2,1)S(1)}, u32[]{:S(2)}, u32[]{:S(2)}) collective-permute-start(bf16[1040,128]{1,0:T(8,128)(2,1)S(1)} %shard_map.89), channel_id=1, source_target_pairs={{0,4},{1,29},{2,6},{3,31},{4,8},{5,1},{6,10},{7,3},{8,12},{9,5},{1... | collective-permute-start | bytes 798728 | tf_op jit(solution)/shard_map/ppermute | solution.py:405
  57.3 6.4 %collective-permute-start.16 = (bf16[1040,128]{1,0:T(8,128)(2,1)S(1)}, bf16[1040,128]{1,0:T(8,128)(2,1)S(1)}, u32[]{:S(2)}, u32[]{:S(2)}) collective-permute-start(bf16[1040,128]{1,0:T(8,128)(2,1)S(1)} %shard_map.92), channel_id=1, source_target_pairs={{0,28},{1,5},{2,30},{3,7},{4,0},{5,9},{6,2},{7,11},{8,4},{9,13},{1... | collective-permute-start | bytes 798728 | tf_op jit(solution)/shard_map/ppermute | solution.py:405

commit v8 on v7

--- a/solution.py
+++ b/solution.py
@@ -485,7 +485,6 @@
         second = call(functools.partial(step_body, 2 * step + 1, skip), message, [VMEM] * 3, scratch, flops=step_flops, moved=step_bytes)(
             own[1], got[1], second
         )
-    second, above = lax.optimization_barrier((second, above))
     first, second = ring(first, 1), ring(second, -1)
 
     base, drive = call(

time: 68.6 us -> 66.4 us (0.968)
  the two profiles are of different devices: /device:TPU:24 before, /device:TPU:4 now
where the time goes in v8:
time: 66.4 us; the launch traced here: 66.1 us
  starting transfers between devices  26.8 us (40%)
  waiting for transfers between devices  23.1 us (35%)
  Pallas kernels  12.3 us (19%)
  local copies, waits for them, and re-layouts  2.95 us (4%)
  other arithmetic  0.7 us (1%)
    ppermute x8, waiting for transfers between devices, ring(): return lax.ppermute(values, 'lon', [(i, target(i)) for i in range(blocks)])  14.1 us
    ppermute x8, starting transfers between devices, ring(): return lax.ppermute(values, 'lon', [(i, target(i)) for i in range(blocks)])  11.2 us
    ppermute x1, starting transfers between devices, shards(): high = lax.ppermute(halo, 'lon', west)  6.19 us
    ppermute x5, waiting for transfers between devices, trade(): return lax.ppermute(values, 'lon', [(i, i ^ mate) for i in range(blocks)])  5.01 us
    pallas_call x1, Pallas kernels, shards(): call(final_body, shape((members, cells), F32), [VMEM] * 6, [pltpu.VMEM((m...  4.5 us
    ppermute x1, starting transfers between devices, shards(): above = lax.ppermute(to_south, 'lat', south)  4.05 us
    ppermute x1, waiting for transfers between devices, shards(): below = lax.ppermute(to_north, 'lat', north)  3.94 us
    ppermute x5, starting transfers between devices, trade(): return lax.ppermute(values, 'lon', [(i, i ^ mate) for i in range(blocks)])  3.83 us
  transfers between devices with their start and end apart: 17, of which 7 were waited for; matrix products, arithmetic and copies ran while one was open for 1% of the time, Pallas kernels for 9%

profile of v8, /device:TPU:4, one launch (start us, length us, event | category | flops | bytes accessed | tf_op | source)
XLA Modules:
  0.0 66.1 jit_solution(13444203731249965722)
XLA Ops:
  0.0 1.2 %collective-permute-start = (bf16[16,32,512]{2,1,0:T(8,128)(2,1)}, bf16[16,32,512]{2,1,0:T(8,128)(2,1)S(1)}, u32[]{:S(2)}, u32[]{:S(2)}) collective-permute-start(bf16[16,32,512]{2,1,0:T(8,128)(2,1)} %bitcast.11), channel_id=1, source_target_pairs={{0,2},{1,3},{2,0},{3,1},{4,6},{5,7},{6,4},{7,5},{8,10},{9,11},{10,... | collective-permute-start | bytes 1572872 | tf_op jit(solution)/shard_map/ppermute | solution.py:408
  1.2 0.8 %collective-permute-start.1 = (bf16[16,32]{1,0:T(8,128)(2,1)}, bf16[16,32]{1,0:T(8,128)(2,1)S(1)}, u32[]{:S(2)}, u32[]{:S(2)}) collective-permute-start(bf16[16,32]{1,0:T(8,128)(2,1)} %bitcast.13), channel_id=1, source_target_pairs={{0,2},{1,3},{2,0},{3,1},{4,6},{5,7},{6,4},{7,5},{8,10},{9,11},{10,... | collective-permute-start | bytes 3080 | tf_op jit(solution)/shard_map/ppermute | solution.py:408
  2.0 0.7 %pad_add_fusion.lists0_hbm = s32[3,16]{1,0:T(4,128)S(1)} fusion(s32[1,16]{1,0:T(1,128)} %param.14, s32[2,16]{1,0:T(2,128)} %bitcast.16), kind=kLoop, calls=%fused_computation | loop fusion | flops 48 | bytes 384 | tf_op jit(solution)/shard_map/concatenate | solution.py:419
  2.7 1.2 %collective-permute-start.2 = (s32[3,16]{1,0:T(4,128)S(1)}, s32[3,16]{1,0:T(4,128)S(1)}, u32[]{:S(2)}, u32[]{:S(2)}) collective-permute-start(s32[3,16]{1,0:T(4,128)S(1)} %pad_add_fusion.lists0_hbm), channel_id=1, source_target_pairs={{0,2},{1,3},{2,0},{3,1},{4,6},{5,7},{6,4},{7,5},{8,10},{9,11},{10,... | collective-permute-start | bytes 584 | tf_op jit(solution)/shard_map/ppermute | solution.py:408
  4.0 1.6 %shard_map.83.halo_ref = bf16[144,512]{1,0:T(8,128)(2,1)} custom-call(bf16[128,512]{1,0:T(8,128)(2,1)} %bitcast.15, bf16[1,128]{1,0:T(2,128)(2,1)} %bitcast.17, s32[1,128]{1,0:T(1,128)} %bitcast.18), custom_call_target="tpu_custom_call" | custom-call | tf_op jit(solution)/shard_map/pallas_call | solution.py:410
  5.6 1.2 %copy-done = bf16[1,1,512,1024]{3,2,1,0:T(8,128)(2,1)S(1)} copy-done((bf16[1,1,512,1024]{3,2,1,0:T(8,128)(2,1)S(1)}, bf16[1,1,512,1024]{3,2,1,0:T(8,128)(2,1)}, u32[]{:S(2)}) %copy-start) | copy-done | bytes 1048600
  6.8 1.0 %copy-done.1 = bf16[1,16,32,512]{3,2,1,0:T(8,128)(2,1)S(1)} copy-done((bf16[1,16,32,512]{3,2,1,0:T(8,128)(2,1)S(1)}, bf16[1,16,32,512]{3,2,1,0:T(8,128)(2,1)}, u32[]{:S(2)}) %copy-start.1) | copy-done | bytes 524312
  7.9 0.7 %copy-done.3 = bf16[1,16,32]{2,1,0:T(8,128)(2,1)S(1)} copy-done((bf16[1,16,32]{2,1,0:T(8,128)(2,1)S(1)}, bf16[1,16,32]{2,1,0:T(8,128)(2,1)}, u32[]{:S(2)}) %copy-start.3) | copy-done | bytes 1048
  9.0 4.9 %collective-permute-done.pert1_ref = bf16[16,32,512]{2,1,0:T(8,128)(2,1)S(1)} collective-permute-done((bf16[16,32,512]{2,1,0:T(8,128)(2,1)}, bf16[16,32,512]{2,1,0:T(8,128)(2,1)S(1)}, u32[]{:S(2)}, u32[]{:S(2)}) %collective-permute-start) | collective-permute-done | bytes 524320 | tf_op jit(solution)/shard_map/ppermute | solution.py:408
  14.0 1.8 %shard_map.84 = (bf16[1,528,128]{2,1,0:T(8,128)(2,1)S(1)}, bf16[7,528,128]{2,1,0:T(8,128)(2,1)S(1)}, bf16[1,528,128]{2,1,0:T(8,128)(2,1)S(1)}, bf16[7,528,128]{2,1,0:T(8,128)(2,1)S(1)}) custom-call(bf16[16,32,512]{2,1,0:T(8,128)(2,1)S(1)} %get-tuple-element.34.pert0_ref, bf16[16,32,512]{2,1,0:T(8,128)(2,1)S(1)} %collective-permute-done.pert1_ref, ...), custom_call_target="tpu_custom_call" | custom-call | tf_op jit(solution)/shard_map/pallas_call | solution.py:435
  16.4 6.2 %collective-permute-start.9 = (bf16[144,512]{1,0:T(8,128)(2,1)S(1)}, bf16[144,512]{1,0:T(8,128)(2,1)S(1)}, u32[]{:S(2)}, u32[]{:S(2)}) collective-permute-start(bf16[144,512]{1,0:T(8,128)(2,1)S(1)} %copy-done.2), channel_id=1, source_target_pairs={{1,0},{2,1},{3,2},{4,3},{5,4},{6,5},{7,6},{8,7},{9,8},{10,9},{11,1... | collective-permute-start | bytes 442376 | tf_op jit(solution)/shard_map/ppermute | solution.py:450
  23.0 3.2 %collective-permute-start.7 = (bf16[528,128]{1,0:T(8,128)(2,1)S(1)}, bf16[528,128]{1,0:T(8,128)(2,1)S(1)}, u32[]{:S(2)}, u32[]{:S(2)}) collective-permute-start(bf16[528,128]{1,0:T(8,128)(2,1)S(1)} %get-tuple-element.44), channel_id=1, source_target_pairs={{0,28},{1,5},{2,30},{3,7},{4,0},{5,9},{6,2},{7,11},{8,4},{9,13},{1... | collective-permute-start | bytes 405512 | tf_op jit(solution)/shard_map/ppermute | solution.py:405
  26.2 3.6 %collective-permute-done.5.came = bf16[512,128]{1,0:T(8,128)(2,1)S(1)} collective-permute-done((bf16[512,128]{1,0:T(8,128)(2,1)S(1)}, bf16[512,128]{1,0:T(8,128)(2,1)S(1)}, u32[]{:S(2)}, u32[]{:S(2)}) %collective-permute-start.5) | collective-permute-done | bytes 131104 | tf_op jit(solution)/shard_map/ppermute | solution.py:405
  30.7 3.3 %collective-permute-start.12 = (bf16[1040,128]{1,0:T(8,128)(2,1)S(1)}, bf16[1040,128]{1,0:T(8,128)(2,1)S(1)}, u32[]{:S(2)}, u32[]{:S(2)}) collective-permute-start(bf16[1040,128]{1,0:T(8,128)(2,1)S(1)} %shard_map.90), channel_id=1, source_target_pairs={{0,28},{1,5},{2,30},{3,7},{4,0},{5,9},{6,2},{7,11},{8,4},{9,13},{1... | collective-permute-start | bytes 798728 | tf_op jit(solution)/shard_map/ppermute | solution.py:405
  34.0 1.2 %shard_map.87 = (f32[512,512]{1,0:T(8,128)S(1)}, f32[1,512]{1,0:T(1,128)S(1)}, bf16[1040,128]{1,0:T(8,128)(2,1)S(1)}, bf16[1040,128]{1,0:T(8,128)(2,1)S(1)}) custom-call(bf16[144,512]{1,0:T(8,128)(2,1)S(1)} %collective-permute-done.8.low_ref, bf16[144,512]{1,0:T(8,128)(2,1)S(1)} %copy-done.2, bf16[144,512]{1,0:T(8,128)(2,1)S(1)} %collective-permute-done.9.high_ref), custom_call_target="tpu_custom_call" | custom-call | flops 603979776 | bytes 2097152 | tf_op jit(solution)/shard_map/pallas_call | solution.py:452
  35.2 5.2 %collective-permute-done.6.came = bf16[1040,128]{1,0:T(8,128)(2,1)S(1)} collective-permute-done((bf16[1040,128]{1,0:T(8,128)(2,1)S(1)}, bf16[1040,128]{1,0:T(8,128)(2,1)S(1)}, u32[]{:S(2)}, u32[]{:S(2)}) %collective-permute-start.6) | collective-permute-done | bytes 266272 | tf_op jit(solution)/shard_map/ppermute | solution.py:405
  41.3 3.3 %collective-permute-start.13 = (bf16[1040,128]{1,0:T(8,128)(2,1)S(1)}, bf16[1040,128]{1,0:T(8,128)(2,1)S(1)}, u32[]{:S(2)}, u32[]{:S(2)}) collective-permute-start(bf16[1040,128]{1,0:T(8,128)(2,1)S(1)} %shard_map.91), channel_id=1, source_target_pairs={{0,28},{1,5},{2,30},{3,7},{4,0},{5,9},{6,2},{7,11},{8,4},{9,13},{1... | collective-permute-start | bytes 798728 | tf_op jit(solution)/shard_map/ppermute | solution.py:405
  44.6 1.6 %collective-permute-start.14 = (bf16[1040,128]{1,0:T(8,128)(2,1)S(1)}, bf16[1040,128]{1,0:T(8,128)(2,1)S(1)}, u32[]{:S(2)}, u32[]{:S(2)}) collective-permute-start(bf16[1040,128]{1,0:T(8,128)(2,1)S(1)} %get-tuple-element.53), channel_id=1, source_target_pairs={{0,32},{32,64},{64,96},{96,128},{128,160},{160,192},{192,224},{224... | collective-permute-start | bytes 798728 | tf_op jit(solution)/shard_map/ppermute | solution.py:477
  46.2 4.1 %collective-permute-start.16 = (bf16[1040,128]{1,0:T(8,128)(2,1)S(1)}, bf16[1040,128]{1,0:T(8,128)(2,1)S(1)}, u32[]{:S(2)}, u32[]{:S(2)}) collective-permute-start(bf16[1040,128]{1,0:T(8,128)(2,1)S(1)} %get-tuple-element.56), channel_id=1, source_target_pairs={{32,0},{64,32},{96,64},{128,96},{160,128},{192,160},{224,192},{0,2... | collective-permute-start | bytes 798728 | tf_op jit(solution)/shard_map/ppermute | solution.py:478
  50.7 3.9 %collective-permute-done.14.below_ref = bf16[1040,128]{1,0:T(8,128)(2,1)S(1)} collective-permute-done((bf16[1040,128]{1,0:T(8,128)(2,1)S(1)}, bf16[1040,128]{1,0:T(8,128)(2,1)S(1)}, u32[]{:S(2)}, u32[]{:S(2)}) %collective-permute-start.14) | collective-permute-done | bytes 266272 | tf_op jit(solution)/shard_map/ppermute | solution.py:477
  55.0 0.8 %collective-permute-start.15 = (bf16[1040,128]{1,0:T(8,128)(2,1)S(1)}, bf16[1040,128]{1,0:T(8,128)(2,1)S(1)}, u32[]{:S(2)}, u32[]{:S(2)}) collective-permute-start(bf16[1040,128]{1,0:T(8,128)(2,1)S(1)} %shard_map.92), channel_id=1, source_target_pairs={{0,28},{1,5},{2,30},{3,7},{4,0},{5,9},{6,2},{7,11},{8,4},{9,13},{1... | collective-permute-start | bytes 798728 | tf_op jit(solution)/shard_map/ppermute | solution.py:405
  56.2 4.0 %collective-permute-done.11.up_ref = bf16[1040,128]{1,0:T(8,128)(2,1)S(1)} collective-permute-done((bf16[1040,128]{1,0:T(8,128)(2,1)S(1)}, bf16[1040,128]{1,0:T(8,128)(2,1)S(1)}, u32[]{:S(2)}, u32[]{:S(2)}) %collective-permute-start.11) | collective-permute-done | bytes 266272 | tf_op jit(solution)/shard_map/ppermute | solution.py:405
  60.3 1.2 %collective-permute-done.15.down_ref = bf16[1040,128]{1,0:T(8,128)(2,1)S(1)} collective-permute-done((bf16[1040,128]{1,0:T(8,128)(2,1)S(1)}, bf16[1040,128]{1,0:T(8,128)(2,1)S(1)}, u32[]{:S(2)}, u32[]{:S(2)}) %collective-permute-start.15) | collective-permute-done | bytes 266272 | tf_op jit(solution)/shard_map/ppermute | solution.py:405
  61.5 4.5 %shard_map.94 = f32[512,1024]{1,0:T(8,128)} custom-call(bf16[1040,128]{1,0:T(8,128)(2,1)S(1)} %collective-permute-done.11.up_ref, bf16[1040,128]{1,0:T(8,128)(2,1)S(1)} %collective-permute-done.15.down_ref, f32[512,512]{1,0:T(8,128)S(1)} %get-tuple-element.59.base_ref, f32[1,512]{1,0:T(1,128)S(1)} %get-tuple-element.60.drive_ref, ...), custom_call_target="tpu_custom_call" | custom-call | tf_op jit(solution)/shard_map/pallas_call | solution.py:498
  (32 shorter events, 4.4 us)
Async XLA Ops:
  0.0 13.9 %collective-permute-start = (bf16[16,32,512]{2,1,0:T(8,128)(2,1)}, bf16[16,32,512]{2,1,0:T(8,128)(2,1)S(1)}, u32[]{:S(2)}, u32[]{:S(2)}) collective-permute-start(bf16[16,32,512]{2,1,0:T(8,128)(2,1)} %bitcast.11), channel_id=1, source_target_pairs={{0,2},{1,3},{2,0},{3,1},{4,6},{5,7},{6,4},{7,5},{8,10},{9,11},{10,... | collective-permute-start | bytes 1572872 | tf_op jit(solution)/shard_map/ppermute | solution.py:408
  1.2 12.8 %collective-permute-start.1 = (bf16[16,32]{1,0:T(8,128)(2,1)}, bf16[16,32]{1,0:T(8,128)(2,1)S(1)}, u32[]{:S(2)}, u32[]{:S(2)}) collective-permute-start(bf16[16,32]{1,0:T(8,128)(2,1)} %bitcast.13), channel_id=1, source_target_pairs={{0,2},{1,3},{2,0},{3,1},{4,6},{5,7},{6,4},{7,5},{8,10},{9,11},{10,... | collective-permute-start | bytes 3080 | tf_op jit(solution)/shard_map/ppermute | solution.py:408
  2.7 11.3 %collective-permute-start.2 = (s32[3,16]{1,0:T(4,128)S(1)}, s32[3,16]{1,0:T(4,128)S(1)}, u32[]{:S(2)}, u32[]{:S(2)}) collective-permute-start(s32[3,16]{1,0:T(4,128)S(1)} %pad_add_fusion.lists0_hbm), channel_id=1, source_target_pairs={{0,2},{1,3},{2,0},{3,1},{4,6},{5,7},{6,4},{7,5},{8,10},{9,11},{10,... | collective-permute-start | bytes 584 | tf_op jit(solution)/shard_map/ppermute | solution.py:408
  5.6 1.2 %copy-start = (bf16[1,1,512,1024]{3,2,1,0:T(8,128)(2,1)S(1)}, bf16[1,1,512,1024]{3,2,1,0:T(8,128)(2,1)}, u32[]{:S(2)}) copy-start(bf16[1,1,512,1024]{3,2,1,0:T(8,128)(2,1)} %param.8) | copy-start | bytes 3145732
  6.8 1.0 %copy-start.1 = (bf16[1,16,32,512]{3,2,1,0:T(8,128)(2,1)S(1)}, bf16[1,16,32,512]{3,2,1,0:T(8,128)(2,1)}, u32[]{:S(2)}) copy-start(bf16[1,16,32,512]{3,2,1,0:T(8,128)(2,1)} %param.12) | copy-start | bytes 1572868
  7.9 0.7 %copy-start.3 = (bf16[1,16,32]{2,1,0:T(8,128)(2,1)S(1)}, bf16[1,16,32]{2,1,0:T(8,128)(2,1)}, u32[]{:S(2)}) copy-start(bf16[1,16,32]{2,1,0:T(8,128)(2,1)} %param.13) | copy-start | bytes 3076
  8.5 7.8 %copy-start.2 = (bf16[144,512]{1,0:T(8,128)(2,1)S(1)}, bf16[144,512]{1,0:T(8,128)(2,1)}, u32[]{:S(2)}) copy-start(bf16[144,512]{1,0:T(8,128)(2,1)} %shard_map.83.halo_ref) | copy-start | bytes 442372
  15.8 14.1 %collective-permute-start.3 = (bf16[7,528,128]{2,1,0:T(8,128)(2,1)S(1)}, bf16[7,528,128]{2,1,0:T(8,128)(2,1)S(1)}, u32[]{:S(2)}, u32[]{:S(2)}) collective-permute-start(bf16[7,528,128]{2,1,0:T(8,128)(2,1)S(1)} %get-tuple-element.40), channel_id=1, source_target_pairs={{0,1},{1,0},{2,3},{3,2},{4,5},{5,4},{6,7},{7,6},{8,9},{9,8},{10,11... | collective-permute-start | bytes 2838536 | tf_op jit(solution)/shard_map/ppermute | solution.py:408
  15.9 6.7 %collective-permute-start.4 = (bf16[1,528,128]{2,1,0:T(8,128)(2,1)S(1)}, bf16[1,528,128]{2,1,0:T(8,128)(2,1)S(1)}, u32[]{:S(2)}, u32[]{:S(2)}) collective-permute-start(bf16[1,528,128]{2,1,0:T(8,128)(2,1)S(1)} %get-tuple-element.42), channel_id=1, source_target_pairs={{0,1},{1,0},{2,3},{3,2},{4,5},{5,4},{6,7},{7,6},{8,9},{9,8},{10,11... | collective-permute-start | bytes 405512 | tf_op jit(solution)/shard_map/ppermute | solution.py:408
  16.4 13.9 %collective-permute-start.9 = (bf16[144,512]{1,0:T(8,128)(2,1)S(1)}, bf16[144,512]{1,0:T(8,128)(2,1)S(1)}, u32[]{:S(2)}, u32[]{:S(2)}) collective-permute-start(bf16[144,512]{1,0:T(8,128)(2,1)S(1)} %copy-done.2), channel_id=1, source_target_pairs={{1,0},{2,1},{3,2},{4,3},{5,4},{6,5},{7,6},{8,7},{9,8},{10,9},{11,1... | collective-permute-start | bytes 442376 | tf_op jit(solution)/shard_map/ppermute | solution.py:450
  22.6 7.8 %collective-permute-start.8 = (bf16[144,512]{1,0:T(8,128)(2,1)S(1)}, bf16[144,512]{1,0:T(8,128)(2,1)S(1)}, u32[]{:S(2)}, u32[]{:S(2)}) collective-permute-start(bf16[144,512]{1,0:T(8,128)(2,1)S(1)} %copy-done.2), channel_id=1, source_target_pairs={{0,1},{1,2},{2,3},{3,4},{4,5},{5,6},{6,7},{7,8},{8,9},{9,10},{10,1... | collective-permute-start | bytes 442376 | tf_op jit(solution)/shard_map/ppermute | solution.py:449
  22.9 7.0 %collective-permute-start.5 = (bf16[512,128]{1,0:T(8,128)(2,1)S(1)}, bf16[512,128]{1,0:T(8,128)(2,1)S(1)}, u32[]{:S(2)}, u32[]{:S(2)}) collective-permute-start(bf16[512,128]{1,0:T(8,128)(2,1)S(1)} %get-tuple-element.43), channel_id=1, source_target_pairs={{0,4},{1,29},{2,6},{3,31},{4,8},{5,1},{6,10},{7,3},{8,12},{9,5},{1... | collective-permute-start | bytes 393224 | tf_op jit(solution)/shard_map/ppermute | solution.py:405
  23.0 7.3 %collective-permute-start.7 = (bf16[528,128]{1,0:T(8,128)(2,1)S(1)}, bf16[528,128]{1,0:T(8,128)(2,1)S(1)}, u32[]{:S(2)}, u32[]{:S(2)}) collective-permute-start(bf16[528,128]{1,0:T(8,128)(2,1)S(1)} %get-tuple-element.44), channel_id=1, source_target_pairs={{0,28},{1,5},{2,30},{3,7},{4,0},{5,9},{6,2},{7,11},{8,4},{9,13},{1... | collective-permute-start | bytes 405512 | tf_op jit(solution)/shard_map/ppermute | solution.py:405
  30.2 10.1 %collective-permute-start.6 = (bf16[1040,128]{1,0:T(8,128)(2,1)S(1)}, bf16[1040,128]{1,0:T(8,128)(2,1)S(1)}, u32[]{:S(2)}, u32[]{:S(2)}) collective-permute-start(bf16[1040,128]{1,0:T(8,128)(2,1)S(1)} %shard_map.86), channel_id=1, source_target_pairs={{0,4},{1,29},{2,6},{3,31},{4,8},{5,1},{6,10},{7,3},{8,12},{9,5},{1... | collective-permute-start | bytes 798728 | tf_op jit(solution)/shard_map/ppermute | solution.py:405
  30.7 10.3 %collective-permute-start.12 = (bf16[1040,128]{1,0:T(8,128)(2,1)S(1)}, bf16[1040,128]{1,0:T(8,128)(2,1)S(1)}, u32[]{:S(2)}, u32[]{:S(2)}) collective-permute-start(bf16[1040,128]{1,0:T(8,128)(2,1)S(1)} %shard_map.90), channel_id=1, source_target_pairs={{0,28},{1,5},{2,30},{3,7},{4,0},{5,9},{6,2},{7,11},{8,4},{9,13},{1... | collective-permute-start | bytes 798728 | tf_op jit(solution)/shard_map/ppermute | solution.py:405
  40.7 9.6 %collective-permute-start.10 = (bf16[1040,128]{1,0:T(8,128)(2,1)S(1)}, bf16[1040,128]{1,0:T(8,128)(2,1)S(1)}, u32[]{:S(2)}, u32[]{:S(2)}) collective-permute-start(bf16[1040,128]{1,0:T(8,128)(2,1)S(1)} %shard_map.88), channel_id=1, source_target_pairs={{0,4},{1,29},{2,6},{3,31},{4,8},{5,1},{6,10},{7,3},{8,12},{9,5},{1... | collective-permute-start | bytes 798728 | tf_op jit(solution)/shard_map/ppermute | solution.py:405
  41.3 9.4 %collective-permute-start.13 = (bf16[1040,128]{1,0:T(8,128)(2,1)S(1)}, bf16[1040,128]{1,0:T(8,128)(2,1)S(1)}, u32[]{:S(2)}, u32[]{:S(2)}) collective-permute-start(bf16[1040,128]{1,0:T(8,128)(2,1)S(1)} %shard_map.91), channel_id=1, source_target_pairs={{0,28},{1,5},{2,30},{3,7},{4,0},{5,9},{6,2},{7,11},{8,4},{9,13},{1... | collective-permute-start | bytes 798728 | tf_op jit(solution)/shard_map/ppermute | solution.py:405
  44.6 10.0 %collective-permute-start.14 = (bf16[1040,128]{1,0:T(8,128)(2,1)S(1)}, bf16[1040,128]{1,0:T(8,128)(2,1)S(1)}, u32[]{:S(2)}, u32[]{:S(2)}) collective-permute-start(bf16[1040,128]{1,0:T(8,128)(2,1)S(1)} %get-tuple-element.53), channel_id=1, source_target_pairs={{0,32},{32,64},{64,96},{96,128},{128,160},{160,192},{192,224},{224... | collective-permute-start | bytes 798728 | tf_op jit(solution)/shard_map/ppermute | solution.py:477
  46.2 9.6 %collective-permute-start.16 = (bf16[1040,128]{1,0:T(8,128)(2,1)S(1)}, bf16[1040,128]{1,0:T(8,128)(2,1)S(1)}, u32[]{:S(2)}, u32[]{:S(2)}) collective-permute-start(bf16[1040,128]{1,0:T(8,128)(2,1)S(1)} %get-tuple-element.56), channel_id=1, source_target_pairs={{32,0},{64,32},{96,64},{128,96},{160,128},{192,160},{224,192},{0,2... | collective-permute-start | bytes 798728 | tf_op jit(solution)/shard_map/ppermute | solution.py:478
  50.6 9.7 %collective-permute-start.11 = (bf16[1040,128]{1,0:T(8,128)(2,1)S(1)}, bf16[1040,128]{1,0:T(8,128)(2,1)S(1)}, u32[]{:S(2)}, u32[]{:S(2)}) collective-permute-start(bf16[1040,128]{1,0:T(8,128)(2,1)S(1)} %shard_map.89), channel_id=1, source_target_pairs={{0,4},{1,29},{2,6},{3,31},{4,8},{5,1},{6,10},{7,3},{8,12},{9,5},{1... | collective-permute-start | bytes 798728 | tf_op jit(solution)/shard_map/ppermute | solution.py:405
  55.0 6.5 %collective-permute-start.15 = (bf16[1040,128]{1,0:T(8,128)(2,1)S(1)}, bf16[1040,128]{1,0:T(8,128)(2,1)S(1)}, u32[]{:S(2)}, u32[]{:S(2)}) collective-permute-start(bf16[1040,128]{1,0:T(8,128)(2,1)S(1)} %shard_map.92), channel_id=1, source_target_pairs={{0,28},{1,5},{2,30},{3,7},{4,0},{5,9},{6,2},{7,11},{8,4},{9,13},{1... | collective-permute-start | bytes 798728 | tf_op jit(solution)/shard_map/ppermute | solution.py:405

commit v9 on v8

--- a/solution.py
+++ b/solution.py
@@ -227,7 +227,7 @@
 def open_body(own_ref, mate_ref, up_ref, down_ref, rows_ref):
     drive = gather_rows(own_ref, 0, mate_ref, 0, rows_ref)
     blocks, total, diagonals, empty = packed(rows_ref, drive)
-    half = len(blocks) * 1 // 2
+    half = len(blocks) * 5 // 8
     for number, block in enumerate(blocks):
         ref, place = (up_ref, number) if number < half else (down_ref, number - half)
         ref[place * LANES : (place + 1) * LANES, :] = block.astype(BF16)
@@ -313,7 +313,7 @@
     return (jnp.sqrt((members - 1.0) * inverse_scale) * inverse_root + weight).astype(BF16)
 
 
-def unpack_into(gram_ref, arrived, factors):
+def unpack_into(gram_ref, base_ref, arrived, factors):
     pieces = gram_ref.shape[0] // LANES
     total, diagonals = 0.0, 0.0
     for ref, factor in zip(arrived, factors):
@@ -323,7 +323,7 @@
 
     def add(part, other, block):
         place = (slice(part * LANES, (part + 1) * LANES), slice(other * LANES, (other + 1) * LANES))
-        gram_ref[place] = gram_ref[place] + block
+        gram_ref[place] = base_ref[place] + block
 
     def block_of(number):
         place = slice(number * LANES, (number + 1) * LANES)
@@ -360,15 +360,14 @@
     band = lax.axis_index("lat")
     from_below = jnp.where(band > 0, 1.0, 0.0).astype(F32)
     from_above = jnp.where(band < lax.axis_size("lat") - 1, 1.0, 0.0).astype(F32)
-    total = unpack_into(gram_ref, (below_ref, above_ref), (from_below, from_above))
+    total = unpack_into(gram_ref, gram_ref, (below_ref, above_ref), (from_below, from_above))
     own = drive[0:pieces] + drive[pieces : 2 * pieces]
     own = jnp.concatenate([own[part : part + 1] for part in range(pieces)], axis=1)
     drive_ref[...] = conv_drive_ref[...] + total + own
 
 
 def final_body(up_ref, down_ref, base_ref, drive_ref, mean_ref, anomaly_ref, out_hbm, gram_ref, out_ref, sems):
-    gram_ref[...] = base_ref[...]
-    drive = drive_ref[...] + unpack_into(gram_ref, (up_ref, down_ref), (1.0, 1.0))
+    drive = drive_ref[...] + unpack_into(gram_ref, base_ref, (up_ref, down_ref), (1.0, 1.0))
     transform = root(gram_ref[...], drive)
     members = gram_ref.shape[0]
     copies = []
@@ -394,7 +393,7 @@
     packet = pieces * 4 * obs + PAD
     triangles = pieces * pieces // 2
     full = triangles * LANES + PAD
-    half = triangles * 1 // 2 * LANES
+    half = triangles * 5 // 8 * LANES
     message = shape((full, LANES), BF16)
 
     def ring(values, step):
@@ -481,7 +480,7 @@
         first = call(functools.partial(step_body, 2 * step, 0), message, [VMEM] * 3, scratch, flops=step_flops, moved=step_bytes)(
             own[1], got[1], first
         )
-        skip = triangles * 1 // 2 if step == 0 else 0
+        skip = triangles * 5 // 8 if step == 0 else 0
         second = call(functools.partial(step_body, 2 * step + 1, skip), message, [VMEM] * 3, scratch, flops=step_flops, moved=step_bytes)(
             own[1], got[1], second
         )

time: 66.4 us -> 65.9 us (level)
  the two profiles are of different devices: /device:TPU:4 before, /device:TPU:98 now
where the time goes in v9:
time: 65.9 us; the launch traced here: 65.7 us
  waiting for transfers between devices  25.6 us (39%)
  starting transfers between devices  23.9 us (36%)
  Pallas kernels  12.3 us (19%)
  local copies, waits for them, and re-layouts  2.95 us (4%)
  other arithmetic  0.7 us (1%)
    ppermute x8, waiting for transfers between devices, ring(): return lax.ppermute(values, 'lon', [(i, target(i)) for i in range(blocks)])  16 us
    ppermute x8, starting transfers between devices, ring(): return lax.ppermute(values, 'lon', [(i, target(i)) for i in range(blocks)])  14.5 us
    ppermute x5, waiting for transfers between devices, trade(): return lax.ppermute(values, 'lon', [(i, i ^ mate) for i in range(blocks)])  7.89 us
    pallas_call x1, Pallas kernels, shards(): call(final_body, shape((members, cells), F32), [VMEM] * 6, [pltpu.VMEM((m...  4.51 us
    ppermute x1, starting transfers between devices, shards(): above = lax.ppermute(to_south, 'lat', south)  4.06 us
    ppermute x5, starting transfers between devices, trade(): return lax.ppermute(values, 'lon', [(i, i ^ mate) for i in range(blocks)])  3.15 us
    unnamed x8, local copies, waits for them, and re-layouts  2.95 us
    pallas_call x1, Pallas kernels, shards(): call(route_body, tuple((shape((count, packet, LANES), BF16) for count in...  1.76 us
  transfers between devices with their start and end apart: 17, of which 8 were waited for; matrix products, arithmetic and copies ran while one was open for 1% of the time, Pallas kernels for 9%

profile of v9, /device:TPU:98, one launch (start us, length us, event | category | flops | bytes accessed | tf_op | source)
XLA Modules:
  0.0 65.7 jit_solution(7521445315770589108)
XLA Ops:
  0.0 0.5 collective-permute-start
  0.5 1.5 %collective-permute-start.1 = (bf16[16,32]{1,0:T(8,128)(2,1)}, bf16[16,32]{1,0:T(8,128)(2,1)S(1)}, u32[]{:S(2)}, u32[]{:S(2)}) collective-permute-start(bf16[16,32]{1,0:T(8,128)(2,1)} %bitcast.13), channel_id=1, source_target_pairs={{0,2},{1,3},{2,0},{3,1},{4,6},{5,7},{6,4},{7,5},{8,10},{9,11},{10,... | collective-permute-start | bytes 3080 | tf_op jit(solution)/shard_map/ppermute | solution.py:407
  2.0 0.7 %pad_add_fusion.lists0_hbm = s32[3,16]{1,0:T(4,128)S(1)} fusion(s32[1,16]{1,0:T(1,128)} %param.14, s32[2,16]{1,0:T(2,128)} %bitcast.16), kind=kLoop, calls=%fused_computation | loop fusion | flops 48 | bytes 384 | tf_op jit(solution)/shard_map/concatenate | solution.py:418
  2.7 0.5 collective-permute-start.2
  3.3 1.6 %shard_map.83.halo_ref = bf16[144,512]{1,0:T(8,128)(2,1)} custom-call(bf16[128,512]{1,0:T(8,128)(2,1)} %bitcast.15, bf16[1,128]{1,0:T(2,128)(2,1)} %bitcast.17, s32[1,128]{1,0:T(1,128)} %bitcast.18), custom_call_target="tpu_custom_call" | custom-call | tf_op jit(solution)/shard_map/pallas_call | solution.py:409
  4.9 1.2 %copy-done = bf16[1,1,512,1024]{3,2,1,0:T(8,128)(2,1)S(1)} copy-done((bf16[1,1,512,1024]{3,2,1,0:T(8,128)(2,1)S(1)}, bf16[1,1,512,1024]{3,2,1,0:T(8,128)(2,1)}, u32[]{:S(2)}) %copy-start) | copy-done | bytes 1048600
  6.1 1.0 %copy-done.1 = bf16[1,16,32,512]{3,2,1,0:T(8,128)(2,1)S(1)} copy-done((bf16[1,16,32,512]{3,2,1,0:T(8,128)(2,1)S(1)}, bf16[1,16,32,512]{3,2,1,0:T(8,128)(2,1)}, u32[]{:S(2)}) %copy-start.1) | copy-done | bytes 524312
  7.2 0.7 %copy-done.3 = bf16[1,16,32]{2,1,0:T(8,128)(2,1)S(1)} copy-done((bf16[1,16,32]{2,1,0:T(8,128)(2,1)S(1)}, bf16[1,16,32]{2,1,0:T(8,128)(2,1)}, u32[]{:S(2)}) %copy-start.3) | copy-done | bytes 1048
  8.3 5.6 %collective-permute-done.pert1_ref = bf16[16,32,512]{2,1,0:T(8,128)(2,1)S(1)} collective-permute-done((bf16[16,32,512]{2,1,0:T(8,128)(2,1)}, bf16[16,32,512]{2,1,0:T(8,128)(2,1)S(1)}, u32[]{:S(2)}, u32[]{:S(2)}) %collective-permute-start) | collective-permute-done | bytes 524320 | tf_op jit(solution)/shard_map/ppermute | solution.py:407
  14.0 1.8 %shard_map.84 = (bf16[1,528,128]{2,1,0:T(8,128)(2,1)S(1)}, bf16[7,528,128]{2,1,0:T(8,128)(2,1)S(1)}, bf16[1,528,128]{2,1,0:T(8,128)(2,1)S(1)}, bf16[7,528,128]{2,1,0:T(8,128)(2,1)S(1)}) custom-call(bf16[16,32,512]{2,1,0:T(8,128)(2,1)S(1)} %get-tuple-element.34.pert0_ref, bf16[16,32,512]{2,1,0:T(8,128)(2,1)S(1)} %collective-permute-done.pert1_ref, ...), custom_call_target="tpu_custom_call" | custom-call | tf_op jit(solution)/shard_map/pallas_call | solution.py:434
  16.4 2.2 %collective-permute-done.4.mate_ref = bf16[1,528,128]{2,1,0:T(8,128)(2,1)S(1)} collective-permute-done((bf16[1,528,128]{2,1,0:T(8,128)(2,1)S(1)}, bf16[1,528,128]{2,1,0:T(8,128)(2,1)S(1)}, u32[]{:S(2)}, u32[]{:S(2)}) %collective-permute-start.4) | collective-permute-done | bytes 135200 | tf_op jit(solution)/shard_map/ppermute | solution.py:407
  18.9 3.2 %collective-permute-start.5 = (bf16[640,128]{1,0:T(8,128)(2,1)S(1)}, bf16[640,128]{1,0:T(8,128)(2,1)S(1)}, u32[]{:S(2)}, u32[]{:S(2)}) collective-permute-start(bf16[640,128]{1,0:T(8,128)(2,1)S(1)} %get-tuple-element.43), channel_id=1, source_target_pairs={{0,4},{1,29},{2,6},{3,31},{4,8},{5,1},{6,10},{7,3},{8,12},{9,5},{1... | collective-permute-start | bytes 491528 | tf_op jit(solution)/shard_map/ppermute | solution.py:404
  22.6 3.7 %collective-permute-done.5.came = bf16[640,128]{1,0:T(8,128)(2,1)S(1)} collective-permute-done((bf16[640,128]{1,0:T(8,128)(2,1)S(1)}, bf16[640,128]{1,0:T(8,128)(2,1)S(1)}, u32[]{:S(2)}, u32[]{:S(2)}) %collective-permute-start.5) | collective-permute-done | bytes 163872 | tf_op jit(solution)/shard_map/ppermute | solution.py:404
  26.7 3.8 %collective-permute-start.6 = (bf16[1040,128]{1,0:T(8,128)(2,1)S(1)}, bf16[1040,128]{1,0:T(8,128)(2,1)S(1)}, u32[]{:S(2)}, u32[]{:S(2)}) collective-permute-start(bf16[1040,128]{1,0:T(8,128)(2,1)S(1)} %shard_map.86), channel_id=1, source_target_pairs={{0,4},{1,29},{2,6},{3,31},{4,8},{5,1},{6,10},{7,3},{8,12},{9,5},{1... | collective-permute-start | bytes 798728 | tf_op jit(solution)/shard_map/ppermute | solution.py:404
  30.9 1.2 %shard_map.87 = (f32[512,512]{1,0:T(8,128)S(1)}, f32[1,512]{1,0:T(1,128)S(1)}, bf16[1040,128]{1,0:T(8,128)(2,1)S(1)}, bf16[1040,128]{1,0:T(8,128)(2,1)S(1)}) custom-call(bf16[144,512]{1,0:T(8,128)(2,1)S(1)} %collective-permute-done.8.low_ref, bf16[144,512]{1,0:T(8,128)(2,1)S(1)} %copy-done.2, bf16[144,512]{1,0:T(8,128)(2,1)S(1)} %collective-permute-done.9.high_ref), custom_call_target="tpu_custom_call" | custom-call | flops 603979776 | bytes 2097152 | tf_op jit(solution)/shard_map/pallas_call | solution.py:451
  32.1 5.0 %collective-permute-done.6.came = bf16[1040,128]{1,0:T(8,128)(2,1)S(1)} collective-permute-done((bf16[1040,128]{1,0:T(8,128)(2,1)S(1)}, bf16[1040,128]{1,0:T(8,128)(2,1)S(1)}, u32[]{:S(2)}, u32[]{:S(2)}) %collective-permute-start.6) | collective-permute-done | bytes 266272 | tf_op jit(solution)/shard_map/ppermute | solution.py:404
  37.5 3.9 %collective-permute-start.10 = (bf16[1040,128]{1,0:T(8,128)(2,1)S(1)}, bf16[1040,128]{1,0:T(8,128)(2,1)S(1)}, u32[]{:S(2)}, u32[]{:S(2)}) collective-permute-start(bf16[1040,128]{1,0:T(8,128)(2,1)S(1)} %shard_map.88), channel_id=1, source_target_pairs={{0,4},{1,29},{2,6},{3,31},{4,8},{5,1},{6,10},{7,3},{8,12},{9,5},{1... | collective-permute-start | bytes 798728 | tf_op jit(solution)/shard_map/ppermute | solution.py:404
  41.9 1.7 %collective-permute-start.14 = (bf16[1040,128]{1,0:T(8,128)(2,1)S(1)}, bf16[1040,128]{1,0:T(8,128)(2,1)S(1)}, u32[]{:S(2)}, u32[]{:S(2)}) collective-permute-start(bf16[1040,128]{1,0:T(8,128)(2,1)S(1)} %get-tuple-element.53), channel_id=1, source_target_pairs={{0,32},{32,64},{64,96},{96,128},{128,160},{160,192},{192,224},{224... | collective-permute-start | bytes 798728 | tf_op jit(solution)/shard_map/ppermute | solution.py:476
  43.5 4.1 %collective-permute-start.16 = (bf16[1040,128]{1,0:T(8,128)(2,1)S(1)}, bf16[1040,128]{1,0:T(8,128)(2,1)S(1)}, u32[]{:S(2)}, u32[]{:S(2)}) collective-permute-start(bf16[1040,128]{1,0:T(8,128)(2,1)S(1)} %get-tuple-element.56), channel_id=1, source_target_pairs={{32,0},{64,32},{96,64},{128,96},{160,128},{192,160},{224,192},{0,2... | collective-permute-start | bytes 798728 | tf_op jit(solution)/shard_map/ppermute | solution.py:477
  47.9 3.4 %collective-permute-start.11 = (bf16[1040,128]{1,0:T(8,128)(2,1)S(1)}, bf16[1040,128]{1,0:T(8,128)(2,1)S(1)}, u32[]{:S(2)}, u32[]{:S(2)}) collective-permute-start(bf16[1040,128]{1,0:T(8,128)(2,1)S(1)} %shard_map.89), channel_id=1, source_target_pairs={{0,4},{1,29},{2,6},{3,31},{4,8},{5,1},{6,10},{7,3},{8,12},{9,5},{1... | collective-permute-start | bytes 798728 | tf_op jit(solution)/shard_map/ppermute | solution.py:404
  51.3 1.7 %collective-permute-done.14.below_ref = bf16[1040,128]{1,0:T(8,128)(2,1)S(1)} collective-permute-done((bf16[1040,128]{1,0:T(8,128)(2,1)S(1)}, bf16[1040,128]{1,0:T(8,128)(2,1)S(1)}, u32[]{:S(2)}, u32[]{:S(2)}) %collective-permute-start.14) | collective-permute-done | bytes 266272 | tf_op jit(solution)/shard_map/ppermute | solution.py:476
  53.8 3.9 %collective-permute-done.11.up_ref = bf16[1040,128]{1,0:T(8,128)(2,1)S(1)} collective-permute-done((bf16[1040,128]{1,0:T(8,128)(2,1)S(1)}, bf16[1040,128]{1,0:T(8,128)(2,1)S(1)}, u32[]{:S(2)}, u32[]{:S(2)}) %collective-permute-start.11) | collective-permute-done | bytes 266272 | tf_op jit(solution)/shard_map/ppermute | solution.py:404
  57.8 3.3 %collective-permute-done.15.down_ref = bf16[1040,128]{1,0:T(8,128)(2,1)S(1)} collective-permute-done((bf16[1040,128]{1,0:T(8,128)(2,1)S(1)}, bf16[1040,128]{1,0:T(8,128)(2,1)S(1)}, u32[]{:S(2)}, u32[]{:S(2)}) %collective-permute-start.15) | collective-permute-done | bytes 266272 | tf_op jit(solution)/shard_map/ppermute | solution.py:404
  61.0 4.5 %shard_map.94 = f32[512,1024]{1,0:T(8,128)} custom-call(bf16[1040,128]{1,0:T(8,128)(2,1)S(1)} %collective-permute-done.11.up_ref, bf16[1040,128]{1,0:T(8,128)(2,1)S(1)} %collective-permute-done.15.down_ref, f32[512,512]{1,0:T(8,128)S(1)} %get-tuple-element.59.base_ref, f32[1,512]{1,0:T(1,128)S(1)} %get-tuple-element.60.drive_ref, ...), custom_call_target="tpu_custom_call" | custom-call | tf_op jit(solution)/shard_map/pallas_call | solution.py:497
  (32 shorter events, 4.6 us)
Async XLA Ops:
  0.0 13.9 %collective-permute-start = (bf16[16,32,512]{2,1,0:T(8,128)(2,1)}, bf16[16,32,512]{2,1,0:T(8,128)(2,1)S(1)}, u32[]{:S(2)}, u32[]{:S(2)}) collective-permute-start(bf16[16,32,512]{2,1,0:T(8,128)(2,1)} %bitcast.11), channel_id=1, source_target_pairs={{0,2},{1,3},{2,0},{3,1},{4,6},{5,7},{6,4},{7,5},{8,10},{9,11},{10,... | collective-permute-start | bytes 1572872 | tf_op jit(solution)/shard_map/ppermute | solution.py:407
  0.5 13.5 %collective-permute-start.1 = (bf16[16,32]{1,0:T(8,128)(2,1)}, bf16[16,32]{1,0:T(8,128)(2,1)S(1)}, u32[]{:S(2)}, u32[]{:S(2)}) collective-permute-start(bf16[16,32]{1,0:T(8,128)(2,1)} %bitcast.13), channel_id=1, source_target_pairs={{0,2},{1,3},{2,0},{3,1},{4,6},{5,7},{6,4},{7,5},{8,10},{9,11},{10,... | collective-permute-start | bytes 3080 | tf_op jit(solution)/shard_map/ppermute | solution.py:407
  2.7 11.3 %collective-permute-start.2 = (s32[3,16]{1,0:T(4,128)S(1)}, s32[3,16]{1,0:T(4,128)S(1)}, u32[]{:S(2)}, u32[]{:S(2)}) collective-permute-start(s32[3,16]{1,0:T(4,128)S(1)} %pad_add_fusion.lists0_hbm), channel_id=1, source_target_pairs={{0,2},{1,3},{2,0},{3,1},{4,6},{5,7},{6,4},{7,5},{8,10},{9,11},{10,... | collective-permute-start | bytes 584 | tf_op jit(solution)/shard_map/ppermute | solution.py:407
  4.9 1.2 %copy-start = (bf16[1,1,512,1024]{3,2,1,0:T(8,128)(2,1)S(1)}, bf16[1,1,512,1024]{3,2,1,0:T(8,128)(2,1)}, u32[]{:S(2)}) copy-start(bf16[1,1,512,1024]{3,2,1,0:T(8,128)(2,1)} %param.8) | copy-start | bytes 3145732
  6.1 1.0 %copy-start.1 = (bf16[1,16,32,512]{3,2,1,0:T(8,128)(2,1)S(1)}, bf16[1,16,32,512]{3,2,1,0:T(8,128)(2,1)}, u32[]{:S(2)}) copy-start(bf16[1,16,32,512]{3,2,1,0:T(8,128)(2,1)} %param.12) | copy-start | bytes 1572868
  7.2 0.7 %copy-start.3 = (bf16[1,16,32]{2,1,0:T(8,128)(2,1)S(1)}, bf16[1,16,32]{2,1,0:T(8,128)(2,1)}, u32[]{:S(2)}) copy-start(bf16[1,16,32]{2,1,0:T(8,128)(2,1)} %param.13) | copy-start | bytes 3076
  7.9 14.3 %copy-start.2 = (bf16[144,512]{1,0:T(8,128)(2,1)S(1)}, bf16[144,512]{1,0:T(8,128)(2,1)}, u32[]{:S(2)}) copy-start(bf16[144,512]{1,0:T(8,128)(2,1)} %shard_map.83.halo_ref) | copy-start | bytes 442372
  15.8 10.6 %collective-permute-start.3 = (bf16[7,528,128]{2,1,0:T(8,128)(2,1)S(1)}, bf16[7,528,128]{2,1,0:T(8,128)(2,1)S(1)}, u32[]{:S(2)}, u32[]{:S(2)}) collective-permute-start(bf16[7,528,128]{2,1,0:T(8,128)(2,1)S(1)} %get-tuple-element.40), channel_id=1, source_target_pairs={{0,1},{1,0},{2,3},{3,2},{4,5},{5,4},{6,7},{7,6},{8,9},{9,8},{10,11... | collective-permute-start | bytes 2838536 | tf_op jit(solution)/shard_map/ppermute | solution.py:407
  15.9 2.7 %collective-permute-start.4 = (bf16[1,528,128]{2,1,0:T(8,128)(2,1)S(1)}, bf16[1,528,128]{2,1,0:T(8,128)(2,1)S(1)}, u32[]{:S(2)}, u32[]{:S(2)}) collective-permute-start(bf16[1,528,128]{2,1,0:T(8,128)(2,1)S(1)} %get-tuple-element.42), channel_id=1, source_target_pairs={{0,1},{1,0},{2,3},{3,2},{4,5},{5,4},{6,7},{7,6},{8,9},{9,8},{10,11... | collective-permute-start | bytes 405512 | tf_op jit(solution)/shard_map/ppermute | solution.py:407
  18.9 7.5 %collective-permute-start.5 = (bf16[640,128]{1,0:T(8,128)(2,1)S(1)}, bf16[640,128]{1,0:T(8,128)(2,1)S(1)}, u32[]{:S(2)}, u32[]{:S(2)}) collective-permute-start(bf16[640,128]{1,0:T(8,128)(2,1)S(1)} %get-tuple-element.43), channel_id=1, source_target_pairs={{0,4},{1,29},{2,6},{3,31},{4,8},{5,1},{6,10},{7,3},{8,12},{9,5},{1... | collective-permute-start | bytes 491528 | tf_op jit(solution)/shard_map/ppermute | solution.py:404
  22.1 8.4 %collective-permute-start.9 = (bf16[144,512]{1,0:T(8,128)(2,1)S(1)}, bf16[144,512]{1,0:T(8,128)(2,1)S(1)}, u32[]{:S(2)}, u32[]{:S(2)}) collective-permute-start(bf16[144,512]{1,0:T(8,128)(2,1)S(1)} %copy-done.2), channel_id=1, source_target_pairs={{1,0},{2,1},{3,2},{4,3},{5,4},{6,5},{7,6},{8,7},{9,8},{10,9},{11,1... | collective-permute-start | bytes 442376 | tf_op jit(solution)/shard_map/ppermute | solution.py:449
  22.1 8.4 %collective-permute-start.8 = (bf16[144,512]{1,0:T(8,128)(2,1)S(1)}, bf16[144,512]{1,0:T(8,128)(2,1)S(1)}, u32[]{:S(2)}, u32[]{:S(2)}) collective-permute-start(bf16[144,512]{1,0:T(8,128)(2,1)S(1)} %copy-done.2), channel_id=1, source_target_pairs={{0,1},{1,2},{2,3},{3,4},{4,5},{5,6},{6,7},{7,8},{8,9},{9,10},{10,1... | collective-permute-start | bytes 442376 | tf_op jit(solution)/shard_map/ppermute | solution.py:448
  22.6 7.9 %collective-permute-start.7 = (bf16[400,128]{1,0:T(8,128)(2,1)S(1)}, bf16[400,128]{1,0:T(8,128)(2,1)S(1)}, u32[]{:S(2)}, u32[]{:S(2)}) collective-permute-start(bf16[400,128]{1,0:T(8,128)(2,1)S(1)} %get-tuple-element.44), channel_id=1, source_target_pairs={{0,28},{1,5},{2,30},{3,7},{4,0},{5,9},{6,2},{7,11},{8,4},{9,13},{1... | collective-permute-start | bytes 307208 | tf_op jit(solution)/shard_map/ppermute | solution.py:404
  26.7 10.4 %collective-permute-start.6 = (bf16[1040,128]{1,0:T(8,128)(2,1)S(1)}, bf16[1040,128]{1,0:T(8,128)(2,1)S(1)}, u32[]{:S(2)}, u32[]{:S(2)}) collective-permute-start(bf16[1040,128]{1,0:T(8,128)(2,1)S(1)} %shard_map.86), channel_id=1, source_target_pairs={{0,4},{1,29},{2,6},{3,31},{4,8},{5,1},{6,10},{7,3},{8,12},{9,5},{1... | collective-permute-start | bytes 798728 | tf_op jit(solution)/shard_map/ppermute | solution.py:404
  30.8 10.6 %collective-permute-start.12 = (bf16[1040,128]{1,0:T(8,128)(2,1)S(1)}, bf16[1040,128]{1,0:T(8,128)(2,1)S(1)}, u32[]{:S(2)}, u32[]{:S(2)}) collective-permute-start(bf16[1040,128]{1,0:T(8,128)(2,1)S(1)} %shard_map.90), channel_id=1, source_target_pairs={{0,28},{1,5},{2,30},{3,7},{4,0},{5,9},{6,2},{7,11},{8,4},{9,13},{1... | collective-permute-start | bytes 798728 | tf_op jit(solution)/shard_map/ppermute | solution.py:404
  37.5 10.1 %collective-permute-start.10 = (bf16[1040,128]{1,0:T(8,128)(2,1)S(1)}, bf16[1040,128]{1,0:T(8,128)(2,1)S(1)}, u32[]{:S(2)}, u32[]{:S(2)}) collective-permute-start(bf16[1040,128]{1,0:T(8,128)(2,1)S(1)} %shard_map.88), channel_id=1, source_target_pairs={{0,4},{1,29},{2,6},{3,31},{4,8},{5,1},{6,10},{7,3},{8,12},{9,5},{1... | collective-permute-start | bytes 798728 | tf_op jit(solution)/shard_map/ppermute | solution.py:404
  41.8 9.5 %collective-permute-start.13 = (bf16[1040,128]{1,0:T(8,128)(2,1)S(1)}, bf16[1040,128]{1,0:T(8,128)(2,1)S(1)}, u32[]{:S(2)}, u32[]{:S(2)}) collective-permute-start(bf16[1040,128]{1,0:T(8,128)(2,1)S(1)} %shard_map.91), channel_id=1, source_target_pairs={{0,28},{1,5},{2,30},{3,7},{4,0},{5,9},{6,2},{7,11},{8,4},{9,13},{1... | collective-permute-start | bytes 798728 | tf_op jit(solution)/shard_map/ppermute | solution.py:404
  41.9 11.1 %collective-permute-start.14 = (bf16[1040,128]{1,0:T(8,128)(2,1)S(1)}, bf16[1040,128]{1,0:T(8,128)(2,1)S(1)}, u32[]{:S(2)}, u32[]{:S(2)}) collective-permute-start(bf16[1040,128]{1,0:T(8,128)(2,1)S(1)} %get-tuple-element.53), channel_id=1, source_target_pairs={{0,32},{32,64},{64,96},{96,128},{128,160},{160,192},{192,224},{224... | collective-permute-start | bytes 798728 | tf_op jit(solution)/shard_map/ppermute | solution.py:476
  43.5 9.9 %collective-permute-start.16 = (bf16[1040,128]{1,0:T(8,128)(2,1)S(1)}, bf16[1040,128]{1,0:T(8,128)(2,1)S(1)}, u32[]{:S(2)}, u32[]{:S(2)}) collective-permute-start(bf16[1040,128]{1,0:T(8,128)(2,1)S(1)} %get-tuple-element.56), channel_id=1, source_target_pairs={{32,0},{64,32},{96,64},{128,96},{160,128},{192,160},{224,192},{0,2... | collective-permute-start | bytes 798728 | tf_op jit(solution)/shard_map/ppermute | solution.py:477
  47.9 9.8 %collective-permute-start.11 = (bf16[1040,128]{1,0:T(8,128)(2,1)S(1)}, bf16[1040,128]{1,0:T(8,128)(2,1)S(1)}, u32[]{:S(2)}, u32[]{:S(2)}) collective-permute-start(bf16[1040,128]{1,0:T(8,128)(2,1)S(1)} %shard_map.89), channel_id=1, source_target_pairs={{0,4},{1,29},{2,6},{3,31},{4,8},{5,1},{6,10},{7,3},{8,12},{9,5},{1... | collective-permute-start | bytes 798728 | tf_op jit(solution)/shard_map/ppermute | solution.py:404
  53.3 7.7 %collective-permute-start.15 = (bf16[1040,128]{1,0:T(8,128)(2,1)S(1)}, bf16[1040,128]{1,0:T(8,128)(2,1)S(1)}, u32[]{:S(2)}, u32[]{:S(2)}) collective-permute-start(bf16[1040,128]{1,0:T(8,128)(2,1)S(1)} %shard_map.92), channel_id=1, source_target_pairs={{0,28},{1,5},{2,30},{3,7},{4,0},{5,9},{6,2},{7,11},{8,4},{9,13},{1... | collective-permute-start | bytes 798728 | tf_op jit(solution)/shard_map/ppermute | solution.py:404
